TPU v7x, 1024 devices: a whole 4x8x16 slice. The times are simulated.
1024 devices in a mesh: dp: 128 (over z_lo, y, core), tensor: 8 (over z_hi, x).
Axes of the slice: x: 4, y: 8, z: 16 (z_hi: 2, z_lo: 8; z = z_hi * 8 + z_lo), core: 2. Of those that a mesh axis runs over, the one named last changes fastest.
Arguments:
- image_features: bfloat16 [8192, 1152], P('dp', 'tensor'), may hold values from -40 to 40
- text_features: bfloat16 [8192, 1152], P('dp', 'tensor'), may hold values from -40 to 40
- image_weight: bfloat16 [1152, 1152], P('tensor'), may hold values from -0.1875 to 0.1875
- text_weight: bfloat16 [1152, 1152], P('tensor'), may hold values from -0.1875 to 0.1875
- log_scale: float32 [1], replicated, may hold values from 1.5 to 2.5
- logit_bias: float32 [1], replicated, may hold values from -4 to -2
Outputs:
- image_weight_grad: float32 [1152, 1152], P('tensor', 'dp')
- text_weight_grad: float32 [1152, 1152], P('tensor', 'dp')
- image_feature_grad: float32 [8192, 1152], P('dp', 'tensor')
- text_feature_grad: float32 [8192, 1152], P('dp', 'tensor')
All inputs are finite; a program needn't handle non-finite values.
Results may differ from a plain program's by a relative error of at most 0.005.
Values may be sent and summed in bfloat16 or wider, within the bound.
No kernel may reach another device: no remote copies, remote signals or barrier semaphores. Data moves between devices by JAX's collectives and lax.ppermute only.
A program may use at most 32 MiB of HBM per device.

v0:
```python
import jax
import jax.numpy as jnp
from jax import lax
from jax.sharding import PartitionSpec as P

EPS = 1e-06


def from_behind(value, axis, by):
    size = lax.axis_size(axis)
    return lax.ppermute(value, axis, [(i, (i + by) % size) for i in range(size)])


def normalize(embed):
    inverse = lax.rsqrt(jnp.sum(embed * embed, axis=-1, keepdims=True) + EPS)
    return (embed * inverse, inverse)


def tile_terms(own_vec, other_vec, matched, scale, bias):
    logits = scale * jnp.dot(own_vec, other_vec.T, preferred_element_type=jnp.float32) + bias
    rows = lax.broadcasted_iota(jnp.int32, logits.shape, 0)
    cols = lax.broadcasted_iota(jnp.int32, logits.shape, 1)
    target = jnp.where(matched & (rows == cols), 1.0, 0.0).astype(jnp.float32)
    coef = (jax.nn.sigmoid(logits) - target).astype(jnp.bfloat16)
    return jnp.dot(coef, other_vec, preferred_element_type=jnp.float32)


def back_norm(direction, unit, inverse):
    inner = jnp.sum(unit * direction, axis=-1, keepdims=True)
    return (inverse * (direction - unit * inner)).astype(jnp.bfloat16)


def forward_sweep(state, turns, distance, accumulate):

    def one_turn(count, carry):
        block, sums = carry
        block = from_behind(block, "dp", distance)
        return (block, accumulate(sums, block, count + 1))

    return lax.fori_loop(0, turns, one_turn, state)


def local(image_features, text_features, image_weight, text_weight, log_scale, logit_bias):
    scale = jnp.exp(log_scale[0])
    bias = logit_bias[0]
    tensor_count = lax.axis_size("tensor")
    data_count = lax.axis_size("dp")
    span = data_count // tensor_count
    tensor_index = lax.axis_index("tensor")
    part_image = jnp.dot(image_features, image_weight, preferred_element_type=jnp.float32)
    part_text = jnp.dot(text_features, text_weight, preferred_element_type=jnp.float32)
    image_embed, text_embed = lax.psum((part_image, part_text), "tensor")
    image_unit, image_inverse = normalize(image_embed)
    text_unit, text_inverse = normalize(text_embed)
    image_vec = image_unit.astype(jnp.bfloat16)
    text_vec = text_unit.astype(jnp.bfloat16)
    distance = 1
    offset = span * tensor_index
    start = jnp.stack([image_vec, text_vec])
    for bit in range((tensor_count - 1).bit_length()):
        moved = from_behind(start, "dp", span << bit)
        start = jnp.where(tensor_index >> bit & 1 == 1, moved, start)

    def accumulate(sums, block, position):
        matched = (offset + distance * position) % data_count == 0
        image_sum = sums[0] + tile_terms(image_vec, block[1], matched, scale, bias)
        text_sum = sums[1] + tile_terms(text_vec, block[0], matched, scale, bias)
        return (image_sum, text_sum)

    empty = jnp.zeros(image_embed.shape, jnp.float32)
    sums = accumulate((empty, empty), start, 0)
    block, sums = forward_sweep((start, sums), span - 1, distance, accumulate)
    image_total, text_total = lax.psum((sums[0], sums[1]), "tensor")
    image_back = back_norm(scale * image_total, image_unit, image_inverse)
    text_back = back_norm(scale * text_total, text_unit, text_inverse)
    image_part = jnp.dot(image_features.T, image_back, preferred_element_type=jnp.float32)
    text_part = jnp.dot(text_features.T, text_back, preferred_element_type=jnp.float32)
    image_feature_grad = jnp.dot(image_back, image_weight.T, preferred_element_type=jnp.float32)
    text_feature_grad = jnp.dot(text_back, text_weight.T, preferred_element_type=jnp.float32)
    image_weight_grad, text_weight_grad = (
        lax.psum_scatter(image_part, "dp", scatter_dimension=1, tiled=True),
        lax.psum_scatter(text_part, "dp", scatter_dimension=1, tiled=True),
    )
    return (image_weight_grad, text_weight_grad, image_feature_grad, text_feature_grad)


def solution(mesh):
    placed = (P("dp", "tensor"), P("dp", "tensor"), P("tensor", None), P("tensor", None), P(), P())
    return jax.shard_map(
        local,
        mesh=mesh,
        in_specs=placed,
        out_specs=(P("tensor", "dp"), P("tensor", "dp"), P("dp", "tensor"), P("dp", "tensor")),
        check_vma=False,
    )
```

profile of v0, /device:TPU:1, one launch (start us, length us, event | category | flops | bytes accessed | tf_op | source)
XLA Modules:
  0.0 2266.5 jit_solution(5994836758228559168)
XLA Ops:
  7.2 1.9 fusion.68
  10.2 169.0 %all-reduce.13.cloned.1.call-done = (f32[64,1152]{1,0:T(8,128)}, f32[64,1152]{1,0:T(8,128)}) async-done(((f32[64,1152]{1,0:T(8,128)}, f32[64,1152]{1,0:T(8,128)}), (f32[64,1152]{1,0:T(8,128)}, f32[64,1152]{1,0:T(8,128)})) %all-reduce.13.cloned.1.call-update) | async-done | bytes 589840 | tf_op jit(solution)/shard_map/psum | solution.py:52
  181.5 2.3 collective-permute-start.1
  185.2 10.4 collective-permute-done.1
  195.7 1.9 collective-permute-start.2
  197.7 17.6 collective-permute-done.2
  215.3 1.9 collective-permute-start.3
  217.3 13.6 collective-permute-done.3
  231.8 280.8 %while.19 = (s32[]{:T(128)}, bf16[2,64,1152]{2,1,0:T(8,128)(2,1)S(1)}, f32[64,1152]{1,0:T(8,128)S(1)}, f32[64,1152]{1,0:T(8,128)S(1)}, f32[]{:T(128)}, /*index=5...) while((s32[]{:T(128)}, ...), condition=%wide.region_5.6_spmd, body=%wide.region_4.5_spmd.sunk | while | flops 37978128 | bytes 3834169 | solution.py:40
  231.8 6.7 collective-permute-start
  238.6 7.0 collective-permute-done
  247.8 1.9 collective-permute-start
  249.7 14.8 collective-permute-done
  268.6 14.8 collective-permute-done
  285.6 1.9 collective-permute-start
  287.5 14.8 collective-permute-done
  306.5 14.8 collective-permute-done
  325.4 14.8 collective-permute-done
  342.4 1.9 collective-permute-start
  344.3 14.8 collective-permute-done
  363.2 14.8 collective-permute-done
  382.1 14.8 collective-permute-done
  401.1 14.8 collective-permute-done
  418.0 1.9 collective-permute-start
  420.0 14.8 collective-permute-done
  436.9 1.9 collective-permute-start
  438.9 14.8 collective-permute-done
  457.8 14.8 collective-permute-done
  476.7 14.8 collective-permute-done
  495.7 14.8 collective-permute-done
  513.5 160.2 %all-reduce.11.cloned.1.call-done = (f32[64,1152]{1,0:T(8,128)}, f32[64,1152]{1,0:T(8,128)}) async-done(((f32[64,1152]{1,0:T(8,128)}, f32[64,1152]{1,0:T(8,128)}), (f32[64,1152]{1,0:T(8,128)}, f32[64,1152]{1,0:T(8,128)})) %all-reduce.11.cloned.1.call-update) | async-done | bytes 589840 | tf_op jit(solution)/shard_map/psum | solution.py:73
  682.7 1573.8 %all-reduce.9.cloned.1.call-done = (f32[144,1152]{1,0:T(8,128)}, f32[144,1152]{1,0:T(8,128)}) async-done(((f32[144,1152]{1,0:T(8,128)}, f32[144,1152]{1,0:T(8,128)}), (f32[144,1152]{1,0:T(8,128)}, f32[144,1152]{1,0:T(8,128)})) %all-reduce.9.cloned.1.call-update) | async-done | bytes 1327120
  (107 shorter events, 66.3 us)
Async XLA Ops:
  7.2 2.0 copy-start
  7.2 2.0 copy-start.9
  7.2 172.0 %all-reduce.13.cloned.1.call-start = ((), (), s32[]{:S(2)}) async-start(), calls=%async_computation.2 | async-start | bytes 1179648 | tf_op jit(solution)/shard_map/psum | solution.py:52
  10.1 663.6 %all-reduce.11.cloned.1.call-start = ((), (), s32[]{:S(2)}) async-start(), calls=%async_computation.1 | async-start | bytes 1179648 | tf_op jit(solution)/shard_map/psum | solution.py:73
  179.2 1.1 copy-start.4
  180.4 1.0 copy-start.3
  181.5 14.1 collective-permute-start.1
  195.7 19.6 collective-permute-start.2
  215.3 15.6 collective-permute-start.3
  231.8 13.8 collective-permute-start
  247.8 16.8 collective-permute-start
  266.7 16.8 collective-permute-start
  285.6 16.8 collective-permute-start
  304.5 16.8 collective-permute-start
  323.4 16.8 collective-permute-start
  342.4 16.8 collective-permute-start
  361.3 16.8 collective-permute-start
  380.2 16.8 collective-permute-start
  399.1 16.8 collective-permute-start
  418.0 16.8 collective-permute-start
  436.9 16.8 collective-permute-start
  455.9 16.8 collective-permute-start
  474.8 16.8 collective-permute-start
  493.7 16.8 collective-permute-start
  512.6 0.7 copy-start.1
  512.6 0.8 copy-start.2
  513.5 1743.1 %all-reduce.9.cloned.1.call-start = ((), (), s32[]{:S(2)}) async-start(), calls=%async_computation | async-start | bytes 2654208
  673.7 1.2 copy-start.7
  674.9 1.0 copy-start.6
  675.9 0.8 copy-start.8
  679.0 2.9 copy-start.5
Sparse Core Ops, SparseCore 0:
  11.6 167.5 all-reduce.12
  513.6 160.0 all-reduce.10
  679.1 1577.4 all-reduce.8
where the time goes:
time: 2270 us
  waiting for transfers between devices  2160 us (95%)
  starting transfers between devices  39.9 us (2%)
  matrix products  39.3 us (2%)
    unnamed x4, waiting for transfers between devices  1570 us
    ppermute x18, waiting for transfers between devices, from_behind(): lax.ppermute(value, axis, [(i, (i + by) % size) for i in range(size)])  256 us
    psum x1, waiting for transfers between devices, local(): image_embed, text_embed = lax.psum((part_image, part_text), 'tensor')  169 us
    psum x1, waiting for transfers between devices, local(): image_total, text_total = lax.psum((sums[0], sums[1]), 'tensor')  160 us
  transfers between devices with their start and end apart: 21, of which 21 were waited for; matrix products, arithmetic and copies ran while one was open for 0% of the time, Pallas kernels for 0%

commit v1 on v0

v1 whole, which is shorter than its diff:
```python
import jax
import jax.numpy as jnp
from jax import lax
from jax.sharding import Mesh, PartitionSpec as P

EPS = 1e-06
DATA = ("zl", "y", "c")
TENSOR = ("zh", "x")
SIZES = {"zl": 8, "y": 8, "c": 2, "zh": 2, "x": 4}
F32 = jnp.float32
BF16 = jnp.bfloat16


def dot(a, b, dims):
    return lax.dot_general(a, b, (dims, ((), ())), preferred_element_type=F32)


def exchange(blocks, axes):
    return lax.all_to_all(blocks, axes, 0, 0, tiled=True)


def spread(block, axes, count):
    return exchange(jnp.broadcast_to(block[None], (count, *block.shape)), axes)


def shifted(value, axis, by):
    size = SIZES[axis]
    return lax.ppermute(value, axis, [(i, (i + by) % size) for i in range(size)])


def flat(*sizes):
    return [lax.broadcasted_iota(jnp.int32, sizes, i).reshape(-1) for i in range(len(sizes))]


def local(image_features, text_features, image_weight, text_weight, log_scale, logit_bias):
    scale = jnp.exp(log_scale[0])
    bias = logit_bias[0]
    zl, y, c, zh, x = (lax.axis_index(axis) for axis in ("zl", "y", "c", "zh", "x"))
    rows, depth = image_features.shape
    width = image_weight.shape[1]
    tensor = SIZES["zh"] * SIZES["x"]
    own = rows // tensor
    both = 2 * own

    with jax.named_scope("embed"):
        parts = [
            dot(features, weight, ((1,), (0,))).astype(BF16).reshape(tensor, own, width)
            for features, weight in ((image_features, image_weight), (text_features, text_weight))
        ]
        parts = exchange(jnp.concatenate(parts, axis=1), TENSOR)
        embed = jnp.sum(parts.astype(F32), axis=0)
        inverse = lax.rsqrt(jnp.sum(embed * embed, axis=-1, keepdims=True) + EPS)
        unit = embed * inverse
        vec = unit.astype(BF16)

    with jax.named_scope("gather_own"):
        mine = spread(vec, "y", SIZES["y"]).reshape(-1, width)
        theirs = shifted(mine, "c", 1)
        held = jnp.concatenate([mine, theirs])

    with jax.named_scope("gather_others"):
        column = lax.all_gather(vec, ("zh", "zl"), tiled=True)
        steps = (0, 1, 3, 2)
        others = jnp.concatenate([column] + [shifted(column, "x", by) for by in steps[1:]])

    with jax.named_scope("pairs"):
        hc, hy, hkind, hrow = flat(2, SIZES["y"], 2, own)
        held_data = (zl * SIZES["y"] + hy) * 2 + jnp.where(hc == 0, c, 1 - c)
        held_id = held_data * rows + (zh * SIZES["x"] + x) * own + hrow
        ox, ozh, ozl, okind, orow = flat(4, 2, SIZES["zl"], 2, own)
        step = jnp.where(ox == 0, 0, jnp.where(ox == 1, 1, jnp.where(ox == 2, 3, 2)))
        other_data = (ozl * SIZES["y"] + y) * 2 + c
        other_id = other_data * rows + (ozh * SIZES["x"] + (x - step + 4) % 4) * own + orow
        logits = scale * dot(held, others, ((1,), (1,))) + bias
        target = jnp.where(held_id[:, None] == other_id[None, :], 1.0, 0.0)
        coef = jnp.where(hkind[:, None] != okind[None, :], jax.nn.sigmoid(logits) - target, 0.0)
        direction = dot(coef.astype(BF16), others, ((1,), (0,)))

    with jax.named_scope("reduce_pairs"):
        half = mine.shape[0]
        direction = direction[:half] + shifted(direction[half:], "c", 1)
        direction = exchange(direction.astype(BF16).reshape(SIZES["y"], both, width), "y")
        direction = scale * jnp.sum(direction.astype(F32), axis=0)

    with jax.named_scope("back"):
        inner = jnp.sum(unit * direction, axis=-1, keepdims=True)
        back = (inverse * (direction - unit * inner)).astype(BF16)
        back = spread(back, TENSOR, tensor).reshape(-1, width)

    with jax.named_scope("feature_grad"):
        weights = jnp.concatenate([image_weight, text_weight])
        grads = dot(back, weights, ((1,), (1,))).reshape(tensor, 2, own, 2 * depth)
        image_feature_grad = grads[:, 0, :, :depth].reshape(rows, depth)
        text_feature_grad = grads[:, 1, :, depth:].reshape(rows, depth)

    with jax.named_scope("weight_grad"):
        blank = jnp.zeros((tensor, own, depth), BF16)
        features = jnp.concatenate(
            [
                jnp.concatenate([image_features.reshape(tensor, own, depth), blank], axis=2),
                jnp.concatenate([blank, text_features.reshape(tensor, own, depth)], axis=2),
            ],
            axis=1,
        ).reshape(2 * rows, 2 * depth)
        share = width // (SIZES["zl"] * SIZES["y"] * 2)
        pc, py, pzl, pk = flat(2, SIZES["y"], SIZES["zl"], share)
        source = ((pzl * SIZES["y"] + py) * 2 + jnp.where(pc == 0, c, 1 - c)) * share + pk
        order = lax.broadcasted_iota(jnp.int32, (width, width), 0) == source[None, :]
        sorted_back = dot(back, order.astype(BF16), ((1,), (0,))).astype(BF16)
        partial = dot(sorted_back, features, ((0,), (0,)))
        partial = partial[: width // 2] + shifted(partial[width // 2 :], "c", 1)
        partial = exchange(partial.astype(BF16).reshape(SIZES["y"], -1, 2 * depth), "y")
        partial = jnp.sum(partial.astype(F32), axis=0)
        partial = exchange(partial.reshape(SIZES["zl"], share, 2 * depth), "zl")
        total = jnp.sum(partial, axis=0).T

    return (total[:depth], total[depth:], image_feature_grad, text_feature_grad)


def solution(mesh):
    names = ("zl", "y", "c", "zh", "x")
    fine = Mesh(mesh.devices.reshape([SIZES[name] for name in names]), names)
    placed = (P(DATA, TENSOR), P(DATA, TENSOR), P(TENSOR, None), P(TENSOR, None), P(), P())
    return jax.shard_map(
        local,
        mesh=fine,
        in_specs=placed,
        out_specs=(P(TENSOR, DATA), P(TENSOR, DATA), P(DATA, TENSOR), P(DATA, TENSOR)),
        check_vma=False,
    )
```

time: 2270 us -> 222 us (0.10)
  waiting for transfers between devices: 2160 us -> 42.8 us
  blocking collectives: 0 us -> 69.7 us
  starting transfers between devices: 39.9 us -> 86.4 us
  matrix products: 39.3 us -> 8.17 us
    unnamed x4 -> x0, waiting for transfers between devices: 1570 us -> none
    psum x2 -> x0, waiting for transfers between devices: 329 us -> none  [the longest x1 169 us: local(): image_embed, text_embed = lax.psum((part_image, part_text), 'tensor')]
    ppermute x18 -> x6, waiting for transfers between devices: 256 us -> 3.44 us  [shifted(): lax.ppermute(value, axis, [(i, (i + by) % size) for i in range(size)])]
    all_to_all x0 -> x4, starting transfers between devices: none -> 49.8 us  [exchange(): return lax.all_to_all(blocks, axes, 0, 0, tiled=True)]
    all_to_all x0 -> x4, waiting for transfers between devices: none -> 39.3 us  [exchange(): return lax.all_to_all(blocks, axes, 0, 0, tiled=True)]
    all_to_all x0 -> x2, blocking collectives: none -> 37.2 us  [exchange(): return lax.all_to_all(blocks, axes, 0, 0, tiled=True)]
    all_gather x0 -> x1, blocking collectives: none -> 32.5 us  [local(): column = lax.all_gather(vec, ('zh', 'zl'), tiled=True)]
    dot_general x38 -> x5, matrix products: 39.3 us -> 8.17 us  [dot(): return lax.dot_general(a, b, (dims, ((), ())), preferred_element_type=F32)]
  transfers between devices with their start and end apart: 21 -> 10, of which waited for: 21 -> 6; matrix products, arithmetic and copies ran while one was open for 0% -> 3% of each run, Pallas kernels for 0% -> 0%
where the time goes in v1:
time: 222 us; the launch traced here: 221 us
  starting transfers between devices  86.4 us (39%)
  blocking collectives  69.7 us (31%)
  waiting for transfers between devices  42.8 us (19%)
  local copies, waits for them, and re-layouts  9.44 us (4%)
  matrix products  8.17 us (4%)
  other arithmetic  2.63 us (1%)
  between operations  2.25 us (1%)
    all_to_all x4, starting transfers between devices, exchange(): return lax.all_to_all(blocks, axes, 0, 0, tiled=True)  49.8 us
    all_to_all x4, waiting for transfers between devices, exchange(): return lax.all_to_all(blocks, axes, 0, 0, tiled=True)  39.3 us
    all_to_all x2, blocking collectives, exchange(): return lax.all_to_all(blocks, axes, 0, 0, tiled=True)  37.2 us
    ppermute x6, starting transfers between devices, shifted(): lax.ppermute(value, axis, [(i, (i + by) % size) for i in range(size)])  36.6 us
    all_gather x1, blocking collectives, local(): column = lax.all_gather(vec, ('zh', 'zl'), tiled=True)  32.5 us
    dot_general x5, matrix products, dot(): return lax.dot_general(a, b, (dims, ((), ())), preferred_element_type=F32)  8.17 us
  transfers between devices with their start and end apart: 10, of which 6 were waited for; matrix products, arithmetic and copies ran while one was open for 3% of the time, Pallas kernels for 0%

profile of v1, /device:TPU:1, one launch (start us, length us, event | category | flops | bytes accessed | tf_op | source)
XLA Modules:
  0.0 221.3 jit_solution(3468056194983078062)
XLA Ops:
  0.6 1.2 fusion.3
  1.8 1.2 fusion.4
  3.0 0.7 pad_maximum_fusion
  3.7 21.7 %all-to-all-start = ((bf16[8,16,1152]{2,1,0:T(8,128)(2,1)}), bf16[8,16,1152]{2,1,0:T(8,128)(2,1)S(1)}, u32[]{:S(2)}, u32[]{:S(2)}) async-start(bf16[8,16,1152]{2,1,0:T(8,128)(2,1)} %pad_maximum_fusion), calls=%async_computation | async-start | bytes 589824 | tf_op jit(solution)/shard_map/embed/all_to_all | solution.py:19
  25.5 15.2 %all-to-all-done = bf16[8,16,1152]{2,1,0:T(8,128)(2,1)S(1)} async-done(((bf16[8,16,1152]{2,1,0:T(8,128)(2,1)}), bf16[8,16,1152]{2,1,0:T(8,128)(2,1)S(1)}, u32[]{:S(2)}, u32[]{:S(2)}) %all-to-all-start) | async-done | bytes 294944 | tf_op jit(solution)/shard_map/embed/all_to_all | solution.py:19
  41.0 32.5 %all_gather.3 = bf16[256,1152]{1,0:T(8,128)(2,1)S(1)} all-gather(bf16[16,1152]{1,0:T(8,128)(2,1)S(1)} %multiply_convert_fusion.1), channel_id=1, replica_groups=mesh['zl'=8,'y'=8,'c'=2,'zh'=2,'x'=4] {'zh','zl'}, dimensions={0}, use_global_device_ids=true | all-gather | bytes 626688 | tf_op jit(solution)/shard_map/gather_others/all_gather | solution.py:62
  73.5 1.9 collective-permute-start.1
  76.0 0.8 broadcast_in_dim.53
  76.8 6.8 %all-to-all-start.1 = ((bf16[8,16,1152]{2,1,0:T(8,128)(2,1)}), bf16[8,16,1152]{2,1,0:T(8,128)(2,1)S(1)}, u32[]{:S(2)}, u32[]{:S(2)}) async-start(bf16[8,16,1152]{2,1,0:T(8,128)(2,1)} %broadcast_in_dim.53), calls=%async_computation.1 | async-start | bytes 589824 | tf_op jit(solution)/shard_map/gather_own/all_to_all | solution.py:19
  83.6 4.6 %collective-permute-start.2 = (bf16[256,1152]{1,0:T(8,128)(2,1)S(1)}, bf16[256,1152]{1,0:T(8,128)(2,1)S(1)}, u32[]{:S(2)}, u32[]{:S(2)}) collective-permute-start(bf16[256,1152]{1,0:T(8,128)(2,1)S(1)} %all_gather.3), channel_id=1, source_target_pairs={{0,3},{1,0},{2,1},{3,2},{4,7},{5,4},{6,5},{7,6},{8,11},{9,8},{10,9... | collective-permute-start | bytes 1769480 | tf_op jit(solution)/shard_map/gather_others/ppermute | solution.py:28
  89.9 1.9 collective-permute-start.3
  91.8 0.9 constant_dynamic-update-slice_fusion.3
  93.3 12.9 %collective-permute-start = (bf16[128,1152]{1,0:T(8,128)(2,1)S(1)}, bf16[128,1152]{1,0:T(8,128)(2,1)S(1)}, u32[]{:S(2)}, u32[]{:S(2)}) collective-permute-start(bf16[128,1152]{1,0:T(8,128)(2,1)S(1)} %bitcast.39), channel_id=1, source_target_pairs={{0,8},{8,0},{1,9},{9,1},{2,10},{10,2},{3,11},{11,3},{4,12},{12,4},... | collective-permute-start | bytes 884744 | tf_op jit(solution)/shard_map/gather_own/ppermute | solution.py:28
  106.1 0.9 constant_dynamic-update-slice_fusion.2
  107.0 0.9 constant_dynamic-update-slice_fusion.1
  107.9 0.9 constant_dynamic-update-slice_fusion
  108.8 4.0 %fusion.14 = f32[256,1152]{1,0:T(8,128)S(1)} fusion(bf16[1024,1152]{1,0:T(8,128)(2,1)} %constant_dynamic-update-slice_fusion, bf16[128,1152]{1,0:T(8,128)(2,1)S(1)} %collective-permute-done, bf16[128,1152]{1,0:T(8,128)(2,1)S(1)} %bitcast.40, s32[1024]{0:T(1024)S(1)} %fusion.52, f32[]{:T(128)} %bitcast.36, f32[]{:T(128)} %bitcast.2, s32[1024]{0:T(1024)S(1)} %ne.35, ...), kind=kOutput, calls=%fused_computation.18 | convolution fusion | flops 1212022784 | bytes 4139016 | tf_op jit(solution)/shard_map/pairs/dot_general | solution.py:15
  112.9 9.3 %collective-permute-start.4 = (f32[128,1152]{1,0:T(8,128)S(1)}, f32[128,1152]{1,0:T(8,128)S(1)}, u32[]{:S(2)}, u32[]{:S(2)}) collective-permute-start(f32[128,1152]{1,0:T(8,128)S(1)} %slice.33), channel_id=1, source_target_pairs={{0,8},{8,0},{1,9},{9,1},{2,10},{10,2},{3,11},{11,3},{4,12},{12,4},... | collective-permute-start | bytes 1769480 | tf_op jit(solution)/shard_map/reduce_pairs/ppermute | solution.py:28
  122.1 1.6 collective-permute-done.4
  123.8 18.6 %all_to_all.30 = bf16[8,16,1152]{2,1,0:T(8,128)(2,1)S(1)} all-to-all(bf16[8,16,1152]{2,1,0:T(8,128)(2,1)S(1)} %bitcast.38), channel_id=1, replica_groups=mesh['zl'=8,'y'=8,'c'=2,'zh'=2,'x'=4] {'y'}, dimensions={0} | all-to-all | bytes 589824 | tf_op jit(solution)/shard_map/reduce_pairs/all_to_all | solution.py:19
  142.8 0.7 broadcast_in_dim.59
  143.5 11.6 %all-to-all-start.3 = ((bf16[8,16,1152]{2,1,0:T(8,128)(2,1)}), bf16[8,16,1152]{2,1,0:T(8,128)(2,1)S(1)}, u32[]{:S(2)}, u32[]{:S(2)}) async-start(bf16[8,16,1152]{2,1,0:T(8,128)(2,1)} %broadcast_in_dim.59), calls=%async_computation.3 | async-start | bytes 589824 | tf_op jit(solution)/shard_map/back/all_to_all | solution.py:19
  155.5 14.7 %all-to-all-done.3 = bf16[8,16,1152]{2,1,0:T(8,128)(2,1)S(1)} async-done(((bf16[8,16,1152]{2,1,0:T(8,128)(2,1)}), bf16[8,16,1152]{2,1,0:T(8,128)(2,1)S(1)}, u32[]{:S(2)}, u32[]{:S(2)}) %all-to-all-start.3) | async-done | bytes 294944 | tf_op jit(solution)/shard_map/back/all_to_all | solution.py:19
  170.2 1.4 fusion.13
  171.8 6.1 %collective-permute-start.5 = (f32[576,288]{0,1:T(8,128)S(1)}, f32[576,288]{0,1:T(8,128)S(1)}, u32[]{:S(2)}, u32[]{:S(2)}) collective-permute-start(f32[576,288]{0,1:T(8,128)S(1)} %slice.35), channel_id=1, source_target_pairs={{0,8},{8,0},{1,9},{9,1},{2,10},{10,2},{3,11},{11,3},{4,12},{12,4},... | collective-permute-start | bytes 1990664 | tf_op jit(solution)/shard_map/weight_grad/ppermute | solution.py:28
  178.0 1.8 collective-permute-done.5
  180.1 18.6 %all_to_all.31 = bf16[8,72,288]{2,1,0:T(8,128)(2,1)S(1)} all-to-all(bf16[8,72,288]{2,1,0:T(8,128)(2,1)S(1)} %bitcast.37), channel_id=1, replica_groups=mesh['zl'=8,'y'=8,'c'=2,'zh'=2,'x'=4] {'y'}, dimensions={0} | all-to-all | bytes 663552 | tf_op jit(solution)/shard_map/weight_grad/all_to_all | solution.py:19
  198.8 0.8 reshape.296
  199.6 9.6 %all-to-all-start.5 = ((f32[8,1,2592]{2,1,0:T(1,128)}), f32[8,1,2592]{2,1,0:T(1,128)S(1)}, u32[]{:S(2)}, u32[]{:S(2)}) async-start(f32[8,1,2592]{2,1,0:T(1,128)} %reshape.296), calls=%async_computation.5 | async-start | bytes 172032 | tf_op jit(solution)/shard_map/weight_grad/all_to_all | solution.py:19
  209.6 0.7 slice_bitcast_fusion
  210.3 8.8 %all-to-all-done.5 = f32[8,1,2592]{2,1,0:T(1,128)S(1)} async-done(((f32[8,1,2592]{2,1,0:T(1,128)}), f32[8,1,2592]{2,1,0:T(1,128)S(1)}, u32[]{:S(2)}, u32[]{:S(2)}) %all-to-all-start.5) | async-done | bytes 82976 | tf_op jit(solution)/shard_map/weight_grad/all_to_all | solution.py:19
  219.7 0.8 reduce
  (50 shorter events, 5.0 us)
Async XLA Ops:
  3.7 37.0 %all-to-all-start = ((bf16[8,16,1152]{2,1,0:T(8,128)(2,1)}), bf16[8,16,1152]{2,1,0:T(8,128)(2,1)S(1)}, u32[]{:S(2)}, u32[]{:S(2)}) async-start(bf16[8,16,1152]{2,1,0:T(8,128)(2,1)} %pad_maximum_fusion), calls=%async_computation | async-start | bytes 589824 | tf_op jit(solution)/shard_map/embed/all_to_all | solution.py:19
  73.5 32.6 %collective-permute-start.1 = (bf16[256,1152]{1,0:T(8,128)(2,1)S(1)}, bf16[256,1152]{1,0:T(8,128)(2,1)S(1)}, u32[]{:S(2)}, u32[]{:S(2)}) collective-permute-start(bf16[256,1152]{1,0:T(8,128)(2,1)S(1)} %all_gather.3), channel_id=1, source_target_pairs={{0,1},{1,2},{2,3},{3,0},{4,5},{5,6},{6,7},{7,4},{8,9},{9,10},{10,1... | collective-permute-start | bytes 1769480 | tf_op jit(solution)/shard_map/gather_others/ppermute | solution.py:28
  76.8 16.5 %all-to-all-start.1 = ((bf16[8,16,1152]{2,1,0:T(8,128)(2,1)}), bf16[8,16,1152]{2,1,0:T(8,128)(2,1)S(1)}, u32[]{:S(2)}, u32[]{:S(2)}) async-start(bf16[8,16,1152]{2,1,0:T(8,128)(2,1)} %broadcast_in_dim.53), calls=%async_computation.1 | async-start | bytes 589824 | tf_op jit(solution)/shard_map/gather_own/all_to_all | solution.py:19
  83.6 23.4 %collective-permute-start.2 = (bf16[256,1152]{1,0:T(8,128)(2,1)S(1)}, bf16[256,1152]{1,0:T(8,128)(2,1)S(1)}, u32[]{:S(2)}, u32[]{:S(2)}) collective-permute-start(bf16[256,1152]{1,0:T(8,128)(2,1)S(1)} %all_gather.3), channel_id=1, source_target_pairs={{0,3},{1,0},{2,1},{3,2},{4,7},{5,4},{6,5},{7,6},{8,11},{9,8},{10,9... | collective-permute-start | bytes 1769480 | tf_op jit(solution)/shard_map/gather_others/ppermute | solution.py:28
  89.9 18.0 %collective-permute-start.3 = (bf16[256,1152]{1,0:T(8,128)(2,1)S(1)}, bf16[256,1152]{1,0:T(8,128)(2,1)S(1)}, u32[]{:S(2)}, u32[]{:S(2)}) collective-permute-start(bf16[256,1152]{1,0:T(8,128)(2,1)S(1)} %all_gather.3), channel_id=1, source_target_pairs={{0,2},{1,3},{2,0},{3,1},{4,6},{5,7},{6,4},{7,5},{8,10},{9,11},{10,... | collective-permute-start | bytes 1769480 | tf_op jit(solution)/shard_map/gather_others/ppermute | solution.py:28
  93.3 15.5 %collective-permute-start = (bf16[128,1152]{1,0:T(8,128)(2,1)S(1)}, bf16[128,1152]{1,0:T(8,128)(2,1)S(1)}, u32[]{:S(2)}, u32[]{:S(2)}) collective-permute-start(bf16[128,1152]{1,0:T(8,128)(2,1)S(1)} %bitcast.39), channel_id=1, source_target_pairs={{0,8},{8,0},{1,9},{9,1},{2,10},{10,2},{3,11},{11,3},{4,12},{12,4},... | collective-permute-start | bytes 884744 | tf_op jit(solution)/shard_map/gather_own/ppermute | solution.py:28
  112.8 42.6 %copy-start.2 = (bf16[64,144]{1,0:T(8,128)(2,1)S(1)}, bf16[64,144]{1,0:T(8,128)(2,1)}, u32[]{:S(2)}) copy-start(bf16[64,144]{1,0:T(8,128)(2,1)} %param.7) | copy-start | bytes 55300
  112.8 42.6 %copy-start.3 = (bf16[64,144]{1,0:T(8,128)(2,1)S(1)}, bf16[64,144]{1,0:T(8,128)(2,1)}, u32[]{:S(2)}) copy-start(bf16[64,144]{1,0:T(8,128)(2,1)} %param.6) | copy-start | bytes 55300
  112.9 10.9 %collective-permute-start.4 = (f32[128,1152]{1,0:T(8,128)S(1)}, f32[128,1152]{1,0:T(8,128)S(1)}, u32[]{:S(2)}, u32[]{:S(2)}) collective-permute-start(f32[128,1152]{1,0:T(8,128)S(1)} %slice.33), channel_id=1, source_target_pairs={{0,8},{8,0},{1,9},{9,1},{2,10},{10,2},{3,11},{11,3},{4,12},{12,4},... | collective-permute-start | bytes 1769480 | tf_op jit(solution)/shard_map/reduce_pairs/ppermute | solution.py:28
  143.5 26.7 %all-to-all-start.3 = ((bf16[8,16,1152]{2,1,0:T(8,128)(2,1)}), bf16[8,16,1152]{2,1,0:T(8,128)(2,1)S(1)}, u32[]{:S(2)}, u32[]{:S(2)}) async-start(bf16[8,16,1152]{2,1,0:T(8,128)(2,1)} %broadcast_in_dim.59), calls=%async_computation.3 | async-start | bytes 589824 | tf_op jit(solution)/shard_map/back/all_to_all | solution.py:19
  171.8 37.4 %copy-start = (bf16[144,1152]{1,0:T(8,128)(2,1)S(1)}, bf16[144,1152]{1,0:T(8,128)(2,1)}, u32[]{:S(2)}) copy-start(bf16[144,1152]{1,0:T(8,128)(2,1)} %param.9) | copy-start | bytes 995332
  171.8 37.4 %copy-start.1 = (bf16[144,1152]{1,0:T(8,128)(2,1)S(1)}, bf16[144,1152]{1,0:T(8,128)(2,1)}, u32[]{:S(2)}) copy-start(bf16[144,1152]{1,0:T(8,128)(2,1)} %param.8) | copy-start | bytes 995332
  171.8 7.9 %collective-permute-start.5 = (f32[576,288]{0,1:T(8,128)S(1)}, f32[576,288]{0,1:T(8,128)S(1)}, u32[]{:S(2)}, u32[]{:S(2)}) collective-permute-start(f32[576,288]{0,1:T(8,128)S(1)} %slice.35), channel_id=1, source_target_pairs={{0,8},{8,0},{1,9},{9,1},{2,10},{10,2},{3,11},{11,3},{4,12},{12,4},... | collective-permute-start | bytes 1990664 | tf_op jit(solution)/shard_map/weight_grad/ppermute | solution.py:28
  199.6 19.5 %all-to-all-start.5 = ((f32[8,1,2592]{2,1,0:T(1,128)}), f32[8,1,2592]{2,1,0:T(1,128)S(1)}, u32[]{:S(2)}, u32[]{:S(2)}) async-start(f32[8,1,2592]{2,1,0:T(1,128)} %reshape.296), calls=%async_computation.5 | async-start | bytes 172032 | tf_op jit(solution)/shard_map/weight_grad/all_to_all | solution.py:19

commit v2 on v1

v2 whole, which is shorter than its diff:
```python
import jax
import jax.numpy as jnp
from jax import lax
from jax.sharding import Mesh, PartitionSpec as P

EPS = 1e-06
DATA = ("zl", "y", "c")
TENSOR = ("zh", "x")
SIZES = {"zl": 8, "y": 8, "c": 2, "zh": 2, "x": 4}
F32 = jnp.float32
BF16 = jnp.bfloat16


def dot(a, b, dims):
    return lax.dot_general(a, b, (dims, ((), ())), preferred_element_type=F32)


def exchange(blocks, axes):
    return lax.all_to_all(blocks, axes, 0, 0, tiled=True)


def spread(block, axes, count):
    return exchange(jnp.broadcast_to(block[None], (count, *block.shape)), axes)


def shifted(value, axis, by):
    size = SIZES[axis]
    return lax.ppermute(value, axis, [(i, (i + by) % size) for i in range(size)])


def flat(*sizes):
    return [lax.broadcasted_iota(jnp.int32, sizes, i).reshape(-1) for i in range(len(sizes))]


def local(image_features, text_features, image_weight, text_weight, log_scale, logit_bias):
    scale = jnp.exp(log_scale[0])
    bias = logit_bias[0]
    zl, y, c, zh, x = (lax.axis_index(axis) for axis in ("zl", "y", "c", "zh", "x"))
    rows, depth = image_features.shape
    width = image_weight.shape[1]
    own = rows // SIZES["x"]

    with jax.named_scope("embed"):
        parts = [
            dot(features, weight, ((1,), (0,))).astype(BF16).reshape(SIZES["x"], own, width)
            for features, weight in ((image_features, image_weight), (text_features, text_weight))
        ]
        parts = exchange(jnp.concatenate(parts, axis=1), "x")
        embed = jnp.sum(parts.astype(F32), axis=0)
        embed = embed + shifted(embed, "zh", 1)
        inverse = lax.rsqrt(jnp.sum(embed * embed, axis=-1, keepdims=True) + EPS)
        unit = embed * inverse
        vec = unit.astype(BF16)

    with jax.named_scope("gather_own"):
        mine = spread(vec, "y", SIZES["y"]).reshape(SIZES["y"], 2, own, width)
        mine = mine.transpose(1, 0, 2, 3).reshape(2, -1, width)
        theirs = shifted(mine, "c", 1)
        held = jnp.concatenate([mine, theirs], axis=1)

    with jax.named_scope("gather_others"):
        half = own // 2
        column = lax.dynamic_slice_in_dim(vec.reshape(2, own, width), zh * half, half, axis=1)
        column = lax.all_gather(column.reshape(2 * half, width), ("zh", "zl"), tiled=True)
        column = column.reshape(-1, 2, half, width).transpose(1, 0, 2, 3).reshape(2, -1, width)
        others = [column] + [shifted(column, "x", by) for by in (1, 3, 2)]

    with jax.named_scope("pairs"):
        hc, hy, hrow = flat(2, SIZES["y"], own)
        held_data = (zl * SIZES["y"] + hy) * 2 + jnp.where(hc == 0, c, 1 - c)
        held_id = held_data * rows + x * own + hrow
        ozh, ozl, orow = flat(2, SIZES["zl"], half)
        other_id = ((ozl * SIZES["y"] + y) * 2 + c) * rows + ozh * half + orow
        sums = [0.0, 0.0]
        for first, second in ((0, 1), (3, 2)):
            places = [(x + SIZES["x"] - by) % SIZES["x"] for by in (first, second)]
            ids = jnp.concatenate([other_id + place * own for place in places])
            pick = {0: 0, 1: 1, 3: 2, 2: 3}
            for kind in range(2):
                block = jnp.concatenate([others[pick[by]][1 - kind] for by in (first, second)])
                logits = scale * dot(held[kind], block, ((1,), (1,))) + bias
                target = jnp.where(held_id[:, None] == ids[None, :], 1.0, 0.0)
                coef = (jax.nn.sigmoid(logits) - target).astype(BF16)
                sums[kind] = sums[kind] + dot(coef, block, ((1,), (0,)))

    with jax.named_scope("reduce_pairs"):
        cut = SIZES["y"] * own
        sent = shifted(jnp.stack([total[cut:] for total in sums]), "c", 1)
        direction = jnp.stack([total[:cut] for total in sums]) + sent
        direction = direction.astype(BF16).reshape(2, SIZES["y"], own, width).transpose(1, 0, 2, 3)
        direction = exchange(direction.reshape(SIZES["y"], 2 * own, width), "y")
        direction = scale * jnp.sum(direction.astype(F32), axis=0)

    with jax.named_scope("back"):
        inner = jnp.sum(unit * direction, axis=-1, keepdims=True)
        back = (inverse * (direction - unit * inner)).astype(BF16)
        back = spread(back, "x", SIZES["x"]).reshape(-1, width)

    with jax.named_scope("feature_grad"):
        weights = jnp.concatenate([image_weight, text_weight])
        grads = dot(back, weights, ((1,), (1,))).reshape(SIZES["x"], 2, own, 2 * depth)
        image_feature_grad = grads[:, 0, :, :depth].reshape(rows, depth)
        text_feature_grad = grads[:, 1, :, depth:].reshape(rows, depth)

    with jax.named_scope("weight_grad"):
        blank = jnp.zeros((SIZES["x"], own, depth), BF16)
        features = jnp.concatenate(
            [
                jnp.concatenate([image_features.reshape(SIZES["x"], own, depth), blank], axis=2),
                jnp.concatenate([blank, text_features.reshape(SIZES["x"], own, depth)], axis=2),
            ],
            axis=1,
        ).reshape(2 * rows, 2 * depth)
        chips = SIZES["zl"] * SIZES["y"]
        share = width // (chips * 2)
        pc, pchip, pk = flat(2, chips, share)
        source = (pchip * 2 + jnp.where(pc == 0, c, 1 - c)) * share + pk
        order = lax.broadcasted_iota(jnp.int32, (width, width), 0) == source[None, :]
        sorted_back = dot(back, order.astype(BF16), ((1,), (0,))).astype(BF16)
        partial = dot(sorted_back, features, ((0,), (0,)))
        partial = partial[: width // 2] + shifted(partial[width // 2 :], "c", 1)
        partial = exchange(partial.astype(BF16).reshape(chips, share, 2 * depth), ("zl", "y"))
        total = jnp.sum(partial.astype(F32), axis=0).T

    return (total[:depth], total[depth:], image_feature_grad, text_feature_grad)


def solution(mesh):
    names = ("zl", "y", "c", "zh", "x")
    fine = Mesh(mesh.devices.reshape([SIZES[name] for name in names]), names)
    placed = (P(DATA, TENSOR), P(DATA, TENSOR), P(TENSOR, None), P(TENSOR, None), P(), P())
    return jax.shard_map(
        local,
        mesh=fine,
        in_specs=placed,
        out_specs=(P(TENSOR, DATA), P(TENSOR, DATA), P(DATA, TENSOR), P(DATA, TENSOR)),
        check_vma=False,
    )
```

time: 222 us -> 211 us (0.950)
  starting transfers between devices: 86.4 us -> 68.3 us
  matrix products: 8.17 us -> 14.3 us
  blocking collectives: 69.7 us -> 64.9 us
  waiting for transfers between devices: 42.8 us -> 47.1 us
    all_to_all x4, starting transfers between devices: 49.8 us -> 19.8 us  [exchange(): return lax.all_to_all(blocks, axes, 0, 0, tiled=True)]
    all_to_all x2 -> x1, blocking collectives: 37.2 us -> 24.8 us  [exchange(): return lax.all_to_all(blocks, axes, 0, 0, tiled=True)]
    ppermute x6 -> x7, starting transfers between devices: 36.6 us -> 48.5 us  [shifted(): lax.ppermute(value, axis, [(i, (i + by) % size) for i in range(size)])]
    all_gather x1, blocking collectives: 32.5 us -> 40 us  [local(): lax.all_gather(column.reshape(2 * half, width), ('zh', 'zl'), tiled=True)]
    dot_general x5 -> x8, matrix products: 8.17 us -> 14.3 us  [dot(): return lax.dot_general(a, b, (dims, ((), ())), preferred_element_type=F32)]
    ppermute x6 -> x7, waiting for transfers between devices: 3.44 us -> 7.21 us  [shifted(): lax.ppermute(value, axis, [(i, (i + by) % size) for i in range(size)])]
    squeeze x1 -> x4, local copies, waits for them, and re-layouts: 0.72 us -> 4.26 us  [local(): others[pick[by]][1 - kind]]
  transfers between devices with their start and end apart: 10 -> 11, of which waited for: 6 -> 8; matrix products, arithmetic and copies ran while one was open for 3% -> 3% of each run, Pallas kernels for 0% -> 0%
where the time goes in v2:
time: 211 us; the launch traced here: 210 us
  starting transfers between devices  68.3 us (32%)
  blocking collectives  64.9 us (31%)
  waiting for transfers between devices  47.1 us (22%)
  matrix products  14.3 us (7%)
  local copies, waits for them, and re-layouts  11.4 us (5%)
  between operations  2.29 us (1%)
    ppermute x7, starting transfers between devices, shifted(): lax.ppermute(value, axis, [(i, (i + by) % size) for i in range(size)])  48.5 us
    all_gather x1, blocking collectives, local(): lax.all_gather(column.reshape(2 * half, width), ('zh', 'zl'), tiled=True)  40 us
    all_to_all x4, waiting for transfers between devices, exchange(): return lax.all_to_all(blocks, axes, 0, 0, tiled=True)  39.9 us
    all_to_all x1, blocking collectives, exchange(): return lax.all_to_all(blocks, axes, 0, 0, tiled=True)  24.8 us
    all_to_all x4, starting transfers between devices, exchange(): return lax.all_to_all(blocks, axes, 0, 0, tiled=True)  19.8 us
    dot_general x8, matrix products, dot(): return lax.dot_general(a, b, (dims, ((), ())), preferred_element_type=F32)  14.3 us
    ppermute x7, waiting for transfers between devices, shifted(): lax.ppermute(value, axis, [(i, (i + by) % size) for i in range(size)])  7.21 us
    squeeze x4, local copies, waits for them, and re-layouts, local(): others[pick[by]][1 - kind]  4.26 us
  transfers between devices with their start and end apart: 11, of which 8 were waited for; matrix products, arithmetic and copies ran while one was open for 3% of the time, Pallas kernels for 0%

profile of v2, /device:TPU:1, one launch (start us, length us, event | category | flops | bytes accessed | tf_op | source)
XLA Modules:
  0.0 210.3 jit_solution(6225065175396201929)
XLA Ops:
  0.6 1.2 convolution_convert_fusion.1
  1.8 1.2 convolution_convert_fusion
  3.7 4.8 %all-to-all-start = ((bf16[4,32,1152]{2,1,0:T(8,128)(2,1)}), bf16[4,32,1152]{2,1,0:T(8,128)(2,1)S(1)}, u32[]{:S(2)}, u32[]{:S(2)}) async-start(bf16[4,32,1152]{2,1,0:T(8,128)(2,1)} %pad_maximum_fusion.2), calls=%async_computation | async-start | bytes 589824 | tf_op jit(solution)/shard_map/embed/all_to_all | solution.py:19
  8.6 5.7 %all-to-all-done = bf16[4,32,1152]{2,1,0:T(8,128)(2,1)S(1)} async-done(((bf16[4,32,1152]{2,1,0:T(8,128)(2,1)}), bf16[4,32,1152]{2,1,0:T(8,128)(2,1)S(1)}, u32[]{:S(2)}, u32[]{:S(2)}) %all-to-all-start) | async-done | bytes 294944 | tf_op jit(solution)/shard_map/embed/all_to_all | solution.py:19
  14.3 19.2 %collective-permute-start = (f32[32,1152]{1,0:T(8,128)S(1)}, f32[32,1152]{1,0:T(8,128)S(1)}, u32[]{:S(2)}, u32[]{:S(2)}) collective-permute-start(f32[32,1152]{1,0:T(8,128)S(1)} %convert_reduce_fusion.2), channel_id=1, source_target_pairs={{0,4},{4,0},{1,5},{5,1},{2,6},{6,2},{3,7},{7,3},{8,12},{12,8},{9,1... | collective-permute-start | bytes 442376 | tf_op jit(solution)/shard_map/embed/ppermute | solution.py:28
  35.3 1.0 collective-permute-done
  36.6 40.0 %all_gather.3 = bf16[256,1152]{1,0:T(8,128)(2,1)S(1)} all-gather(bf16[16,1152]{1,0:T(8,128)(2,1)S(1)} %dynamic-slice_bitcast_fusion), channel_id=1, replica_groups=mesh['zl'=8,'y'=8,'c'=2,'zh'=2,'x'=4] {'zh','zl'}, dimensions={0}, use_global_device_ids=true | all-gather | bytes 626688 | tf_op jit(solution)/shard_map/gather_others/all_gather | solution.py:64
  76.6 2.8 %collective-permute-start.3 = (bf16[2,128,1152]{2,1,0:T(8,128)(2,1)S(1)}, bf16[2,128,1152]{2,1,0:T(8,128)(2,1)S(1)}, u32[]{:S(2)}, u32[]{:S(2)}) collective-permute-start(bf16[2,128,1152]{2,1,0:T(8,128)(2,1)S(1)} %bitcast.86), channel_id=1, source_target_pairs={{0,3},{1,0},{2,1},{3,2},{4,7},{5,4},{6,5},{7,6},{8,11},{9,8},{10,9... | collective-permute-start | bytes 1769480 | tf_op jit(solution)/shard_map/gather_others/ppermute | solution.py:28
  80.3 6.8 %all-to-all-start.1 = ((bf16[8,32,1152]{2,1,0:T(8,128)(2,1)}), bf16[8,32,1152]{2,1,0:T(8,128)(2,1)S(1)}, u32[]{:S(2)}, u32[]{:S(2)}) async-start(bf16[8,32,1152]{2,1,0:T(8,128)(2,1)} %broadcast_in_dim.52), calls=%async_computation.1 | async-start | bytes 1179648 | tf_op jit(solution)/shard_map/gather_own/all_to_all | solution.py:19
  87.2 3.1 %collective-permute-start.4 = (bf16[2,128,1152]{2,1,0:T(8,128)(2,1)S(1)}, bf16[2,128,1152]{2,1,0:T(8,128)(2,1)}, u32[]{:S(2)}, u32[]{:S(2)}) collective-permute-start(bf16[2,128,1152]{2,1,0:T(8,128)(2,1)S(1)} %bitcast.87), channel_id=1, source_target_pairs={{0,2},{1,3},{2,0},{3,1},{4,6},{5,7},{6,4},{7,5},{8,10},{9,11},{10,... | collective-permute-start | bytes 1769480 | tf_op jit(solution)/shard_map/gather_others/ppermute | solution.py:28
  90.3 1.9 collective-permute-start.2
  93.0 0.9 slice_bitcast_fusion.9
  93.9 6.1 %all-to-all-done.1 = bf16[8,32,1152]{2,1,0:T(8,128)(2,1)S(1)} async-done(((bf16[8,32,1152]{2,1,0:T(8,128)(2,1)}), bf16[8,32,1152]{2,1,0:T(8,128)(2,1)S(1)}, u32[]{:S(2)}, u32[]{:S(2)}) %all-to-all-start.1) | async-done | bytes 589856 | tf_op jit(solution)/shard_map/gather_own/all_to_all | solution.py:19
  100.1 11.1 %collective-permute-start.1 = (bf16[2,128,1152]{2,1,0:T(8,128)(2,1)S(1)}, bf16[2,128,1152]{2,1,0:T(8,128)(2,1)S(1)}, u32[]{:S(2)}, u32[]{:S(2)}) collective-permute-start(bf16[2,128,1152]{2,1,0:T(8,128)(2,1)S(1)} %bitcast.89), channel_id=1, source_target_pairs={{0,8},{8,0},{1,9},{9,1},{2,10},{10,2},{3,11},{11,3},{4,12},{12,4},... | collective-permute-start | bytes 1769480 | tf_op jit(solution)/shard_map/gather_own/ppermute | solution.py:28
  111.1 1.8 slice_bitcast_fusion.8
  113.0 1.9 collective-permute-done.2
  115.7 2.0 fusion.34
  117.7 2.3 %convolution_add_fusion.1 = f32[256,1152]{1,0:T(8,128)S(1)} fusion(f32[256,1152]{1,0:T(8,128)} %fusion.34, bf16[128,1152]{1,0:T(8,128)(2,1)S(1)} %get-tuple-element.12, bf16[128,1152]{1,0:T(8,128)(2,1)S(1)} %copy-done.2, s32[256]{0:T(256)S(1)} %pad_add_fusion, f32[]{:T(128)} %bitcast.77, f32[]{:T(128)} %bitcast.2, s32[256]{0:T(256)S(1)} %reshape.180, ...), kind=kOutput, calls=%fused_computation.3 | convolution fusion | flops 306413568 | bytes 4720648 | tf_op jit(solution)/shard_map/pairs/dot_general | solution.py:15
  120.1 3.4 %fusion.33 = f32[256,1152]{1,0:T(8,128)} fusion(bf16[128,1152]{1,0:T(8,128)(2,1)} %get-tuple-element.17, bf16[128,1152]{1,0:T(8,128)(2,1)} %get-tuple-element.15, s32[256]{0:T(256)S(1)} %pad_add_fusion.1, f32[]{:T(128)} %bitcast.78, f32[]{:T(128)} %bitcast.2, s32[256]{0:T(256)S(1)} %reshape.180, bf16[2,128,1152]{2,1,0:T(8,128)(2,1)} %copy-done.6, ...), kind=kOutput, calls=%fused_computation.48 | convolution fusion | flops 306118656 | bytes 2951176 | tf_op jit(solution)/shard_map/pairs/dot_general | solution.py:15
  123.5 2.5 %convolution_add_fusion = f32[256,1152]{1,0:T(8,128)S(1)} fusion(f32[256,1152]{1,0:T(8,128)} %fusion.33, bf16[128,1152]{1,0:T(8,128)(2,1)} %get-tuple-element.13, bf16[128,1152]{1,0:T(8,128)(2,1)S(1)} %get-tuple-element.11, s32[256]{0:T(256)S(1)} %pad_add_fusion, f32[]{:T(128)} %bitcast.79, f32[]{:T(128)} %bitcast.2, s32[256]{0:T(256)S(1)} %reshape.180, ...), kind=kOutput, calls=%fused_computation.2 | convolution fusion | flops 306413568 | bytes 4130824 | tf_op jit(solution)/shard_map/pairs/dot_general | solution.py:15
  126.1 6.0 %collective-permute-start.5 = (f32[2,128,1152]{2,1,0:T(8,128)S(1)}, f32[2,128,1152]{2,1,0:T(8,128)S(1)}, u32[]{:S(2)}, u32[]{:S(2)}) collective-permute-start(f32[2,128,1152]{2,1,0:T(8,128)S(1)} %pad_maximum_fusion), channel_id=1, source_target_pairs={{0,8},{8,0},{1,9},{9,1},{2,10},{10,2},{3,11},{11,3},{4,12},{12,4},... | collective-permute-start | bytes 3538952 | tf_op jit(solution)/shard_map/reduce_pairs/ppermute | solution.py:28
  132.1 2.5 %collective-permute-done.5 = f32[2,128,1152]{2,1,0:T(8,128)S(1)} collective-permute-done((f32[2,128,1152]{2,1,0:T(8,128)S(1)}, f32[2,128,1152]{2,1,0:T(8,128)S(1)}, u32[]{:S(2)}, u32[]{:S(2)}) %collective-permute-start.5) | collective-permute-done | bytes 1179680 | tf_op jit(solution)/shard_map/reduce_pairs/ppermute | solution.py:28
  134.7 24.8 %all_to_all.25 = bf16[8,32,1152]{2,1,0:T(8,128)(2,1)S(1)} all-to-all(bf16[8,32,1152]{2,1,0:T(8,128)(2,1)S(1)} %bitcast.84), channel_id=1, replica_groups=mesh['zl'=8,'y'=8,'c'=2,'zh'=2,'x'=4] {'y'}, dimensions={0} | all-to-all | bytes 1179648 | tf_op jit(solution)/shard_map/reduce_pairs/all_to_all | solution.py:19
  160.7 3.5 %all-to-all-start.3 = ((bf16[4,32,1152]{2,1,0:T(8,128)(2,1)}), bf16[4,32,1152]{2,1,0:T(8,128)(2,1)S(1)}, u32[]{:S(2)}, u32[]{:S(2)}) async-start(bf16[4,32,1152]{2,1,0:T(8,128)(2,1)} %broadcast_in_dim.56), calls=%async_computation.3 | async-start | bytes 589824 | tf_op jit(solution)/shard_map/back/all_to_all | solution.py:19
  164.5 5.3 %all-to-all-done.3 = bf16[4,32,1152]{2,1,0:T(8,128)(2,1)S(1)} async-done(((bf16[4,32,1152]{2,1,0:T(8,128)(2,1)}), bf16[4,32,1152]{2,1,0:T(8,128)(2,1)S(1)}, u32[]{:S(2)}, u32[]{:S(2)}) %all-to-all-start.3) | async-done | bytes 294944 | tf_op jit(solution)/shard_map/back/all_to_all | solution.py:19
  169.8 1.4 fusion.4
  171.5 4.5 %collective-permute-start.6 = (f32[576,288]{0,1:T(8,128)S(1)}, f32[576,288]{0,1:T(8,128)S(1)}, u32[]{:S(2)}, u32[]{:S(2)}) collective-permute-start(f32[576,288]{0,1:T(8,128)S(1)} %slice.99), channel_id=1, source_target_pairs={{0,8},{8,0},{1,9},{9,1},{2,10},{10,2},{3,11},{11,3},{4,12},{12,4},... | collective-permute-start | bytes 1990664 | tf_op jit(solution)/shard_map/weight_grad/ppermute | solution.py:28
  176.0 1.8 collective-permute-done.6
  178.4 1.6 reshape.192
  180.0 4.7 %all-to-all-start.4 = ((bf16[64,2,1296]{2,1,0:T(2,128)(2,1)}), bf16[64,2,1296]{2,1,0:T(2,128)(2,1)S(1)}, u32[]{:S(2)}, u32[]{:S(2)}) async-start(bf16[64,2,1296]{2,1,0:T(2,128)(2,1)} %reshape.192), calls=%async_computation.4 | async-start | bytes 720896 | tf_op jit(solution)/shard_map/weight_grad/all_to_all | solution.py:19
  185.8 22.7 %all-to-all-done.4 = bf16[64,2,1296]{2,1,0:T(2,128)(2,1)S(1)} async-done(((bf16[64,2,1296]{2,1,0:T(2,128)(2,1)}), bf16[64,2,1296]{2,1,0:T(2,128)(2,1)S(1)}, u32[]{:S(2)}, u32[]{:S(2)}) %all-to-all-start.4) | async-done | bytes 331808 | tf_op jit(solution)/shard_map/weight_grad/all_to_all | solution.py:19
  208.5 0.9 reshape.193
  (58 shorter events, 8.6 us)
Async XLA Ops:
  3.7 10.5 %all-to-all-start = ((bf16[4,32,1152]{2,1,0:T(8,128)(2,1)}), bf16[4,32,1152]{2,1,0:T(8,128)(2,1)S(1)}, u32[]{:S(2)}, u32[]{:S(2)}) async-start(bf16[4,32,1152]{2,1,0:T(8,128)(2,1)} %pad_maximum_fusion.2), calls=%async_computation | async-start | bytes 589824 | tf_op jit(solution)/shard_map/embed/all_to_all | solution.py:19
  14.3 22.0 %collective-permute-start = (f32[32,1152]{1,0:T(8,128)S(1)}, f32[32,1152]{1,0:T(8,128)S(1)}, u32[]{:S(2)}, u32[]{:S(2)}) collective-permute-start(f32[32,1152]{1,0:T(8,128)S(1)} %convert_reduce_fusion.2), channel_id=1, source_target_pairs={{0,4},{4,0},{1,5},{5,1},{2,6},{6,2},{3,7},{7,3},{8,12},{12,8},{9,1... | collective-permute-start | bytes 442376 | tf_op jit(solution)/shard_map/embed/ppermute | solution.py:28
  76.6 16.3 %collective-permute-start.3 = (bf16[2,128,1152]{2,1,0:T(8,128)(2,1)S(1)}, bf16[2,128,1152]{2,1,0:T(8,128)(2,1)S(1)}, u32[]{:S(2)}, u32[]{:S(2)}) collective-permute-start(bf16[2,128,1152]{2,1,0:T(8,128)(2,1)S(1)} %bitcast.86), channel_id=1, source_target_pairs={{0,3},{1,0},{2,1},{3,2},{4,7},{5,4},{6,5},{7,6},{8,11},{9,8},{10,9... | collective-permute-start | bytes 1769480 | tf_op jit(solution)/shard_map/gather_others/ppermute | solution.py:28
  80.3 19.7 %all-to-all-start.1 = ((bf16[8,32,1152]{2,1,0:T(8,128)(2,1)}), bf16[8,32,1152]{2,1,0:T(8,128)(2,1)S(1)}, u32[]{:S(2)}, u32[]{:S(2)}) async-start(bf16[8,32,1152]{2,1,0:T(8,128)(2,1)} %broadcast_in_dim.52), calls=%async_computation.1 | async-start | bytes 1179648 | tf_op jit(solution)/shard_map/gather_own/all_to_all | solution.py:19
  87.2 24.0 %collective-permute-start.4 = (bf16[2,128,1152]{2,1,0:T(8,128)(2,1)S(1)}, bf16[2,128,1152]{2,1,0:T(8,128)(2,1)}, u32[]{:S(2)}, u32[]{:S(2)}) collective-permute-start(bf16[2,128,1152]{2,1,0:T(8,128)(2,1)S(1)} %bitcast.87), channel_id=1, source_target_pairs={{0,2},{1,3},{2,0},{3,1},{4,6},{5,7},{6,4},{7,5},{8,10},{9,11},{10,... | collective-permute-start | bytes 1769480 | tf_op jit(solution)/shard_map/gather_others/ppermute | solution.py:28
  90.3 24.6 %collective-permute-start.2 = (bf16[2,128,1152]{2,1,0:T(8,128)(2,1)S(1)}, bf16[2,128,1152]{2,1,0:T(8,128)(2,1)S(1)}, u32[]{:S(2)}, u32[]{:S(2)}) collective-permute-start(bf16[2,128,1152]{2,1,0:T(8,128)(2,1)S(1)} %bitcast.88), channel_id=1, source_target_pairs={{0,1},{1,2},{2,3},{3,0},{4,5},{5,6},{6,7},{7,4},{8,9},{9,10},{10,1... | collective-permute-start | bytes 1769480 | tf_op jit(solution)/shard_map/gather_others/ppermute | solution.py:28
  100.1 15.6 %copy-start.3 = (bf16[128,1152]{1,0:T(8,128)(2,1)S(1)}, bf16[128,1152]{1,0:T(8,128)(2,1)}, u32[]{:S(2)}) copy-start(bf16[128,1152]{1,0:T(8,128)(2,1)} %get-tuple-element.14) | copy-start | bytes 884740
  100.1 15.6 %collective-permute-start.1 = (bf16[2,128,1152]{2,1,0:T(8,128)(2,1)S(1)}, bf16[2,128,1152]{2,1,0:T(8,128)(2,1)S(1)}, u32[]{:S(2)}, u32[]{:S(2)}) collective-permute-start(bf16[2,128,1152]{2,1,0:T(8,128)(2,1)S(1)} %bitcast.89), channel_id=1, source_target_pairs={{0,8},{8,0},{1,9},{9,1},{2,10},{10,2},{3,11},{11,3},{4,12},{12,4},... | collective-permute-start | bytes 1769480 | tf_op jit(solution)/shard_map/gather_own/ppermute | solution.py:28
  115.7 2.0 copy-start.6
  115.7 2.0 copy-start.2
  126.1 8.4 %collective-permute-start.5 = (f32[2,128,1152]{2,1,0:T(8,128)S(1)}, f32[2,128,1152]{2,1,0:T(8,128)S(1)}, u32[]{:S(2)}, u32[]{:S(2)}) collective-permute-start(f32[2,128,1152]{2,1,0:T(8,128)S(1)} %pad_maximum_fusion), channel_id=1, source_target_pairs={{0,8},{8,0},{1,9},{9,1},{2,10},{10,2},{3,11},{11,3},{4,12},{12,4},... | collective-permute-start | bytes 3538952 | tf_op jit(solution)/shard_map/reduce_pairs/ppermute | solution.py:28
  159.6 4.8 %copy-start.4 = (bf16[64,144]{1,0:T(8,128)(2,1)S(1)}, bf16[64,144]{1,0:T(8,128)(2,1)}, u32[]{:S(2)}) copy-start(bf16[64,144]{1,0:T(8,128)(2,1)} %param.7) | copy-start | bytes 55300
  159.6 4.8 %copy-start.5 = (bf16[64,144]{1,0:T(8,128)(2,1)S(1)}, bf16[64,144]{1,0:T(8,128)(2,1)}, u32[]{:S(2)}) copy-start(bf16[64,144]{1,0:T(8,128)(2,1)} %param.6) | copy-start | bytes 55300
  160.7 9.1 %all-to-all-start.3 = ((bf16[4,32,1152]{2,1,0:T(8,128)(2,1)}), bf16[4,32,1152]{2,1,0:T(8,128)(2,1)S(1)}, u32[]{:S(2)}, u32[]{:S(2)}) async-start(bf16[4,32,1152]{2,1,0:T(8,128)(2,1)} %broadcast_in_dim.56), calls=%async_computation.3 | async-start | bytes 589824 | tf_op jit(solution)/shard_map/back/all_to_all | solution.py:19
  171.5 6.3 %collective-permute-start.6 = (f32[576,288]{0,1:T(8,128)S(1)}, f32[576,288]{0,1:T(8,128)S(1)}, u32[]{:S(2)}, u32[]{:S(2)}) collective-permute-start(f32[576,288]{0,1:T(8,128)S(1)} %slice.99), channel_id=1, source_target_pairs={{0,8},{8,0},{1,9},{9,1},{2,10},{10,2},{3,11},{11,3},{4,12},{12,4},... | collective-permute-start | bytes 1990664 | tf_op jit(solution)/shard_map/weight_grad/ppermute | solution.py:28
  178.4 6.3 %copy-start = (bf16[144,1152]{1,0:T(8,128)(2,1)S(1)}, bf16[144,1152]{1,0:T(8,128)(2,1)}, u32[]{:S(2)}) copy-start(bf16[144,1152]{1,0:T(8,128)(2,1)} %param.9) | copy-start | bytes 995332
  178.4 6.3 %copy-start.1 = (bf16[144,1152]{1,0:T(8,128)(2,1)S(1)}, bf16[144,1152]{1,0:T(8,128)(2,1)}, u32[]{:S(2)}) copy-start(bf16[144,1152]{1,0:T(8,128)(2,1)} %param.8) | copy-start | bytes 995332
  180.0 28.5 %all-to-all-start.4 = ((bf16[64,2,1296]{2,1,0:T(2,128)(2,1)}), bf16[64,2,1296]{2,1,0:T(2,128)(2,1)S(1)}, u32[]{:S(2)}, u32[]{:S(2)}) async-start(bf16[64,2,1296]{2,1,0:T(2,128)(2,1)} %reshape.192), calls=%async_computation.4 | async-start | bytes 720896 | tf_op jit(solution)/shard_map/weight_grad/all_to_all | solution.py:19

commit v3 on v2

--- a/solution.py
+++ b/solution.py
@@ -1,12 +1,15 @@
 import jax
 import jax.numpy as jnp
 from jax import lax
+from jax.experimental import pallas as pl
+from jax.experimental.pallas import tpu as pltpu
 from jax.sharding import Mesh, PartitionSpec as P
 
 EPS = 1e-06
 DATA = ("zl", "y", "c")
 TENSOR = ("zh", "x")
 SIZES = {"zl": 8, "y": 8, "c": 2, "zh": 2, "x": 4}
+STEPS = (0, 1, 3, 2)
 F32 = jnp.float32
 BF16 = jnp.bfloat16
 
@@ -32,6 +35,40 @@
     return [lax.broadcasted_iota(jnp.int32, sizes, i).reshape(-1) for i in range(len(sizes))]
 
 
+def pair_kernel(factors, own_ids, other_ids, mine, theirs, *refs):
+    others, (mine_sum, theirs_sum, held) = refs[: len(STEPS)], refs[len(STEPS) :]
+    size = others[0].shape[0]
+    for i, block in enumerate(others):
+        held[i * size : (i + 1) * size, :] = block[...]
+    partners = held[...]
+    for i, (rows, out) in enumerate(((mine, mine_sum), (theirs, theirs_sum))):
+        logits = factors[0] * dot(rows[...], partners, ((1,), (1,))) + factors[1]
+        target = jnp.where(own_ids[:, i : i + 1] == other_ids[0:1, :], 1.0, 0.0)
+        crossed = own_ids[:, i + 2 : i + 3] != other_ids[1:2, :]
+        coef = jnp.where(crossed, jax.nn.sigmoid(logits) - target, 0.0)
+        out[...] = dot(coef.astype(BF16), partners, ((1,), (0,)))
+
+
+def pair_sums(factors, own_ids, other_ids, mine, theirs, others):
+    count, width = mine.shape
+    partners = len(others) * others[0].shape[0]
+    whole = pl.BlockSpec(memory_space=pltpu.VMEM)
+    out = jax.ShapeDtypeStruct((count, width), F32)
+    return pl.pallas_call(
+        pair_kernel,
+        out_shape=(out, out),
+        in_specs=[pl.BlockSpec(memory_space=pltpu.SMEM)] + [whole] * (4 + len(others)),
+        out_specs=(whole, whole),
+        scratch_shapes=[pltpu.VMEM((partners, width), BF16)],
+        compiler_params=pltpu.CompilerParams(vmem_limit_bytes=24 * 2**20),
+        cost_estimate=pl.CostEstimate(
+            flops=8 * count * partners * width,
+            bytes_accessed=12 * count * width + 2 * partners * width,
+            transcendentals=2 * count * partners,
+        ),
+    )(factors, own_ids, other_ids, mine, theirs, *others)
+
+
 def local(image_features, text_features, image_weight, text_weight, log_scale, logit_bias):
     scale = jnp.exp(log_scale[0])
     bias = logit_bias[0]
@@ -53,43 +90,37 @@
         vec = unit.astype(BF16)
 
     with jax.named_scope("gather_own"):
-        mine = spread(vec, "y", SIZES["y"]).reshape(SIZES["y"], 2, own, width)
-        mine = mine.transpose(1, 0, 2, 3).reshape(2, -1, width)
+        mine = spread(vec, "y", SIZES["y"]).reshape(-1, width)
         theirs = shifted(mine, "c", 1)
-        held = jnp.concatenate([mine, theirs], axis=1)
 
     with jax.named_scope("gather_others"):
         half = own // 2
         column = lax.dynamic_slice_in_dim(vec.reshape(2, own, width), zh * half, half, axis=1)
-        column = lax.all_gather(column.reshape(2 * half, width), ("zh", "zl"), tiled=True)
-        column = column.reshape(-1, 2, half, width).transpose(1, 0, 2, 3).reshape(2, -1, width)
-        others = [column] + [shifted(column, "x", by) for by in (1, 3, 2)]
+        column = lax.all_gather(column.reshape(2 * half, width), "zl", tiled=True)
+        others = [column] + [shifted(column, "x", by) for by in STEPS[1:]]
 
     with jax.named_scope("pairs"):
-        hc, hy, hrow = flat(2, SIZES["y"], own)
-        held_data = (zl * SIZES["y"] + hy) * 2 + jnp.where(hc == 0, c, 1 - c)
-        held_id = held_data * rows + x * own + hrow
-        ozh, ozl, orow = flat(2, SIZES["zl"], half)
-        other_id = ((ozl * SIZES["y"] + y) * 2 + c) * rows + ozh * half + orow
-        sums = [0.0, 0.0]
-        for first, second in ((0, 1), (3, 2)):
-            places = [(x + SIZES["x"] - by) % SIZES["x"] for by in (first, second)]
-            ids = jnp.concatenate([other_id + place * own for place in places])
-            pick = {0: 0, 1: 1, 3: 2, 2: 3}
-            for kind in range(2):
-                block = jnp.concatenate([others[pick[by]][1 - kind] for by in (first, second)])
-                logits = scale * dot(held[kind], block, ((1,), (1,))) + bias
-                target = jnp.where(held_id[:, None] == ids[None, :], 1.0, 0.0)
-                coef = (jax.nn.sigmoid(logits) - target).astype(BF16)
-                sums[kind] = sums[kind] + dot(coef, block, ((1,), (0,)))
+        hy, hkind, hrow = flat(SIZES["y"], 2, own)
+        data = (zl * SIZES["y"] + hy) * 2
+        row = x * own + hrow
+        mine_id = (data + c) * rows + row
+        theirs_id = (data + 1 - c) * rows + row
+        ostep, ozl, okind, orow = flat(len(STEPS), SIZES["zl"], 2, half)
+        step = jnp.where(ostep == 0, 0, jnp.where(ostep == 1, 1, jnp.where(ostep == 2, 3, 2)))
+        place = (x - step + SIZES["x"]) % SIZES["x"]
+        other_id = ((ozl * SIZES["y"] + y) * 2 + c) * rows + place * own + zh * half + orow
+        kinds = jnp.stack([hkind, hkind], axis=1)
+        own_ids = jnp.concatenate([jnp.stack([mine_id, theirs_id], axis=1), kinds], axis=1)
+        other_ids = jnp.stack([other_id, okind])
+        mine_sum, theirs_sum = pair_sums(
+            jnp.stack([scale, bias]), own_ids, other_ids, mine, theirs, others
+        )
 
     with jax.named_scope("reduce_pairs"):
-        cut = SIZES["y"] * own
-        sent = shifted(jnp.stack([total[cut:] for total in sums]), "c", 1)
-        direction = jnp.stack([total[:cut] for total in sums]) + sent
-        direction = direction.astype(BF16).reshape(2, SIZES["y"], own, width).transpose(1, 0, 2, 3)
-        direction = exchange(direction.reshape(SIZES["y"], 2 * own, width), "y")
-        direction = scale * jnp.sum(direction.astype(F32), axis=0)
+        direction = mine_sum + shifted(theirs_sum, "c", 1)
+        direction = exchange(direction.astype(BF16).reshape(SIZES["y"], 2 * own, width), "y")
+        direction = jnp.sum(direction.astype(F32), axis=0)
+        direction = scale * (direction + shifted(direction, "zh", 1))
 
     with jax.named_scope("back"):
         inner = jnp.sum(unit * direction, axis=-1, keepdims=True)

time: 211 us -> 242 us (1.15)
  waiting for transfers between devices: 47.1 us -> 70.6 us
  blocking collectives: 64.9 us -> 82.3 us
  matrix products: 14.3 us -> 4.15 us
  local copies, waits for them, and re-layouts: 11.4 us -> 7.22 us
  starting transfers between devices: 68.3 us -> 71 us
    ppermute x7 -> x8, waiting for transfers between devices: 7.21 us -> 28 us  [shifted(): lax.ppermute(value, axis, [(i, (i + by) % size) for i in range(size)])]
    all_gather x1, blocking collectives: 40 us -> 50.2 us  [local(): column = lax.all_gather(column.reshape(2 * half, width), 'zl', tiled=True)]
    dot_general x8 -> x4, matrix products: 14.3 us -> 4.15 us  [dot(): return lax.dot_general(a, b, (dims, ((), ())), preferred_element_type=F32)]
    ppermute x7 -> x8, starting transfers between devices: 48.5 us -> 56.1 us  [shifted(): lax.ppermute(value, axis, [(i, (i + by) % size) for i in range(size)])]
    all_to_all x1 -> x2, blocking collectives: 24.8 us -> 32.1 us  [exchange(): return lax.all_to_all(blocks, axes, 0, 0, tiled=True)]
    all_to_all x4 -> x3, starting transfers between devices: 19.8 us -> 14.9 us  [exchange(): return lax.all_to_all(blocks, axes, 0, 0, tiled=True)]
    squeeze x4 -> x0, local copies, waits for them, and re-layouts: 4.26 us -> none  [local(): others[pick[by]][1 - kind]]
    all_to_all x4 -> x3, waiting for transfers between devices: 39.9 us -> 42.6 us  [exchange(): return lax.all_to_all(blocks, axes, 0, 0, tiled=True)]
  transfers between devices with their start and end apart: 11 -> 11, of which waited for: 8 -> 10; matrix products, arithmetic and copies ran while one was open for 3% -> 1% of each run, Pallas kernels for 0% -> 0%
where the time goes in v3:
time: 242 us; the launch traced here: 241 us
  blocking collectives  82.3 us (34%)
  starting transfers between devices  71 us (29%)
  waiting for transfers between devices  70.6 us (29%)
  local copies, waits for them, and re-layouts  7.22 us (3%)
  matrix products  4.15 us (2%)
    ppermute x8, starting transfers between devices, shifted(): lax.ppermute(value, axis, [(i, (i + by) % size) for i in range(size)])  56.1 us
    all_gather x1, blocking collectives, local(): column = lax.all_gather(column.reshape(2 * half, width), 'zl', tiled=True)  50.2 us
    all_to_all x3, waiting for transfers between devices, exchange(): return lax.all_to_all(blocks, axes, 0, 0, tiled=True)  42.6 us
    all_to_all x2, blocking collectives, exchange(): return lax.all_to_all(blocks, axes, 0, 0, tiled=True)  32.1 us
    ppermute x8, waiting for transfers between devices, shifted(): lax.ppermute(value, axis, [(i, (i + by) % size) for i in range(size)])  28 us
    all_to_all x3, starting transfers between devices, exchange(): return lax.all_to_all(blocks, axes, 0, 0, tiled=True)  14.9 us
  transfers between devices with their start and end apart: 11, of which 10 were waited for; matrix products, arithmetic and copies ran while one was open for 1% of the time, Pallas kernels for 0%

profile of v3, /device:TPU:1, one launch (start us, length us, event | category | flops | bytes accessed | tf_op | source)
XLA Modules:
  0.0 241.2 jit_solution(3660584523419440729)
XLA Ops:
  0.6 1.2 convolution_convert_fusion.1
  1.8 1.2 convolution_convert_fusion
  3.0 10.3 %all_to_all.25 = bf16[4,32,1152]{2,1,0:T(8,128)(2,1)S(1)} all-to-all(bf16[4,32,1152]{2,1,0:T(8,128)(2,1)S(1)} %pad_maximum_fusion), channel_id=1, replica_groups=mesh['zl'=8,'y'=8,'c'=2,'zh'=2,'x'=4] {'x'}, dimensions={0} | all-to-all | bytes 589824 | tf_op jit(solution)/shard_map/embed/all_to_all | solution.py:22
  13.4 19.2 %collective-permute-start = (f32[32,1152]{1,0:T(8,128)S(1)}, f32[32,1152]{1,0:T(8,128)S(1)}, u32[]{:S(2)}, u32[]{:S(2)}) collective-permute-start(f32[32,1152]{1,0:T(8,128)S(1)} %convert_reduce_fusion.2), channel_id=1, source_target_pairs={{0,4},{4,0},{1,5},{5,1},{2,6},{6,2},{3,7},{7,3},{8,12},{12,8},{9,1... | collective-permute-start | bytes 442376 | tf_op jit(solution)/shard_map/embed/ppermute | solution.py:31
  32.6 2.8 %collective-permute-done = f32[32,1152]{1,0:T(8,128)S(1)} collective-permute-done((f32[32,1152]{1,0:T(8,128)S(1)}, f32[32,1152]{1,0:T(8,128)S(1)}, u32[]{:S(2)}, u32[]{:S(2)}) %collective-permute-start) | collective-permute-done | bytes 147488 | tf_op jit(solution)/shard_map/embed/ppermute | solution.py:31
  35.7 0.9 broadcast_in_dim.37
  36.5 6.8 %all-to-all-start.1 = ((bf16[8,32,1152]{2,1,0:T(8,128)(2,1)}), bf16[8,32,1152]{2,1,0:T(8,128)(2,1)S(1)}, u32[]{:S(2)}, u32[]{:S(2)}) async-start(bf16[8,32,1152]{2,1,0:T(8,128)(2,1)} %broadcast_in_dim.37), calls=%async_computation.1 | async-start | bytes 1179648 | tf_op jit(solution)/shard_map/gather_own/all_to_all | solution.py:22
  45.7 13.9 %all-to-all-done.1 = bf16[8,32,1152]{2,1,0:T(8,128)(2,1)S(1)} async-done(((bf16[8,32,1152]{2,1,0:T(8,128)(2,1)}), bf16[8,32,1152]{2,1,0:T(8,128)(2,1)S(1)}, u32[]{:S(2)}, u32[]{:S(2)}) %all-to-all-start.1) | async-done | bytes 589856 | tf_op jit(solution)/shard_map/gather_own/all_to_all | solution.py:22
  59.6 5.5 %collective-permute-start.1 = (bf16[256,1152]{1,0:T(8,128)(2,1)S(1)}, bf16[256,1152]{1,0:T(8,128)(2,1)S(1)}, u32[]{:S(2)}, u32[]{:S(2)}) collective-permute-start(bf16[256,1152]{1,0:T(8,128)(2,1)S(1)} %bitcast.28), channel_id=1, source_target_pairs={{0,8},{8,0},{1,9},{9,1},{2,10},{10,2},{3,11},{11,3},{4,12},{12,4},... | collective-permute-start | bytes 1769480 | tf_op jit(solution)/shard_map/gather_own/ppermute | solution.py:31
  65.1 50.2 %all_gather.3.refs_0_ = bf16[128,1152]{1,0:T(8,128)(2,1)S(1)} all-gather(bf16[16,1152]{1,0:T(8,128)(2,1)S(1)} %dynamic-slice_bitcast_fusion), channel_id=1, replica_groups=mesh['zl'=8,'y'=8,'c'=2,'zh'=2,'x'=4] {'zl'}, dimensions={0}, use_global_device_ids=true | all-gather | bytes 331776 | tf_op jit(solution)/shard_map/gather_others/all_gather | solution.py:99
  115.3 2.2 collective-permute-start.2
  117.5 4.3 %collective-permute-start.3 = (bf16[128,1152]{1,0:T(8,128)(2,1)S(1)}, bf16[128,1152]{1,0:T(8,128)(2,1)S(1)}, u32[]{:S(2)}, u32[]{:S(2)}) collective-permute-start(bf16[128,1152]{1,0:T(8,128)(2,1)S(1)} %all_gather.3.refs_0_), channel_id=1, source_target_pairs={{0,3},{1,0},{2,1},{3,2},{4,7},{5,4},{6,5},{7,6},{8,11},{9,8},{10,9... | collective-permute-start | bytes 884744 | tf_op jit(solution)/shard_map/gather_others/ppermute | solution.py:31
  121.8 1.9 collective-permute-start.4
  124.0 4.6 %collective-permute-done.3.refs_2_ = bf16[128,1152]{1,0:T(8,128)(2,1)S(1)} collective-permute-done((bf16[128,1152]{1,0:T(8,128)(2,1)S(1)}, bf16[128,1152]{1,0:T(8,128)(2,1)S(1)}, u32[]{:S(2)}, u32[]{:S(2)}) %collective-permute-start.3) | collective-permute-done | bytes 294944 | tf_op jit(solution)/shard_map/gather_others/ppermute | solution.py:31
  128.6 4.9 %collective-permute-done.4.refs_3_ = bf16[128,1152]{1,0:T(8,128)(2,1)S(1)} collective-permute-done((bf16[128,1152]{1,0:T(8,128)(2,1)S(1)}, bf16[128,1152]{1,0:T(8,128)(2,1)S(1)}, u32[]{:S(2)}, u32[]{:S(2)}) %collective-permute-start.4) | collective-permute-done | bytes 294944 | tf_op jit(solution)/shard_map/gather_others/ppermute | solution.py:31
  133.6 2.4 pairs.1
  136.0 7.3 %collective-permute-start.5 = (f32[256,1152]{1,0:T(8,128)S(1)}, f32[256,1152]{1,0:T(8,128)S(1)}, u32[]{:S(2)}, u32[]{:S(2)}) collective-permute-start(f32[256,1152]{1,0:T(8,128)S(1)} %get-tuple-element.7), channel_id=1, source_target_pairs={{0,8},{8,0},{1,9},{9,1},{2,10},{10,2},{3,11},{11,3},{4,12},{12,4},... | collective-permute-start | bytes 3538952 | tf_op jit(solution)/shard_map/reduce_pairs/ppermute | solution.py:31
  143.3 2.5 %collective-permute-done.5 = f32[256,1152]{1,0:T(8,128)S(1)} collective-permute-done((f32[256,1152]{1,0:T(8,128)S(1)}, f32[256,1152]{1,0:T(8,128)S(1)}, u32[]{:S(2)}, u32[]{:S(2)}) %collective-permute-start.5) | collective-permute-done | bytes 1179680 | tf_op jit(solution)/shard_map/reduce_pairs/ppermute | solution.py:31
  145.9 21.8 %all_to_all.26 = bf16[8,32,1152]{2,1,0:T(8,128)(2,1)S(1)} all-to-all(bf16[8,32,1152]{2,1,0:T(8,128)(2,1)S(1)} %bitcast.30), channel_id=1, replica_groups=mesh['zl'=8,'y'=8,'c'=2,'zh'=2,'x'=4] {'y'}, dimensions={0} | all-to-all | bytes 1179648 | tf_op jit(solution)/shard_map/reduce_pairs/all_to_all | solution.py:22
  167.7 11.9 %collective-permute-start.6 = (f32[32,1152]{1,0:T(8,128)S(1)}, f32[32,1152]{1,0:T(8,128)S(1)}, u32[]{:S(2)}, u32[]{:S(2)}) collective-permute-start(f32[32,1152]{1,0:T(8,128)S(1)} %convert_reduce_fusion.1), channel_id=1, source_target_pairs={{0,4},{4,0},{1,5},{5,1},{2,6},{6,2},{3,7},{7,3},{8,12},{12,8},{9,1... | collective-permute-start | bytes 442376 | tf_op jit(solution)/shard_map/reduce_pairs/ppermute | solution.py:31
  179.6 11.1 %collective-permute-done.6 = f32[32,1152]{1,0:T(8,128)S(1)} collective-permute-done((f32[32,1152]{1,0:T(8,128)S(1)}, f32[32,1152]{1,0:T(8,128)S(1)}, u32[]{:S(2)}, u32[]{:S(2)}) %collective-permute-start.6) | collective-permute-done | bytes 147488 | tf_op jit(solution)/shard_map/reduce_pairs/ppermute | solution.py:31
  191.1 0.7 broadcast_in_dim.38
  191.8 3.5 %all-to-all-start.3 = ((bf16[4,32,1152]{2,1,0:T(8,128)(2,1)}), bf16[4,32,1152]{2,1,0:T(8,128)(2,1)S(1)}, u32[]{:S(2)}, u32[]{:S(2)}) async-start(bf16[4,32,1152]{2,1,0:T(8,128)(2,1)} %broadcast_in_dim.38), calls=%async_computation.3 | async-start | bytes 589824 | tf_op jit(solution)/shard_map/back/all_to_all | solution.py:22
  195.6 5.7 %all-to-all-done.3 = bf16[4,32,1152]{2,1,0:T(8,128)(2,1)S(1)} async-done(((bf16[4,32,1152]{2,1,0:T(8,128)(2,1)}), bf16[4,32,1152]{2,1,0:T(8,128)(2,1)S(1)}, u32[]{:S(2)}, u32[]{:S(2)}) %all-to-all-start.3) | async-done | bytes 294944 | tf_op jit(solution)/shard_map/back/all_to_all | solution.py:22
  201.3 1.4 fusion.3
  202.9 3.8 %collective-permute-start.7 = (f32[576,288]{0,1:T(8,128)S(1)}, f32[576,288]{0,1:T(8,128)S(1)}, u32[]{:S(2)}, u32[]{:S(2)}) collective-permute-start(f32[576,288]{0,1:T(8,128)S(1)} %slice.25), channel_id=1, source_target_pairs={{0,8},{8,0},{1,9},{9,1},{2,10},{10,2},{3,11},{11,3},{4,12},{12,4},... | collective-permute-start | bytes 1990664 | tf_op jit(solution)/shard_map/weight_grad/ppermute | solution.py:31
  206.7 1.8 collective-permute-done.7
  209.1 1.6 reshape.335
  210.7 4.6 %all-to-all-start.4 = ((bf16[64,2,1296]{2,1,0:T(2,128)(2,1)}), bf16[64,2,1296]{2,1,0:T(2,128)(2,1)S(1)}, u32[]{:S(2)}, u32[]{:S(2)}) async-start(bf16[64,2,1296]{2,1,0:T(2,128)(2,1)} %reshape.335), calls=%async_computation.4 | async-start | bytes 720896 | tf_op jit(solution)/shard_map/weight_grad/all_to_all | solution.py:22
  215.7 0.7 fusion.21
  216.4 23.0 %all-to-all-done.4 = bf16[64,2,1296]{2,1,0:T(2,128)(2,1)S(1)} async-done(((bf16[64,2,1296]{2,1,0:T(2,128)(2,1)}), bf16[64,2,1296]{2,1,0:T(2,128)(2,1)S(1)}, u32[]{:S(2)}, u32[]{:S(2)}) %all-to-all-start.4) | async-done | bytes 331808 | tf_op jit(solution)/shard_map/weight_grad/all_to_all | solution.py:22
  239.5 0.9 reshape.336
  (48 shorter events, 4.4 us)
Async XLA Ops:
  13.4 22.0 %collective-permute-start = (f32[32,1152]{1,0:T(8,128)S(1)}, f32[32,1152]{1,0:T(8,128)S(1)}, u32[]{:S(2)}, u32[]{:S(2)}) collective-permute-start(f32[32,1152]{1,0:T(8,128)S(1)} %convert_reduce_fusion.2), channel_id=1, source_target_pairs={{0,4},{4,0},{1,5},{5,1},{2,6},{6,2},{3,7},{7,3},{8,12},{12,8},{9,1... | collective-permute-start | bytes 442376 | tf_op jit(solution)/shard_map/embed/ppermute | solution.py:31
  36.5 23.1 %all-to-all-start.1 = ((bf16[8,32,1152]{2,1,0:T(8,128)(2,1)}), bf16[8,32,1152]{2,1,0:T(8,128)(2,1)S(1)}, u32[]{:S(2)}, u32[]{:S(2)}) async-start(bf16[8,32,1152]{2,1,0:T(8,128)(2,1)} %broadcast_in_dim.37), calls=%async_computation.1 | async-start | bytes 1179648 | tf_op jit(solution)/shard_map/gather_own/all_to_all | solution.py:22
  59.6 73.9 %collective-permute-start.1 = (bf16[256,1152]{1,0:T(8,128)(2,1)S(1)}, bf16[256,1152]{1,0:T(8,128)(2,1)S(1)}, u32[]{:S(2)}, u32[]{:S(2)}) collective-permute-start(bf16[256,1152]{1,0:T(8,128)(2,1)S(1)} %bitcast.28), channel_id=1, source_target_pairs={{0,8},{8,0},{1,9},{9,1},{2,10},{10,2},{3,11},{11,3},{4,12},{12,4},... | collective-permute-start | bytes 1769480 | tf_op jit(solution)/shard_map/gather_own/ppermute | solution.py:31
  115.3 8.7 %collective-permute-start.2 = (bf16[128,1152]{1,0:T(8,128)(2,1)S(1)}, bf16[128,1152]{1,0:T(8,128)(2,1)S(1)}, u32[]{:S(2)}, u32[]{:S(2)}) collective-permute-start(bf16[128,1152]{1,0:T(8,128)(2,1)S(1)} %all_gather.3.refs_0_), channel_id=1, source_target_pairs={{0,1},{1,2},{2,3},{3,0},{4,5},{5,6},{6,7},{7,4},{8,9},{9,10},{10,1... | collective-permute-start | bytes 884744 | tf_op jit(solution)/shard_map/gather_others/ppermute | solution.py:31
  117.5 11.1 %collective-permute-start.3 = (bf16[128,1152]{1,0:T(8,128)(2,1)S(1)}, bf16[128,1152]{1,0:T(8,128)(2,1)S(1)}, u32[]{:S(2)}, u32[]{:S(2)}) collective-permute-start(bf16[128,1152]{1,0:T(8,128)(2,1)S(1)} %all_gather.3.refs_0_), channel_id=1, source_target_pairs={{0,3},{1,0},{2,1},{3,2},{4,7},{5,4},{6,5},{7,6},{8,11},{9,8},{10,9... | collective-permute-start | bytes 884744 | tf_op jit(solution)/shard_map/gather_others/ppermute | solution.py:31
  121.8 11.7 %collective-permute-start.4 = (bf16[128,1152]{1,0:T(8,128)(2,1)S(1)}, bf16[128,1152]{1,0:T(8,128)(2,1)S(1)}, u32[]{:S(2)}, u32[]{:S(2)}) collective-permute-start(bf16[128,1152]{1,0:T(8,128)(2,1)S(1)} %all_gather.3.refs_0_), channel_id=1, source_target_pairs={{0,2},{1,3},{2,0},{3,1},{4,6},{5,7},{6,4},{7,5},{8,10},{9,11},{10,... | collective-permute-start | bytes 884744 | tf_op jit(solution)/shard_map/gather_others/ppermute | solution.py:31
  136.0 9.8 %collective-permute-start.5 = (f32[256,1152]{1,0:T(8,128)S(1)}, f32[256,1152]{1,0:T(8,128)S(1)}, u32[]{:S(2)}, u32[]{:S(2)}) collective-permute-start(f32[256,1152]{1,0:T(8,128)S(1)} %get-tuple-element.7), channel_id=1, source_target_pairs={{0,8},{8,0},{1,9},{9,1},{2,10},{10,2},{3,11},{11,3},{4,12},{12,4},... | collective-permute-start | bytes 3538952 | tf_op jit(solution)/shard_map/reduce_pairs/ppermute | solution.py:31
  167.6 27.8 %copy-start.2 = (bf16[64,144]{1,0:T(8,128)(2,1)S(1)}, bf16[64,144]{1,0:T(8,128)(2,1)}, u32[]{:S(2)}) copy-start(bf16[64,144]{1,0:T(8,128)(2,1)} %param.7) | copy-start | bytes 55300
  167.6 27.9 %copy-start.3 = (bf16[64,144]{1,0:T(8,128)(2,1)S(1)}, bf16[64,144]{1,0:T(8,128)(2,1)}, u32[]{:S(2)}) copy-start(bf16[64,144]{1,0:T(8,128)(2,1)} %param.6) | copy-start | bytes 55300
  167.7 23.0 %collective-permute-start.6 = (f32[32,1152]{1,0:T(8,128)S(1)}, f32[32,1152]{1,0:T(8,128)S(1)}, u32[]{:S(2)}, u32[]{:S(2)}) collective-permute-start(f32[32,1152]{1,0:T(8,128)S(1)} %convert_reduce_fusion.1), channel_id=1, source_target_pairs={{0,4},{4,0},{1,5},{5,1},{2,6},{6,2},{3,7},{7,3},{8,12},{12,8},{9,1... | collective-permute-start | bytes 442376 | tf_op jit(solution)/shard_map/reduce_pairs/ppermute | solution.py:31
  191.8 9.5 %all-to-all-start.3 = ((bf16[4,32,1152]{2,1,0:T(8,128)(2,1)}), bf16[4,32,1152]{2,1,0:T(8,128)(2,1)S(1)}, u32[]{:S(2)}, u32[]{:S(2)}) async-start(bf16[4,32,1152]{2,1,0:T(8,128)(2,1)} %broadcast_in_dim.38), calls=%async_computation.3 | async-start | bytes 589824 | tf_op jit(solution)/shard_map/back/all_to_all | solution.py:22
  202.9 5.6 %collective-permute-start.7 = (f32[576,288]{0,1:T(8,128)S(1)}, f32[576,288]{0,1:T(8,128)S(1)}, u32[]{:S(2)}, u32[]{:S(2)}) collective-permute-start(f32[576,288]{0,1:T(8,128)S(1)} %slice.25), channel_id=1, source_target_pairs={{0,8},{8,0},{1,9},{9,1},{2,10},{10,2},{3,11},{11,3},{4,12},{12,4},... | collective-permute-start | bytes 1990664 | tf_op jit(solution)/shard_map/weight_grad/ppermute | solution.py:31
  208.9 6.4 %copy-start = (bf16[144,1152]{1,0:T(8,128)(2,1)S(1)}, bf16[144,1152]{1,0:T(8,128)(2,1)}, u32[]{:S(2)}) copy-start(bf16[144,1152]{1,0:T(8,128)(2,1)} %param.9) | copy-start | bytes 995332
  208.9 6.4 %copy-start.1 = (bf16[144,1152]{1,0:T(8,128)(2,1)S(1)}, bf16[144,1152]{1,0:T(8,128)(2,1)}, u32[]{:S(2)}) copy-start(bf16[144,1152]{1,0:T(8,128)(2,1)} %param.8) | copy-start | bytes 995332
  210.7 28.8 %all-to-all-start.4 = ((bf16[64,2,1296]{2,1,0:T(2,128)(2,1)}), bf16[64,2,1296]{2,1,0:T(2,128)(2,1)S(1)}, u32[]{:S(2)}, u32[]{:S(2)}) async-start(bf16[64,2,1296]{2,1,0:T(2,128)(2,1)} %reshape.335), calls=%async_computation.4 | async-start | bytes 720896 | tf_op jit(solution)/shard_map/weight_grad/all_to_all | solution.py:22

commit v4 on v3

--- a/solution.py
+++ b/solution.py
@@ -10,6 +10,9 @@
 TENSOR = ("zh", "x")
 SIZES = {"zl": 8, "y": 8, "c": 2, "zh": 2, "x": 4}
 STEPS = (0, 1, 3, 2)
+FIRST = (0, -1, 1)
+GROUPS = FIRST + (-3, -4, -2, 3, 2)
+RUN = 16
 F32 = jnp.float32
 BF16 = jnp.bfloat16
 
@@ -31,22 +34,38 @@
     return lax.ppermute(value, axis, [(i, (i + by) % size) for i in range(size)])
 
 
+def along_z(value, by):
+    size = SIZES["zh"] * SIZES["zl"]
+    place = [(z % SIZES["zl"]) * SIZES["zh"] + z // SIZES["zl"] for z in range(size)]
+    pairs = [(place[z], place[(z + by) % size]) for z in range(size)]
+    return lax.ppermute(value, ("zl", "zh"), pairs)
+
+
 def flat(*sizes):
     return [lax.broadcasted_iota(jnp.int32, sizes, i).reshape(-1) for i in range(len(sizes))]
 
 
 def pair_kernel(factors, own_ids, other_ids, mine, theirs, *refs):
-    others, (mine_sum, theirs_sum, held) = refs[: len(STEPS)], refs[len(STEPS) :]
-    size = others[0].shape[0]
-    for i, block in enumerate(others):
-        held[i * size : (i + 1) * size, :] = block[...]
-    partners = held[...]
-    for i, (rows, out) in enumerate(((mine, mine_sum), (theirs, theirs_sum))):
-        logits = factors[0] * dot(rows[...], partners, ((1,), (1,))) + factors[1]
-        target = jnp.where(own_ids[:, i : i + 1] == other_ids[0:1, :], 1.0, 0.0)
-        crossed = own_ids[:, i + 2 : i + 3] != other_ids[1:2, :]
-        coef = jnp.where(crossed, jax.nn.sigmoid(logits) - target, 0.0)
-        out[...] = dot(coef.astype(BF16), partners, ((1,), (0,)))
+    blocks, (mine_sum, theirs_sum, held, partners) = refs[: len(STEPS)], refs[len(STEPS) :]
+    run = RUN
+    for kind in range(2):
+        for target, sources in ((held, (mine, theirs)), (partners, blocks)):
+            at = 0
+            for source in sources:
+                for start in range(kind * run, source.shape[0], 2 * run):
+                    target[kind, at : at + run, :] = source[start : start + run, :]
+                    at += run
+    matched = own_ids[...] == other_ids[...]
+    count = held.shape[1] // 2
+    for kind in range(2):
+        other = partners[1 - kind]
+        logits = factors[0] * dot(held[kind], other, ((1,), (1,))) + factors[1]
+        coef = jax.nn.sigmoid(logits) - jnp.where(matched, 1.0, 0.0)
+        total = dot(coef.astype(BF16), other, ((1,), (0,)))
+        for part, out in ((total[:count], mine_sum), (total[count:], theirs_sum)):
+            for at in range(0, count, run):
+                start = 2 * at + kind * run
+                out[start : start + run, :] = part[at : at + run]
 
 
 def pair_sums(factors, own_ids, other_ids, mine, theirs, others):
@@ -59,12 +78,15 @@
         out_shape=(out, out),
         in_specs=[pl.BlockSpec(memory_space=pltpu.SMEM)] + [whole] * (4 + len(others)),
         out_specs=(whole, whole),
-        scratch_shapes=[pltpu.VMEM((partners, width), BF16)],
-        compiler_params=pltpu.CompilerParams(vmem_limit_bytes=24 * 2**20),
+        scratch_shapes=[
+            pltpu.VMEM((2, count, width), BF16),
+            pltpu.VMEM((2, partners // 2, width), BF16),
+        ],
+        compiler_params=pltpu.CompilerParams(vmem_limit_bytes=28 * 2**20),
         cost_estimate=pl.CostEstimate(
-            flops=8 * count * partners * width,
+            flops=4 * count * partners * width,
             bytes_accessed=12 * count * width + 2 * partners * width,
-            transcendentals=2 * count * partners,
+            transcendentals=count * partners,
         ),
     )(factors, own_ids, other_ids, mine, theirs, *others)
 
@@ -72,7 +94,7 @@
 def local(image_features, text_features, image_weight, text_weight, log_scale, logit_bias):
     scale = jnp.exp(log_scale[0])
     bias = logit_bias[0]
-    zl, y, c, zh, x = (lax.axis_index(axis) for axis in ("zl", "y", "c", "zh", "x"))
+    zl, y, c, x = (lax.axis_index(axis) for axis in ("zl", "y", "c", "x"))
     rows, depth = image_features.shape
     width = image_weight.shape[1]
     own = rows // SIZES["x"]
@@ -94,33 +116,36 @@
         theirs = shifted(mine, "c", 1)
 
     with jax.named_scope("gather_others"):
-        half = own // 2
-        column = lax.dynamic_slice_in_dim(vec.reshape(2, own, width), zh * half, half, axis=1)
-        column = lax.all_gather(column.reshape(2 * half, width), "zl", tiled=True)
+        behind, ahead = along_z(vec, 1), along_z(vec, -1)
+        near = jnp.concatenate([vec, behind, ahead])
+        far = [along_z(near, 3), along_z(jnp.concatenate([vec, behind]), -3)]
+        column = jnp.concatenate([near] + far)
         others = [column] + [shifted(column, "x", by) for by in STEPS[1:]]
 
     with jax.named_scope("pairs"):
-        hy, hkind, hrow = flat(SIZES["y"], 2, own)
-        data = (zl * SIZES["y"] + hy) * 2
-        row = x * own + hrow
-        mine_id = (data + c) * rows + row
-        theirs_id = (data + 1 - c) * rows + row
-        ostep, ozl, okind, orow = flat(len(STEPS), SIZES["zl"], 2, half)
-        step = jnp.where(ostep == 0, 0, jnp.where(ostep == 1, 1, jnp.where(ostep == 2, 3, 2)))
-        place = (x - step + SIZES["x"]) % SIZES["x"]
-        other_id = ((ozl * SIZES["y"] + y) * 2 + c) * rows + place * own + zh * half + orow
-        kinds = jnp.stack([hkind, hkind], axis=1)
-        own_ids = jnp.concatenate([jnp.stack([mine_id, theirs_id], axis=1), kinds], axis=1)
-        other_ids = jnp.stack([other_id, okind])
+        hc, hy, hrow = flat(2, SIZES["y"], own)
+        held_data = (zl * SIZES["y"] + hy) * 2 + jnp.where(hc == 0, c, 1 - c)
+        held_id = held_data * rows + x * own + hrow
+        orow = lax.iota(jnp.int32, own)
+        other_id = []
+        for step in STEPS:
+            for group in GROUPS:
+                data = ((zl + group + SIZES["zl"]) % SIZES["zl"] * SIZES["y"] + y) * 2 + c
+                place = (x - step + SIZES["x"]) % SIZES["x"]
+                other_id.append(data * rows + place * own + orow)
         mine_sum, theirs_sum = pair_sums(
-            jnp.stack([scale, bias]), own_ids, other_ids, mine, theirs, others
+            jnp.stack([scale, bias]),
+            held_id[:, None],
+            jnp.concatenate(other_id)[None, :],
+            mine,
+            theirs,
+            others,
         )
 
     with jax.named_scope("reduce_pairs"):
         direction = mine_sum + shifted(theirs_sum, "c", 1)
         direction = exchange(direction.astype(BF16).reshape(SIZES["y"], 2 * own, width), "y")
-        direction = jnp.sum(direction.astype(F32), axis=0)
-        direction = scale * (direction + shifted(direction, "zh", 1))
+        direction = scale * jnp.sum(direction.astype(F32), axis=0)
 
     with jax.named_scope("back"):
         inner = jnp.sum(unit * direction, axis=-1, keepdims=True)

time: 242 us -> 203 us (0.84)
  blocking collectives: 82.3 us -> 24.6 us
  starting transfers between devices: 71 us -> 103 us
  waiting for transfers between devices: 70.6 us -> 56.7 us
    all_gather x1 -> x0, blocking collectives: 50.2 us -> none  [local(): column = lax.all_gather(column.reshape(2 * half, width), 'zl', tiled=True)]
    ppermute x0 -> x4, starting transfers between devices: none -> 28.7 us  [along_z(): return lax.ppermute(value, ('zl', 'zh'), pairs)]
    ppermute x8 -> x7, waiting for transfers between devices: 28 us -> 15.7 us  [shifted(): lax.ppermute(value, axis, [(i, (i + by) % size) for i in range(size)])]
    all_to_all x3 -> x4, starting transfers between devices: 14.9 us -> 26.2 us  [exchange(): return lax.all_to_all(blocks, axes, 0, 0, tiled=True)]
    all_to_all x3 -> x4, waiting for transfers between devices: 42.6 us -> 33.7 us  [exchange(): return lax.all_to_all(blocks, axes, 0, 0, tiled=True)]
    ppermute x8 -> x7, starting transfers between devices: 56.1 us -> 48.2 us  [shifted(): lax.ppermute(value, axis, [(i, (i + by) % size) for i in range(size)])]
    all_to_all x2 -> x1, blocking collectives: 32.1 us -> 24.6 us  [exchange(): return lax.all_to_all(blocks, axes, 0, 0, tiled=True)]
    ppermute x0 -> x4, waiting for transfers between devices: none -> 7.31 us  [along_z(): return lax.ppermute(value, ('zl', 'zh'), pairs)]
  transfers between devices with their start and end apart: 11 -> 15, of which waited for: 10 -> 8; matrix products, arithmetic and copies ran while one was open for 1% -> 1% of each run, Pallas kernels for 0% -> 0%
where the time goes in v4:
time: 203 us
  starting transfers between devices  103 us (51%)
  waiting for transfers between devices  56.7 us (28%)
  blocking collectives  24.6 us (12%)
  local copies, waits for them, and re-layouts  6.62 us (3%)
  matrix products  4.15 us (2%)
  Pallas kernels  2.89 us (1%)
  between operations  2.39 us (1%)
  other arithmetic  2.14 us (1%)
    ppermute x7, starting transfers between devices, shifted(): lax.ppermute(value, axis, [(i, (i + by) % size) for i in range(size)])  48.2 us
    all_to_all x4, waiting for transfers between devices, exchange(): return lax.all_to_all(blocks, axes, 0, 0, tiled=True)  33.7 us
    ppermute x4, starting transfers between devices, along_z(): return lax.ppermute(value, ('zl', 'zh'), pairs)  28.7 us
    all_to_all x4, starting transfers between devices, exchange(): return lax.all_to_all(blocks, axes, 0, 0, tiled=True)  26.2 us
    all_to_all x1, blocking collectives, exchange(): return lax.all_to_all(blocks, axes, 0, 0, tiled=True)  24.6 us
    ppermute x7, waiting for transfers between devices, shifted(): lax.ppermute(value, axis, [(i, (i + by) % size) for i in range(size)])  15.7 us
    ppermute x4, waiting for transfers between devices, along_z(): return lax.ppermute(value, ('zl', 'zh'), pairs)  7.31 us
    dot_general x4, matrix products, dot(): return lax.dot_general(a, b, (dims, ((), ())), preferred_element_type=F32)  4.15 us
  transfers between devices with their start and end apart: 15, of which 8 were waited for; matrix products, arithmetic and copies ran while one was open for 1% of the time, Pallas kernels for 0%

profile of v4, /device:TPU:1, one launch (start us, length us, event | category | flops | bytes accessed | tf_op | source)
XLA Modules:
  0.0 202.5 jit_solution(14070496907333607675)
XLA Ops:
  0.6 1.2 convolution_convert_fusion.1
  1.8 1.2 convolution_convert_fusion
  3.0 0.7 pad_maximum_fusion
  3.8 4.8 %all-to-all-start = ((bf16[4,32,1152]{2,1,0:T(8,128)(2,1)}), bf16[4,32,1152]{2,1,0:T(8,128)(2,1)S(1)}, u32[]{:S(2)}, u32[]{:S(2)}) async-start(bf16[4,32,1152]{2,1,0:T(8,128)(2,1)} %pad_maximum_fusion), calls=%async_computation | async-start | bytes 589824 | tf_op jit(solution)/shard_map/embed/all_to_all | solution.py:25
  8.7 5.6 %all-to-all-done = bf16[4,32,1152]{2,1,0:T(8,128)(2,1)S(1)} async-done(((bf16[4,32,1152]{2,1,0:T(8,128)(2,1)}), bf16[4,32,1152]{2,1,0:T(8,128)(2,1)S(1)}, u32[]{:S(2)}, u32[]{:S(2)}) %all-to-all-start) | async-done | bytes 294944 | tf_op jit(solution)/shard_map/embed/all_to_all | solution.py:25
  14.3 19.2 %collective-permute-start = (f32[32,1152]{1,0:T(8,128)S(1)}, f32[32,1152]{1,0:T(8,128)S(1)}, u32[]{:S(2)}, u32[]{:S(2)}) collective-permute-start(f32[32,1152]{1,0:T(8,128)S(1)} %convert_reduce_fusion.2), channel_id=1, source_target_pairs={{0,4},{4,0},{1,5},{5,1},{2,6},{6,2},{3,7},{7,3},{8,12},{12,8},{9,1... | collective-permute-start | bytes 442376 | tf_op jit(solution)/shard_map/embed/ppermute | solution.py:34
  33.6 2.8 %collective-permute-done = f32[32,1152]{1,0:T(8,128)S(1)} collective-permute-done((f32[32,1152]{1,0:T(8,128)S(1)}, f32[32,1152]{1,0:T(8,128)S(1)}, u32[]{:S(2)}, u32[]{:S(2)}) %collective-permute-start) | collective-permute-done | bytes 147488 | tf_op jit(solution)/shard_map/embed/ppermute | solution.py:34
  36.6 2.8 %collective-permute-start.2 = (bf16[32,1152]{1,0:T(8,128)(2,1)S(1)}, bf16[32,1152]{1,0:T(8,128)(2,1)S(1)}, u32[]{:S(2)}, u32[]{:S(2)}) collective-permute-start(bf16[32,1152]{1,0:T(8,128)(2,1)S(1)} %get-tuple-element.9), channel_id=1, source_target_pairs={{0,128},{128,256},{256,384},{384,512},{512,640},{640,768},{768,896... | collective-permute-start | bytes 221192 | tf_op jit(solution)/shard_map/gather_others/ppermute | solution.py:41
  39.4 10.3 %collective-permute-start.3 = (bf16[32,1152]{1,0:T(8,128)(2,1)S(1)}, bf16[32,1152]{1,0:T(8,128)(2,1)S(1)}, u32[]{:S(2)}, u32[]{:S(2)}) collective-permute-start(bf16[32,1152]{1,0:T(8,128)(2,1)S(1)} %get-tuple-element.9), channel_id=1, source_target_pairs={{0,900},{128,0},{256,128},{384,256},{512,384},{640,512},{768,640},... | collective-permute-start | bytes 221192 | tf_op jit(solution)/shard_map/gather_others/ppermute | solution.py:41
  49.7 0.9 broadcast_in_dim.39
  50.6 6.8 %all-to-all-start.1 = ((bf16[8,32,1152]{2,1,0:T(8,128)(2,1)}), bf16[8,32,1152]{2,1,0:T(8,128)(2,1)S(1)}, u32[]{:S(2)}, u32[]{:S(2)}) async-start(bf16[8,32,1152]{2,1,0:T(8,128)(2,1)} %broadcast_in_dim.39), calls=%async_computation.1 | async-start | bytes 1179648 | tf_op jit(solution)/shard_map/gather_own/all_to_all | solution.py:25
  57.5 3.4 %collective-permute-start.4 = (bf16[96,1152]{1,0:T(8,128)(2,1)S(1)}, bf16[96,1152]{1,0:T(8,128)(2,1)S(1)}, u32[]{:S(2)}, u32[]{:S(2)}) collective-permute-start(bf16[96,1152]{1,0:T(8,128)(2,1)S(1)} %pad_maximum_fusion.1), channel_id=1, source_target_pairs={{0,384},{128,512},{256,640},{384,768},{512,896},{640,4},{768,132},... | collective-permute-start | bytes 663560 | tf_op jit(solution)/shard_map/gather_others/ppermute | solution.py:41
  60.9 12.2 %collective-permute-start.5 = (bf16[64,1152]{1,0:T(8,128)(2,1)S(1)}, bf16[64,1152]{1,0:T(8,128)(2,1)S(1)}, u32[]{:S(2)}, u32[]{:S(2)}) collective-permute-start(bf16[64,1152]{1,0:T(8,128)(2,1)S(1)} %pad_maximum_fusion.2), channel_id=1, source_target_pairs={{0,644},{128,772},{256,900},{384,0},{512,128},{640,256},{768,384},... | collective-permute-start | bytes 442376 | tf_op jit(solution)/shard_map/gather_others/ppermute | solution.py:41
  73.1 7.3 %collective-permute-done.4 = bf16[96,1152]{1,0:T(8,128)(2,1)S(1)} collective-permute-done((bf16[96,1152]{1,0:T(8,128)(2,1)S(1)}, bf16[96,1152]{1,0:T(8,128)(2,1)S(1)}, u32[]{:S(2)}, u32[]{:S(2)}) %collective-permute-start.4) | collective-permute-done | bytes 221216 | tf_op jit(solution)/shard_map/gather_others/ppermute | solution.py:41
  80.5 2.2 %collective-permute-start.6 = (bf16[256,1152]{1,0:T(8,128)(2,1)S(1)}, bf16[256,1152]{1,0:T(8,128)(2,1)S(1)}, u32[]{:S(2)}, u32[]{:S(2)}) collective-permute-start(bf16[256,1152]{1,0:T(8,128)(2,1)S(1)} %constant_dynamic-update-slice_fusion.refs_0_), channel_id=1, source_target_pairs={{0,1},{1,2},{2,3},{3,0},{4,5},{5,6},{6,7},{7,4},{8,9},{9,10},{10,1... | collective-permute-start | bytes 1769480 | tf_op jit(solution)/shard_map/gather_others/ppermute | solution.py:34
  82.7 4.3 %collective-permute-start.7 = (bf16[256,1152]{1,0:T(8,128)(2,1)S(1)}, bf16[256,1152]{1,0:T(8,128)(2,1)S(1)}, u32[]{:S(2)}, u32[]{:S(2)}) collective-permute-start(bf16[256,1152]{1,0:T(8,128)(2,1)S(1)} %constant_dynamic-update-slice_fusion.refs_0_), channel_id=1, source_target_pairs={{0,3},{1,0},{2,1},{3,2},{4,7},{5,4},{6,5},{7,6},{8,11},{9,8},{10,9... | collective-permute-start | bytes 1769480 | tf_op jit(solution)/shard_map/gather_others/ppermute | solution.py:34
  87.0 1.9 collective-permute-start.8
  88.9 6.8 %collective-permute-start.1 = (bf16[256,1152]{1,0:T(8,128)(2,1)S(1)}, bf16[256,1152]{1,0:T(8,128)(2,1)}, u32[]{:S(2)}, u32[]{:S(2)}) collective-permute-start(bf16[256,1152]{1,0:T(8,128)(2,1)S(1)} %bitcast.26), channel_id=1, source_target_pairs={{0,8},{8,0},{1,9},{9,1},{2,10},{10,2},{3,11},{11,3},{4,12},{12,4},... | collective-permute-start | bytes 1769480 | tf_op jit(solution)/shard_map/gather_own/ppermute | solution.py:34
  97.5 8.6 %collective-permute-done.8.refs_3_ = bf16[256,1152]{1,0:T(8,128)(2,1)S(1)} collective-permute-done((bf16[256,1152]{1,0:T(8,128)(2,1)S(1)}, bf16[256,1152]{1,0:T(8,128)(2,1)S(1)}, u32[]{:S(2)}, u32[]{:S(2)}) %collective-permute-start.8) | collective-permute-done | bytes 589856 | tf_op jit(solution)/shard_map/gather_others/ppermute | solution.py:34
  106.1 2.9 %pairs.1 = (f32[256,1152]{1,0:T(8,128)S(1)}, f32[256,1152]{1,0:T(8,128)S(1)}) custom-call(f32[2]{0:T(128)S(1)} %pad_maximum_fusion.3.factors, s32[256,1]{1,0:T(8,128)S(1)} %reshape.160.own_ids, s32[1,512]{1,0:T(1,128)S(1)} %bitcast.28, bf16[256,1152]{1,0:T(8,128)(2,1)S(1)} %bitcast.27, bf16[256,1152]{1,0:T(8,128)(2,1)} %collective-permute-done.1.theirs, ...), custom_call_target="tpu_custom_call" | custom-call | flops 1207959552 | bytes 5898240 | tf_op jit(solution)/shard_map/pairs/pallas_call | solution.py:76
  109.0 9.0 %collective-permute-start.9 = (f32[256,1152]{1,0:T(8,128)S(1)}, f32[256,1152]{1,0:T(8,128)S(1)}, u32[]{:S(2)}, u32[]{:S(2)}) collective-permute-start(f32[256,1152]{1,0:T(8,128)S(1)} %get-tuple-element.7), channel_id=1, source_target_pairs={{0,8},{8,0},{1,9},{9,1},{2,10},{10,2},{3,11},{11,3},{4,12},{12,4},... | collective-permute-start | bytes 3538952 | tf_op jit(solution)/shard_map/reduce_pairs/ppermute | solution.py:34
  118.0 2.5 %collective-permute-done.9 = f32[256,1152]{1,0:T(8,128)S(1)} collective-permute-done((f32[256,1152]{1,0:T(8,128)S(1)}, f32[256,1152]{1,0:T(8,128)S(1)}, u32[]{:S(2)}, u32[]{:S(2)}) %collective-permute-start.9) | collective-permute-done | bytes 1179680 | tf_op jit(solution)/shard_map/reduce_pairs/ppermute | solution.py:34
  120.6 24.6 %all_to_all.25 = bf16[8,32,1152]{2,1,0:T(8,128)(2,1)S(1)} all-to-all(bf16[8,32,1152]{2,1,0:T(8,128)(2,1)S(1)} %bitcast.29), channel_id=1, replica_groups=mesh['zl'=8,'y'=8,'c'=2,'zh'=2,'x'=4] {'y'}, dimensions={0} | all-to-all | bytes 1179648 | tf_op jit(solution)/shard_map/reduce_pairs/all_to_all | solution.py:25
  146.3 4.6 %all-to-all-start.3 = ((bf16[4,32,1152]{2,1,0:T(8,128)(2,1)}), bf16[4,32,1152]{2,1,0:T(8,128)(2,1)S(1)}, u32[]{:S(2)}, u32[]{:S(2)}) async-start(bf16[4,32,1152]{2,1,0:T(8,128)(2,1)} %broadcast_in_dim.40), calls=%async_computation.3 | async-start | bytes 589824 | tf_op jit(solution)/shard_map/back/all_to_all | solution.py:25
  151.3 5.4 %all-to-all-done.3 = bf16[4,32,1152]{2,1,0:T(8,128)(2,1)S(1)} async-done(((bf16[4,32,1152]{2,1,0:T(8,128)(2,1)}), bf16[4,32,1152]{2,1,0:T(8,128)(2,1)S(1)}, u32[]{:S(2)}, u32[]{:S(2)}) %all-to-all-start.3) | async-done | bytes 294944 | tf_op jit(solution)/shard_map/back/all_to_all | solution.py:25
  156.7 1.4 fusion.3
  158.3 4.8 %collective-permute-start.10 = (f32[576,288]{0,1:T(8,128)S(1)}, f32[576,288]{0,1:T(8,128)S(1)}, u32[]{:S(2)}, u32[]{:S(2)}) collective-permute-start(f32[576,288]{0,1:T(8,128)S(1)} %slice.25), channel_id=1, source_target_pairs={{0,8},{8,0},{1,9},{9,1},{2,10},{10,2},{3,11},{11,3},{4,12},{12,4},... | collective-permute-start | bytes 1990664 | tf_op jit(solution)/shard_map/weight_grad/ppermute | solution.py:34
  163.1 1.8 collective-permute-done.10
  165.5 1.6 reshape.161
  167.0 9.9 %all-to-all-start.4 = ((bf16[64,2,1296]{2,1,0:T(2,128)(2,1)}), bf16[64,2,1296]{2,1,0:T(2,128)(2,1)S(1)}, u32[]{:S(2)}, u32[]{:S(2)}) async-start(bf16[64,2,1296]{2,1,0:T(2,128)(2,1)} %reshape.161), calls=%async_computation.4 | async-start | bytes 720896 | tf_op jit(solution)/shard_map/weight_grad/all_to_all | solution.py:25
  178.0 22.7 %all-to-all-done.4 = bf16[64,2,1296]{2,1,0:T(2,128)(2,1)S(1)} async-done(((bf16[64,2,1296]{2,1,0:T(2,128)(2,1)}), bf16[64,2,1296]{2,1,0:T(2,128)(2,1)S(1)}, u32[]{:S(2)}, u32[]{:S(2)}) %all-to-all-start.4) | async-done | bytes 331808 | tf_op jit(solution)/shard_map/weight_grad/all_to_all | solution.py:25
  200.8 0.9 reshape.162
  (61 shorter events, 5.1 us)
Async XLA Ops:
  3.8 10.5 %all-to-all-start = ((bf16[4,32,1152]{2,1,0:T(8,128)(2,1)}), bf16[4,32,1152]{2,1,0:T(8,128)(2,1)S(1)}, u32[]{:S(2)}, u32[]{:S(2)}) async-start(bf16[4,32,1152]{2,1,0:T(8,128)(2,1)} %pad_maximum_fusion), calls=%async_computation | async-start | bytes 589824 | tf_op jit(solution)/shard_map/embed/all_to_all | solution.py:25
  14.3 22.0 %collective-permute-start = (f32[32,1152]{1,0:T(8,128)S(1)}, f32[32,1152]{1,0:T(8,128)S(1)}, u32[]{:S(2)}, u32[]{:S(2)}) collective-permute-start(f32[32,1152]{1,0:T(8,128)S(1)} %convert_reduce_fusion.2), channel_id=1, source_target_pairs={{0,4},{4,0},{1,5},{5,1},{2,6},{6,2},{3,7},{7,3},{8,12},{12,8},{9,1... | collective-permute-start | bytes 442376 | tf_op jit(solution)/shard_map/embed/ppermute | solution.py:34
  36.6 20.8 %collective-permute-start.2 = (bf16[32,1152]{1,0:T(8,128)(2,1)S(1)}, bf16[32,1152]{1,0:T(8,128)(2,1)S(1)}, u32[]{:S(2)}, u32[]{:S(2)}) collective-permute-start(bf16[32,1152]{1,0:T(8,128)(2,1)S(1)} %get-tuple-element.9), channel_id=1, source_target_pairs={{0,128},{128,256},{256,384},{384,512},{512,640},{640,768},{768,896... | collective-permute-start | bytes 221192 | tf_op jit(solution)/shard_map/gather_others/ppermute | solution.py:41
  39.4 18.0 %collective-permute-start.3 = (bf16[32,1152]{1,0:T(8,128)(2,1)S(1)}, bf16[32,1152]{1,0:T(8,128)(2,1)S(1)}, u32[]{:S(2)}, u32[]{:S(2)}) collective-permute-start(bf16[32,1152]{1,0:T(8,128)(2,1)S(1)} %get-tuple-element.9), channel_id=1, source_target_pairs={{0,900},{128,0},{256,128},{384,256},{512,384},{640,512},{768,640},... | collective-permute-start | bytes 221192 | tf_op jit(solution)/shard_map/gather_others/ppermute | solution.py:41
  50.6 38.4 %all-to-all-start.1 = ((bf16[8,32,1152]{2,1,0:T(8,128)(2,1)}), bf16[8,32,1152]{2,1,0:T(8,128)(2,1)S(1)}, u32[]{:S(2)}, u32[]{:S(2)}) async-start(bf16[8,32,1152]{2,1,0:T(8,128)(2,1)} %broadcast_in_dim.39), calls=%async_computation.1 | async-start | bytes 1179648 | tf_op jit(solution)/shard_map/gather_own/all_to_all | solution.py:25
  57.5 23.0 %collective-permute-start.4 = (bf16[96,1152]{1,0:T(8,128)(2,1)S(1)}, bf16[96,1152]{1,0:T(8,128)(2,1)S(1)}, u32[]{:S(2)}, u32[]{:S(2)}) collective-permute-start(bf16[96,1152]{1,0:T(8,128)(2,1)S(1)} %pad_maximum_fusion.1), channel_id=1, source_target_pairs={{0,384},{128,512},{256,640},{384,768},{512,896},{640,4},{768,132},... | collective-permute-start | bytes 663560 | tf_op jit(solution)/shard_map/gather_others/ppermute | solution.py:41
  60.9 19.6 %collective-permute-start.5 = (bf16[64,1152]{1,0:T(8,128)(2,1)S(1)}, bf16[64,1152]{1,0:T(8,128)(2,1)S(1)}, u32[]{:S(2)}, u32[]{:S(2)}) collective-permute-start(bf16[64,1152]{1,0:T(8,128)(2,1)S(1)} %pad_maximum_fusion.2), channel_id=1, source_target_pairs={{0,644},{128,772},{256,900},{384,0},{512,128},{640,256},{768,384},... | collective-permute-start | bytes 442376 | tf_op jit(solution)/shard_map/gather_others/ppermute | solution.py:41
  80.5 17.0 %collective-permute-start.6 = (bf16[256,1152]{1,0:T(8,128)(2,1)S(1)}, bf16[256,1152]{1,0:T(8,128)(2,1)S(1)}, u32[]{:S(2)}, u32[]{:S(2)}) collective-permute-start(bf16[256,1152]{1,0:T(8,128)(2,1)S(1)} %constant_dynamic-update-slice_fusion.refs_0_), channel_id=1, source_target_pairs={{0,1},{1,2},{2,3},{3,0},{4,5},{5,6},{6,7},{7,4},{8,9},{9,10},{10,1... | collective-permute-start | bytes 1769480 | tf_op jit(solution)/shard_map/gather_others/ppermute | solution.py:34
  82.7 14.8 %collective-permute-start.7 = (bf16[256,1152]{1,0:T(8,128)(2,1)S(1)}, bf16[256,1152]{1,0:T(8,128)(2,1)S(1)}, u32[]{:S(2)}, u32[]{:S(2)}) collective-permute-start(bf16[256,1152]{1,0:T(8,128)(2,1)S(1)} %constant_dynamic-update-slice_fusion.refs_0_), channel_id=1, source_target_pairs={{0,3},{1,0},{2,1},{3,2},{4,7},{5,4},{6,5},{7,6},{8,11},{9,8},{10,9... | collective-permute-start | bytes 1769480 | tf_op jit(solution)/shard_map/gather_others/ppermute | solution.py:34
  87.0 19.1 %collective-permute-start.8 = (bf16[256,1152]{1,0:T(8,128)(2,1)S(1)}, bf16[256,1152]{1,0:T(8,128)(2,1)S(1)}, u32[]{:S(2)}, u32[]{:S(2)}) collective-permute-start(bf16[256,1152]{1,0:T(8,128)(2,1)S(1)} %constant_dynamic-update-slice_fusion.refs_0_), channel_id=1, source_target_pairs={{0,2},{1,3},{2,0},{3,1},{4,6},{5,7},{6,4},{7,5},{8,10},{9,11},{10,... | collective-permute-start | bytes 1769480 | tf_op jit(solution)/shard_map/gather_others/ppermute | solution.py:34
  88.9 17.2 %collective-permute-start.1 = (bf16[256,1152]{1,0:T(8,128)(2,1)S(1)}, bf16[256,1152]{1,0:T(8,128)(2,1)}, u32[]{:S(2)}, u32[]{:S(2)}) collective-permute-start(bf16[256,1152]{1,0:T(8,128)(2,1)S(1)} %bitcast.26), channel_id=1, source_target_pairs={{0,8},{8,0},{1,9},{9,1},{2,10},{10,2},{3,11},{11,3},{4,12},{12,4},... | collective-permute-start | bytes 1769480 | tf_op jit(solution)/shard_map/gather_own/ppermute | solution.py:34
  109.0 11.4 %collective-permute-start.9 = (f32[256,1152]{1,0:T(8,128)S(1)}, f32[256,1152]{1,0:T(8,128)S(1)}, u32[]{:S(2)}, u32[]{:S(2)}) collective-permute-start(f32[256,1152]{1,0:T(8,128)S(1)} %get-tuple-element.7), channel_id=1, source_target_pairs={{0,8},{8,0},{1,9},{9,1},{2,10},{10,2},{3,11},{11,3},{4,12},{12,4},... | collective-permute-start | bytes 3538952 | tf_op jit(solution)/shard_map/reduce_pairs/ppermute | solution.py:34
  145.2 6.0 %copy-start.2 = (bf16[64,144]{1,0:T(8,128)(2,1)S(1)}, bf16[64,144]{1,0:T(8,128)(2,1)}, u32[]{:S(2)}) copy-start(bf16[64,144]{1,0:T(8,128)(2,1)} %param.7) | copy-start | bytes 55300
  145.2 6.0 %copy-start.3 = (bf16[64,144]{1,0:T(8,128)(2,1)S(1)}, bf16[64,144]{1,0:T(8,128)(2,1)}, u32[]{:S(2)}) copy-start(bf16[64,144]{1,0:T(8,128)(2,1)} %param.6) | copy-start | bytes 55300
  146.3 10.3 %all-to-all-start.3 = ((bf16[4,32,1152]{2,1,0:T(8,128)(2,1)}), bf16[4,32,1152]{2,1,0:T(8,128)(2,1)S(1)}, u32[]{:S(2)}, u32[]{:S(2)}) async-start(bf16[4,32,1152]{2,1,0:T(8,128)(2,1)} %broadcast_in_dim.40), calls=%async_computation.3 | async-start | bytes 589824 | tf_op jit(solution)/shard_map/back/all_to_all | solution.py:25
  158.3 6.6 %collective-permute-start.10 = (f32[576,288]{0,1:T(8,128)S(1)}, f32[576,288]{0,1:T(8,128)S(1)}, u32[]{:S(2)}, u32[]{:S(2)}) collective-permute-start(f32[576,288]{0,1:T(8,128)S(1)} %slice.25), channel_id=1, source_target_pairs={{0,8},{8,0},{1,9},{9,1},{2,10},{10,2},{3,11},{11,3},{4,12},{12,4},... | collective-permute-start | bytes 1990664 | tf_op jit(solution)/shard_map/weight_grad/ppermute | solution.py:34
  165.2 11.6 %copy-start = (bf16[144,1152]{1,0:T(8,128)(2,1)S(1)}, bf16[144,1152]{1,0:T(8,128)(2,1)}, u32[]{:S(2)}) copy-start(bf16[144,1152]{1,0:T(8,128)(2,1)} %param.9) | copy-start | bytes 995332
  165.3 11.6 %copy-start.1 = (bf16[144,1152]{1,0:T(8,128)(2,1)S(1)}, bf16[144,1152]{1,0:T(8,128)(2,1)}, u32[]{:S(2)}) copy-start(bf16[144,1152]{1,0:T(8,128)(2,1)} %param.8) | copy-start | bytes 995332
  167.0 33.8 %all-to-all-start.4 = ((bf16[64,2,1296]{2,1,0:T(2,128)(2,1)}), bf16[64,2,1296]{2,1,0:T(2,128)(2,1)S(1)}, u32[]{:S(2)}, u32[]{:S(2)}) async-start(bf16[64,2,1296]{2,1,0:T(2,128)(2,1)} %reshape.161), calls=%async_computation.4 | async-start | bytes 720896 | tf_op jit(solution)/shard_map/weight_grad/all_to_all | solution.py:25

commit v5 on v4

--- a/solution.py
+++ b/solution.py
@@ -10,8 +10,8 @@
 TENSOR = ("zh", "x")
 SIZES = {"zl": 8, "y": 8, "c": 2, "zh": 2, "x": 4}
 STEPS = (0, 1, 3, 2)
-FIRST = (0, -1, 1)
-GROUPS = FIRST + (-3, -4, -2, 3, 2)
+NEAR = (0, -1, 1)
+FAR = (-3, -4, -2, 3, 2)
 RUN = 16
 F32 = jnp.float32
 BF16 = jnp.bfloat16
@@ -46,7 +46,7 @@
 
 
 def pair_kernel(factors, own_ids, other_ids, mine, theirs, *refs):
-    blocks, (mine_sum, theirs_sum, held, partners) = refs[: len(STEPS)], refs[len(STEPS) :]
+    blocks, (mine_sum, theirs_sum, held, partners) = refs[:-4], refs[-4:]
     run = RUN
     for kind in range(2):
         for target, sources in ((held, (mine, theirs)), (partners, blocks)):
@@ -70,7 +70,7 @@
 
 def pair_sums(factors, own_ids, other_ids, mine, theirs, others):
     count, width = mine.shape
-    partners = len(others) * others[0].shape[0]
+    partners = sum(block.shape[0] for block in others)
     whole = pl.BlockSpec(memory_space=pltpu.VMEM)
     out = jax.ShapeDtypeStruct((count, width), F32)
     return pl.pallas_call(
@@ -111,16 +111,19 @@
         unit = embed * inverse
         vec = unit.astype(BF16)
 
-    with jax.named_scope("gather_own"):
-        mine = spread(vec, "y", SIZES["y"]).reshape(-1, width)
-        theirs = shifted(mine, "c", 1)
-
     with jax.named_scope("gather_others"):
         behind, ahead = along_z(vec, 1), along_z(vec, -1)
         near = jnp.concatenate([vec, behind, ahead])
         far = [along_z(near, 3), along_z(jnp.concatenate([vec, behind]), -3)]
-        column = jnp.concatenate([near] + far)
-        others = [column] + [shifted(column, "x", by) for by in STEPS[1:]]
+        near_moved = [shifted(near, "x", by) for by in STEPS[1:]]
+        vec, near_moved[0] = lax.optimization_barrier((vec, near_moved[0]))
+        far = jnp.concatenate(far)
+        far_moved = [shifted(far, "x", by) for by in STEPS[1:]]
+        others = [near, *near_moved, far, *far_moved]
+
+    with jax.named_scope("gather_own"):
+        mine = spread(vec, "y", SIZES["y"]).reshape(-1, width)
+        theirs = shifted(mine, "c", 1)
 
     with jax.named_scope("pairs"):
         hc, hy, hrow = flat(2, SIZES["y"], own)
@@ -128,8 +131,8 @@
         held_id = held_data * rows + x * own + hrow
         orow = lax.iota(jnp.int32, own)
         other_id = []
-        for step in STEPS:
-            for group in GROUPS:
+        for groups in (NEAR, FAR):
+            for step, group in ((step, group) for step in STEPS for group in groups):
                 data = ((zl + group + SIZES["zl"]) % SIZES["zl"] * SIZES["y"] + y) * 2 + c
                 place = (x - step + SIZES["x"]) % SIZES["x"]
                 other_id.append(data * rows + place * own + orow)

time: 203 us -> 214 us (1.054)
  waiting for transfers between devices: 56.7 us -> 70.7 us
  starting transfers between devices: 103 us -> 96.8 us
  other arithmetic: 2.14 us -> 4.37 us
    ppermute x7 -> x10, waiting for transfers between devices: 15.7 us -> 24.8 us  [shifted(): lax.ppermute(value, axis, [(i, (i + by) % size) for i in range(size)])]
    all_to_all x4, starting transfers between devices: 26.2 us -> 19.9 us  [exchange(): return lax.all_to_all(blocks, axes, 0, 0, tiled=True)]
    ppermute x4, waiting for transfers between devices: 7.31 us -> 12.1 us  [along_z(): return lax.ppermute(value, ('zl', 'zh'), pairs)]
    add x16, other arithmetic: 0.12 us -> 2.37 us  [local(): other_id.append(data * rows + place * own + orow)]
    ppermute x7 -> x10, starting transfers between devices: 48.2 us -> 46.4 us  [shifted(): lax.ppermute(value, axis, [(i, (i + by) % size) for i in range(size)])]
  transfers between devices with their start and end apart: 15 -> 18, of which waited for: 8 -> 10; matrix products, arithmetic and copies ran while one was open for 1% -> 2% of each run, Pallas kernels for 0% -> 0%
where the time goes in v5:
time: 214 us; the launch traced here: 213 us
  starting transfers between devices  96.8 us (45%)
  waiting for transfers between devices  70.7 us (33%)
  blocking collectives  24.6 us (11%)
  local copies, waits for them, and re-layouts  7.3 us (3%)
  other arithmetic  4.37 us (2%)
  matrix products  4.15 us (2%)
  Pallas kernels  2.77 us (1%)
  between operations  2.49 us (1%)
    ppermute x10, starting transfers between devices, shifted(): lax.ppermute(value, axis, [(i, (i + by) % size) for i in range(size)])  46.4 us
    all_to_all x4, waiting for transfers between devices, exchange(): return lax.all_to_all(blocks, axes, 0, 0, tiled=True)  33.8 us
    ppermute x4, starting transfers between devices, along_z(): return lax.ppermute(value, ('zl', 'zh'), pairs)  30.5 us
    ppermute x10, waiting for transfers between devices, shifted(): lax.ppermute(value, axis, [(i, (i + by) % size) for i in range(size)])  24.8 us
    all_to_all x1, blocking collectives, exchange(): return lax.all_to_all(blocks, axes, 0, 0, tiled=True)  24.6 us
    all_to_all x4, starting transfers between devices, exchange(): return lax.all_to_all(blocks, axes, 0, 0, tiled=True)  19.9 us
    ppermute x4, waiting for transfers between devices, along_z(): return lax.ppermute(value, ('zl', 'zh'), pairs)  12.1 us
  transfers between devices with their start and end apart: 18, of which 10 were waited for; matrix products, arithmetic and copies ran while one was open for 2% of the time, Pallas kernels for 0%

profile of v5, /device:TPU:1, one launch (start us, length us, event | category | flops | bytes accessed | tf_op | source)
XLA Modules:
  0.0 213.2 jit_solution(10061719254037668153)
XLA Ops:
  3.7 4.8 %all-to-all-start = ((bf16[4,32,1152]{2,1,0:T(8,128)(2,1)}), bf16[4,32,1152]{2,1,0:T(8,128)(2,1)S(1)}, u32[]{:S(2)}, u32[]{:S(2)}) async-start(bf16[4,32,1152]{2,1,0:T(8,128)(2,1)} %pad_maximum_fusion), calls=%async_computation | async-start | bytes 589824 | tf_op jit(solution)/shard_map/embed/all_to_all | solution.py:25
  8.6 5.7 %all-to-all-done = bf16[4,32,1152]{2,1,0:T(8,128)(2,1)S(1)} async-done(((bf16[4,32,1152]{2,1,0:T(8,128)(2,1)}), bf16[4,32,1152]{2,1,0:T(8,128)(2,1)S(1)}, u32[]{:S(2)}, u32[]{:S(2)}) %all-to-all-start) | async-done | bytes 294944 | tf_op jit(solution)/shard_map/embed/all_to_all | solution.py:25
  14.3 19.2 %collective-permute-start = (f32[32,1152]{1,0:T(8,128)S(1)}, f32[32,1152]{1,0:T(8,128)S(1)}, u32[]{:S(2)}, u32[]{:S(2)}) collective-permute-start(f32[32,1152]{1,0:T(8,128)S(1)} %convert_reduce_fusion.2), channel_id=1, source_target_pairs={{0,4},{4,0},{1,5},{5,1},{2,6},{6,2},{3,7},{7,3},{8,12},{12,8},{9,1... | collective-permute-start | bytes 442376 | tf_op jit(solution)/shard_map/embed/ppermute | solution.py:34
  33.6 2.8 %collective-permute-done = f32[32,1152]{1,0:T(8,128)S(1)} collective-permute-done((f32[32,1152]{1,0:T(8,128)S(1)}, f32[32,1152]{1,0:T(8,128)S(1)}, u32[]{:S(2)}, u32[]{:S(2)}) %collective-permute-start) | collective-permute-done | bytes 147488 | tf_op jit(solution)/shard_map/embed/ppermute | solution.py:34
  36.6 2.8 %collective-permute-start.1 = (bf16[32,1152]{1,0:T(8,128)(2,1)S(1)}, bf16[32,1152]{1,0:T(8,128)(2,1)S(1)}, u32[]{:S(2)}, u32[]{:S(2)}) collective-permute-start(bf16[32,1152]{1,0:T(8,128)(2,1)S(1)} %multiply_convert_fusion.1), channel_id=1, source_target_pairs={{0,128},{128,256},{256,384},{384,512},{512,640},{640,768},{768,896... | collective-permute-start | bytes 221192 | tf_op jit(solution)/shard_map/gather_others/ppermute | solution.py:41
  39.4 10.3 %collective-permute-start.2 = (bf16[32,1152]{1,0:T(8,128)(2,1)S(1)}, bf16[32,1152]{1,0:T(8,128)(2,1)S(1)}, u32[]{:S(2)}, u32[]{:S(2)}) collective-permute-start(bf16[32,1152]{1,0:T(8,128)(2,1)S(1)} %multiply_convert_fusion.1), channel_id=1, source_target_pairs={{0,900},{128,0},{256,128},{384,256},{512,384},{640,512},{768,640},... | collective-permute-start | bytes 221192 | tf_op jit(solution)/shard_map/gather_others/ppermute | solution.py:41
  49.7 1.4 collective-permute-done.2
  51.1 2.2 %collective-permute-start.3 = (bf16[96,1152]{1,0:T(8,128)(2,1)S(1)}, bf16[96,1152]{1,0:T(8,128)(2,1)S(1)}, u32[]{:S(2)}, u32[]{:S(2)}) collective-permute-start(bf16[96,1152]{1,0:T(8,128)(2,1)S(1)} %pad_maximum_fusion.1.refs_0_), channel_id=1, source_target_pairs={{0,1},{1,2},{2,3},{3,0},{4,5},{5,6},{6,7},{7,4},{8,9},{9,10},{10,1... | collective-permute-start | bytes 663560 | tf_op jit(solution)/shard_map/gather_others/ppermute | solution.py:34
  53.3 5.7 %collective-permute-done.3.refs_1_ = bf16[96,1152]{1,0:T(8,128)(2,1)S(1)} collective-permute-done((bf16[96,1152]{1,0:T(8,128)(2,1)S(1)}, bf16[96,1152]{1,0:T(8,128)(2,1)S(1)}, u32[]{:S(2)}, u32[]{:S(2)}) %collective-permute-start.3) | collective-permute-done | bytes 221216 | tf_op jit(solution)/shard_map/gather_others/ppermute | solution.py:34
  59.8 6.8 %all-to-all-start.1 = ((bf16[8,32,1152]{2,1,0:T(8,128)(2,1)}), bf16[8,32,1152]{2,1,0:T(8,128)(2,1)S(1)}, u32[]{:S(2)}, u32[]{:S(2)}) async-start(bf16[8,32,1152]{2,1,0:T(8,128)(2,1)} %broadcast_in_dim.39), calls=%async_computation.1 | async-start | bytes 1179648 | tf_op jit(solution)/shard_map/gather_own/all_to_all | solution.py:25
  68.0 6.4 %collective-permute-start.7 = (bf16[96,1152]{1,0:T(8,128)(2,1)S(1)}, bf16[96,1152]{1,0:T(8,128)(2,1)S(1)}, u32[]{:S(2)}, u32[]{:S(2)}) collective-permute-start(bf16[96,1152]{1,0:T(8,128)(2,1)S(1)} %pad_maximum_fusion.1.refs_0_), channel_id=1, source_target_pairs={{0,384},{128,512},{256,640},{384,768},{512,896},{640,4},{768,132},... | collective-permute-start | bytes 663560 | tf_op jit(solution)/shard_map/gather_others/ppermute | solution.py:41
  74.3 1.9 collective-permute-start.5
  76.3 11.0 %collective-permute-start.8 = (bf16[64,1152]{1,0:T(8,128)(2,1)S(1)}, bf16[64,1152]{1,0:T(8,128)(2,1)S(1)}, u32[]{:S(2)}, u32[]{:S(2)}) collective-permute-start(bf16[64,1152]{1,0:T(8,128)(2,1)S(1)} %pad_maximum_fusion.2), channel_id=1, source_target_pairs={{0,644},{128,772},{256,900},{384,0},{512,128},{640,256},{768,384},... | collective-permute-start | bytes 442376 | tf_op jit(solution)/shard_map/gather_others/ppermute | solution.py:41
  87.3 10.8 %collective-permute-done.7 = bf16[96,1152]{1,0:T(8,128)(2,1)S(1)} collective-permute-done((bf16[96,1152]{1,0:T(8,128)(2,1)S(1)}, bf16[96,1152]{1,0:T(8,128)(2,1)S(1)}, u32[]{:S(2)}, u32[]{:S(2)}) %collective-permute-start.7) | collective-permute-done | bytes 221216 | tf_op jit(solution)/shard_map/gather_others/ppermute | solution.py:41
  98.1 3.2 %collective-permute-start.4 = (bf16[256,1152]{1,0:T(8,128)(2,1)S(1)}, bf16[256,1152]{1,0:T(8,128)(2,1)S(1)}, u32[]{:S(2)}, u32[]{:S(2)}) collective-permute-start(bf16[256,1152]{1,0:T(8,128)(2,1)S(1)} %bitcast.26), channel_id=1, source_target_pairs={{0,8},{8,0},{1,9},{9,1},{2,10},{10,2},{3,11},{11,3},{4,12},{12,4},... | collective-permute-start | bytes 1769480 | tf_op jit(solution)/shard_map/gather_own/ppermute | solution.py:34
  101.4 1.9 collective-permute-start.10
  103.3 2.7 %collective-permute-start.11 = (bf16[160,1152]{1,0:T(8,128)(2,1)S(1)}, bf16[160,1152]{1,0:T(8,128)(2,1)S(1)}, u32[]{:S(2)}, u32[]{:S(2)}) collective-permute-start(bf16[160,1152]{1,0:T(8,128)(2,1)S(1)} %constant_dynamic-update-slice_fusion.refs_4_), channel_id=1, source_target_pairs={{0,2},{1,3},{2,0},{3,1},{4,6},{5,7},{6,4},{7,5},{8,10},{9,11},{10,... | collective-permute-start | bytes 1105928 | tf_op jit(solution)/shard_map/gather_others/ppermute | solution.py:34
  106.1 2.5 %collective-permute-start.9 = (bf16[160,1152]{1,0:T(8,128)(2,1)S(1)}, bf16[160,1152]{1,0:T(8,128)(2,1)S(1)}, u32[]{:S(2)}, u32[]{:S(2)}) collective-permute-start(bf16[160,1152]{1,0:T(8,128)(2,1)S(1)} %constant_dynamic-update-slice_fusion.refs_4_), channel_id=1, source_target_pairs={{0,1},{1,2},{2,3},{3,0},{4,5},{5,6},{6,7},{7,4},{8,9},{9,10},{10,1... | collective-permute-start | bytes 1105928 | tf_op jit(solution)/shard_map/gather_others/ppermute | solution.py:34
  110.7 5.5 %collective-permute-start.6 = (bf16[96,1152]{1,0:T(8,128)(2,1)S(1)}, bf16[96,1152]{1,0:T(8,128)(2,1)}, u32[]{:S(2)}, u32[]{:S(2)}) collective-permute-start(bf16[96,1152]{1,0:T(8,128)(2,1)S(1)} %pad_maximum_fusion.1.refs_0_), channel_id=1, source_target_pairs={{0,2},{1,3},{2,0},{3,1},{4,6},{5,7},{6,4},{7,5},{8,10},{9,11},{10,... | collective-permute-start | bytes 663560 | tf_op jit(solution)/shard_map/gather_others/ppermute | solution.py:34
  117.6 12.1 %collective-permute-done.6.refs_3_ = bf16[96,1152]{1,0:T(8,128)(2,1)} collective-permute-done((bf16[96,1152]{1,0:T(8,128)(2,1)S(1)}, bf16[96,1152]{1,0:T(8,128)(2,1)}, u32[]{:S(2)}, u32[]{:S(2)}) %collective-permute-start.6) | collective-permute-done | bytes 221216 | tf_op jit(solution)/shard_map/gather_others/ppermute | solution.py:34
  129.7 2.8 %pairs.1 = (f32[256,1152]{1,0:T(8,128)S(1)}, f32[256,1152]{1,0:T(8,128)S(1)}) custom-call(f32[2]{0:T(128)S(1)} %pad_maximum_fusion.3.factors, s32[256,1]{1,0:T(8,128)S(1)} %reshape.160.own_ids, s32[1,512]{1,0:T(1,128)S(1)} %bitcast.28, bf16[256,1152]{1,0:T(8,128)(2,1)S(1)} %bitcast.27, bf16[256,1152]{1,0:T(8,128)(2,1)S(1)} %collective-permute-done.4.theirs, ...), custom_call_target="tpu_custom_call" | custom-call | flops 1207959552 | bytes 5898240 | tf_op jit(solution)/shard_map/pairs/pallas_call | solution.py:76
  132.5 2.7 %collective-permute-start.12 = (f32[256,1152]{1,0:T(8,128)S(1)}, f32[256,1152]{1,0:T(8,128)S(1)}, u32[]{:S(2)}, u32[]{:S(2)}) collective-permute-start(f32[256,1152]{1,0:T(8,128)S(1)} %get-tuple-element.11), channel_id=1, source_target_pairs={{0,8},{8,0},{1,9},{9,1},{2,10},{10,2},{3,11},{11,3},{4,12},{12,4},... | collective-permute-start | bytes 3538952 | tf_op jit(solution)/shard_map/reduce_pairs/ppermute | solution.py:34
  135.2 2.5 %collective-permute-done.12 = f32[256,1152]{1,0:T(8,128)S(1)} collective-permute-done((f32[256,1152]{1,0:T(8,128)S(1)}, f32[256,1152]{1,0:T(8,128)S(1)}, u32[]{:S(2)}, u32[]{:S(2)}) %collective-permute-start.12) | collective-permute-done | bytes 1179680 | tf_op jit(solution)/shard_map/reduce_pairs/ppermute | solution.py:34
  137.8 24.6 %all_to_all.25 = bf16[8,32,1152]{2,1,0:T(8,128)(2,1)S(1)} all-to-all(bf16[8,32,1152]{2,1,0:T(8,128)(2,1)S(1)} %bitcast.29), channel_id=1, replica_groups=mesh['zl'=8,'y'=8,'c'=2,'zh'=2,'x'=4] {'y'}, dimensions={0} | all-to-all | bytes 1179648 | tf_op jit(solution)/shard_map/reduce_pairs/all_to_all | solution.py:25
  163.6 3.5 %all-to-all-start.3 = ((bf16[4,32,1152]{2,1,0:T(8,128)(2,1)}), bf16[4,32,1152]{2,1,0:T(8,128)(2,1)S(1)}, u32[]{:S(2)}, u32[]{:S(2)}) async-start(bf16[4,32,1152]{2,1,0:T(8,128)(2,1)} %broadcast_in_dim.40), calls=%async_computation.3 | async-start | bytes 589824 | tf_op jit(solution)/shard_map/back/all_to_all | solution.py:25
  167.4 5.3 %all-to-all-done.3 = bf16[4,32,1152]{2,1,0:T(8,128)(2,1)S(1)} async-done(((bf16[4,32,1152]{2,1,0:T(8,128)(2,1)}), bf16[4,32,1152]{2,1,0:T(8,128)(2,1)S(1)}, u32[]{:S(2)}, u32[]{:S(2)}) %all-to-all-start.3) | async-done | bytes 294944 | tf_op jit(solution)/shard_map/back/all_to_all | solution.py:25
  172.7 1.4 fusion.3
  174.4 4.5 %collective-permute-start.13 = (f32[576,288]{0,1:T(8,128)S(1)}, f32[576,288]{0,1:T(8,128)S(1)}, u32[]{:S(2)}, u32[]{:S(2)}) collective-permute-start(f32[576,288]{0,1:T(8,128)S(1)} %slice.25), channel_id=1, source_target_pairs={{0,8},{8,0},{1,9},{9,1},{2,10},{10,2},{3,11},{11,3},{4,12},{12,4},... | collective-permute-start | bytes 1990664 | tf_op jit(solution)/shard_map/weight_grad/ppermute | solution.py:34
  178.9 1.8 collective-permute-done.13
  181.2 1.6 reshape.161
  182.8 4.8 %all-to-all-start.4 = ((bf16[64,2,1296]{2,1,0:T(2,128)(2,1)}), bf16[64,2,1296]{2,1,0:T(2,128)(2,1)S(1)}, u32[]{:S(2)}, u32[]{:S(2)}) async-start(bf16[64,2,1296]{2,1,0:T(2,128)(2,1)} %reshape.161), calls=%async_computation.4 | async-start | bytes 720896 | tf_op jit(solution)/shard_map/weight_grad/all_to_all | solution.py:25
  188.7 22.7 %all-to-all-done.4 = bf16[64,2,1296]{2,1,0:T(2,128)(2,1)S(1)} async-done(((bf16[64,2,1296]{2,1,0:T(2,128)(2,1)}), bf16[64,2,1296]{2,1,0:T(2,128)(2,1)S(1)}, u32[]{:S(2)}, u32[]{:S(2)}) %all-to-all-start.4) | async-done | bytes 331808 | tf_op jit(solution)/shard_map/weight_grad/all_to_all | solution.py:25
  (69 shorter events, 12.9 us)
Async XLA Ops:
  3.7 10.5 %all-to-all-start = ((bf16[4,32,1152]{2,1,0:T(8,128)(2,1)}), bf16[4,32,1152]{2,1,0:T(8,128)(2,1)S(1)}, u32[]{:S(2)}, u32[]{:S(2)}) async-start(bf16[4,32,1152]{2,1,0:T(8,128)(2,1)} %pad_maximum_fusion), calls=%async_computation | async-start | bytes 589824 | tf_op jit(solution)/shard_map/embed/all_to_all | solution.py:25
  14.3 22.0 %collective-permute-start = (f32[32,1152]{1,0:T(8,128)S(1)}, f32[32,1152]{1,0:T(8,128)S(1)}, u32[]{:S(2)}, u32[]{:S(2)}) collective-permute-start(f32[32,1152]{1,0:T(8,128)S(1)} %convert_reduce_fusion.2), channel_id=1, source_target_pairs={{0,4},{4,0},{1,5},{5,1},{2,6},{6,2},{3,7},{7,3},{8,12},{12,8},{9,1... | collective-permute-start | bytes 442376 | tf_op jit(solution)/shard_map/embed/ppermute | solution.py:34
  36.5 13.2 %copy-start = (f32[32,1152]{1,0:T(8,128)}, f32[32,1152]{1,0:T(8,128)S(1)}, u32[]{:S(2)}) copy-start(f32[32,1152]{1,0:T(8,128)S(1)} %get-tuple-element.13) | copy-start | bytes 442372
  36.6 13.1 %collective-permute-start.1 = (bf16[32,1152]{1,0:T(8,128)(2,1)S(1)}, bf16[32,1152]{1,0:T(8,128)(2,1)S(1)}, u32[]{:S(2)}, u32[]{:S(2)}) collective-permute-start(bf16[32,1152]{1,0:T(8,128)(2,1)S(1)} %multiply_convert_fusion.1), channel_id=1, source_target_pairs={{0,128},{128,256},{256,384},{384,512},{512,640},{640,768},{768,896... | collective-permute-start | bytes 221192 | tf_op jit(solution)/shard_map/gather_others/ppermute | solution.py:41
  39.4 11.7 %collective-permute-start.2 = (bf16[32,1152]{1,0:T(8,128)(2,1)S(1)}, bf16[32,1152]{1,0:T(8,128)(2,1)S(1)}, u32[]{:S(2)}, u32[]{:S(2)}) collective-permute-start(bf16[32,1152]{1,0:T(8,128)(2,1)S(1)} %multiply_convert_fusion.1), channel_id=1, source_target_pairs={{0,900},{128,0},{256,128},{384,256},{512,384},{640,512},{768,640},... | collective-permute-start | bytes 221192 | tf_op jit(solution)/shard_map/gather_others/ppermute | solution.py:41
  51.1 7.9 %collective-permute-start.3 = (bf16[96,1152]{1,0:T(8,128)(2,1)S(1)}, bf16[96,1152]{1,0:T(8,128)(2,1)S(1)}, u32[]{:S(2)}, u32[]{:S(2)}) collective-permute-start(bf16[96,1152]{1,0:T(8,128)(2,1)S(1)} %pad_maximum_fusion.1.refs_0_), channel_id=1, source_target_pairs={{0,1},{1,2},{2,3},{3,0},{4,5},{5,6},{6,7},{7,4},{8,9},{9,10},{10,1... | collective-permute-start | bytes 663560 | tf_op jit(solution)/shard_map/gather_others/ppermute | solution.py:34
  59.8 38.3 %all-to-all-start.1 = ((bf16[8,32,1152]{2,1,0:T(8,128)(2,1)}), bf16[8,32,1152]{2,1,0:T(8,128)(2,1)S(1)}, u32[]{:S(2)}, u32[]{:S(2)}) async-start(bf16[8,32,1152]{2,1,0:T(8,128)(2,1)} %broadcast_in_dim.39), calls=%async_computation.1 | async-start | bytes 1179648 | tf_op jit(solution)/shard_map/gather_own/all_to_all | solution.py:25
  68.0 30.1 %collective-permute-start.7 = (bf16[96,1152]{1,0:T(8,128)(2,1)S(1)}, bf16[96,1152]{1,0:T(8,128)(2,1)S(1)}, u32[]{:S(2)}, u32[]{:S(2)}) collective-permute-start(bf16[96,1152]{1,0:T(8,128)(2,1)S(1)} %pad_maximum_fusion.1.refs_0_), channel_id=1, source_target_pairs={{0,384},{128,512},{256,640},{384,768},{512,896},{640,4},{768,132},... | collective-permute-start | bytes 663560 | tf_op jit(solution)/shard_map/gather_others/ppermute | solution.py:41
  74.3 36.3 %collective-permute-start.5 = (bf16[96,1152]{1,0:T(8,128)(2,1)S(1)}, bf16[96,1152]{1,0:T(8,128)(2,1)S(1)}, u32[]{:S(2)}, u32[]{:S(2)}) collective-permute-start(bf16[96,1152]{1,0:T(8,128)(2,1)S(1)} %pad_maximum_fusion.1.refs_0_), channel_id=1, source_target_pairs={{0,3},{1,0},{2,1},{3,2},{4,7},{5,4},{6,5},{7,6},{8,11},{9,8},{10,9... | collective-permute-start | bytes 663560 | tf_op jit(solution)/shard_map/gather_others/ppermute | solution.py:34
  76.3 25.1 %collective-permute-start.8 = (bf16[64,1152]{1,0:T(8,128)(2,1)S(1)}, bf16[64,1152]{1,0:T(8,128)(2,1)S(1)}, u32[]{:S(2)}, u32[]{:S(2)}) collective-permute-start(bf16[64,1152]{1,0:T(8,128)(2,1)S(1)} %pad_maximum_fusion.2), channel_id=1, source_target_pairs={{0,644},{128,772},{256,900},{384,0},{512,128},{640,256},{768,384},... | collective-permute-start | bytes 442376 | tf_op jit(solution)/shard_map/gather_others/ppermute | solution.py:41
  98.1 31.6 %collective-permute-start.4 = (bf16[256,1152]{1,0:T(8,128)(2,1)S(1)}, bf16[256,1152]{1,0:T(8,128)(2,1)S(1)}, u32[]{:S(2)}, u32[]{:S(2)}) collective-permute-start(bf16[256,1152]{1,0:T(8,128)(2,1)S(1)} %bitcast.26), channel_id=1, source_target_pairs={{0,8},{8,0},{1,9},{9,1},{2,10},{10,2},{3,11},{11,3},{4,12},{12,4},... | collective-permute-start | bytes 1769480 | tf_op jit(solution)/shard_map/gather_own/ppermute | solution.py:34
  101.4 28.3 %collective-permute-start.10 = (bf16[160,1152]{1,0:T(8,128)(2,1)S(1)}, bf16[160,1152]{1,0:T(8,128)(2,1)S(1)}, u32[]{:S(2)}, u32[]{:S(2)}) collective-permute-start(bf16[160,1152]{1,0:T(8,128)(2,1)S(1)} %constant_dynamic-update-slice_fusion.refs_4_), channel_id=1, source_target_pairs={{0,3},{1,0},{2,1},{3,2},{4,7},{5,4},{6,5},{7,6},{8,11},{9,8},{10,9... | collective-permute-start | bytes 1105928 | tf_op jit(solution)/shard_map/gather_others/ppermute | solution.py:34
  103.3 26.4 %collective-permute-start.11 = (bf16[160,1152]{1,0:T(8,128)(2,1)S(1)}, bf16[160,1152]{1,0:T(8,128)(2,1)S(1)}, u32[]{:S(2)}, u32[]{:S(2)}) collective-permute-start(bf16[160,1152]{1,0:T(8,128)(2,1)S(1)} %constant_dynamic-update-slice_fusion.refs_4_), channel_id=1, source_target_pairs={{0,2},{1,3},{2,0},{3,1},{4,6},{5,7},{6,4},{7,5},{8,10},{9,11},{10,... | collective-permute-start | bytes 1105928 | tf_op jit(solution)/shard_map/gather_others/ppermute | solution.py:34
  106.1 23.6 %collective-permute-start.9 = (bf16[160,1152]{1,0:T(8,128)(2,1)S(1)}, bf16[160,1152]{1,0:T(8,128)(2,1)S(1)}, u32[]{:S(2)}, u32[]{:S(2)}) collective-permute-start(bf16[160,1152]{1,0:T(8,128)(2,1)S(1)} %constant_dynamic-update-slice_fusion.refs_4_), channel_id=1, source_target_pairs={{0,1},{1,2},{2,3},{3,0},{4,5},{5,6},{6,7},{7,4},{8,9},{9,10},{10,1... | collective-permute-start | bytes 1105928 | tf_op jit(solution)/shard_map/gather_others/ppermute | solution.py:34
  110.7 19.0 %collective-permute-start.6 = (bf16[96,1152]{1,0:T(8,128)(2,1)S(1)}, bf16[96,1152]{1,0:T(8,128)(2,1)}, u32[]{:S(2)}, u32[]{:S(2)}) collective-permute-start(bf16[96,1152]{1,0:T(8,128)(2,1)S(1)} %pad_maximum_fusion.1.refs_0_), channel_id=1, source_target_pairs={{0,2},{1,3},{2,0},{3,1},{4,6},{5,7},{6,4},{7,5},{8,10},{9,11},{10,... | collective-permute-start | bytes 663560 | tf_op jit(solution)/shard_map/gather_others/ppermute | solution.py:34
  132.5 5.2 %collective-permute-start.12 = (f32[256,1152]{1,0:T(8,128)S(1)}, f32[256,1152]{1,0:T(8,128)S(1)}, u32[]{:S(2)}, u32[]{:S(2)}) collective-permute-start(f32[256,1152]{1,0:T(8,128)S(1)} %get-tuple-element.11), channel_id=1, source_target_pairs={{0,8},{8,0},{1,9},{9,1},{2,10},{10,2},{3,11},{11,3},{4,12},{12,4},... | collective-permute-start | bytes 3538952 | tf_op jit(solution)/shard_map/reduce_pairs/ppermute | solution.py:34
  137.8 24.7 %copy-start.1 = (f32[32,1152]{1,0:T(8,128)S(1)}, f32[32,1152]{1,0:T(8,128)}, u32[]{:S(2)}) copy-start(f32[32,1152]{1,0:T(8,128)} %copy-done) | copy-start | bytes 442372
  162.5 4.8 %copy-start.4 = (bf16[64,144]{1,0:T(8,128)(2,1)S(1)}, bf16[64,144]{1,0:T(8,128)(2,1)}, u32[]{:S(2)}) copy-start(bf16[64,144]{1,0:T(8,128)(2,1)} %param.7) | copy-start | bytes 55300
  162.5 4.8 %copy-start.5 = (bf16[64,144]{1,0:T(8,128)(2,1)S(1)}, bf16[64,144]{1,0:T(8,128)(2,1)}, u32[]{:S(2)}) copy-start(bf16[64,144]{1,0:T(8,128)(2,1)} %param.6) | copy-start | bytes 55300
  163.6 9.1 %all-to-all-start.3 = ((bf16[4,32,1152]{2,1,0:T(8,128)(2,1)}), bf16[4,32,1152]{2,1,0:T(8,128)(2,1)S(1)}, u32[]{:S(2)}, u32[]{:S(2)}) async-start(bf16[4,32,1152]{2,1,0:T(8,128)(2,1)} %broadcast_in_dim.40), calls=%async_computation.3 | async-start | bytes 589824 | tf_op jit(solution)/shard_map/back/all_to_all | solution.py:25
  174.4 6.3 %collective-permute-start.13 = (f32[576,288]{0,1:T(8,128)S(1)}, f32[576,288]{0,1:T(8,128)S(1)}, u32[]{:S(2)}, u32[]{:S(2)}) collective-permute-start(f32[576,288]{0,1:T(8,128)S(1)} %slice.25), channel_id=1, source_target_pairs={{0,8},{8,0},{1,9},{9,1},{2,10},{10,2},{3,11},{11,3},{4,12},{12,4},... | collective-permute-start | bytes 1990664 | tf_op jit(solution)/shard_map/weight_grad/ppermute | solution.py:34
  181.0 6.6 %copy-start.2 = (bf16[144,1152]{1,0:T(8,128)(2,1)S(1)}, bf16[144,1152]{1,0:T(8,128)(2,1)}, u32[]{:S(2)}) copy-start(bf16[144,1152]{1,0:T(8,128)(2,1)} %param.9) | copy-start | bytes 995332
  181.0 6.6 %copy-start.3 = (bf16[144,1152]{1,0:T(8,128)(2,1)S(1)}, bf16[144,1152]{1,0:T(8,128)(2,1)}, u32[]{:S(2)}) copy-start(bf16[144,1152]{1,0:T(8,128)(2,1)} %param.8) | copy-start | bytes 995332
  182.8 28.7 %all-to-all-start.4 = ((bf16[64,2,1296]{2,1,0:T(2,128)(2,1)}), bf16[64,2,1296]{2,1,0:T(2,128)(2,1)S(1)}, u32[]{:S(2)}, u32[]{:S(2)}) async-start(bf16[64,2,1296]{2,1,0:T(2,128)(2,1)} %reshape.161), calls=%async_computation.4 | async-start | bytes 720896 | tf_op jit(solution)/shard_map/weight_grad/all_to_all | solution.py:25

commit v6 on v4

--- a/solution.py
+++ b/solution.py
@@ -10,8 +10,7 @@
 TENSOR = ("zh", "x")
 SIZES = {"zl": 8, "y": 8, "c": 2, "zh": 2, "x": 4}
 STEPS = (0, 1, 3, 2)
-FIRST = (0, -1, 1)
-GROUPS = FIRST + (-3, -4, -2, 3, 2)
+GROUPS = (0, -4, -1, -5, 1, -3, -2, -6)
 RUN = 16
 F32 = jnp.float32
 BF16 = jnp.bfloat16
@@ -116,10 +115,8 @@
         theirs = shifted(mine, "c", 1)
 
     with jax.named_scope("gather_others"):
-        behind, ahead = along_z(vec, 1), along_z(vec, -1)
-        near = jnp.concatenate([vec, behind, ahead])
-        far = [along_z(near, 3), along_z(jnp.concatenate([vec, behind]), -3)]
-        column = jnp.concatenate([near] + far)
+        pair = jnp.concatenate([vec, along_z(vec, 4)])
+        column = jnp.concatenate([pair] + [along_z(pair, by) for by in (1, -1, 2)])
         others = [column] + [shifted(column, "x", by) for by in STEPS[1:]]
 
     with jax.named_scope("pairs"):

time: 203 us -> 197 us (0.970)
  starting transfers between devices: 103 us -> 94.3 us
    ppermute x4, starting transfers between devices: 28.7 us -> 23.8 us  [along_z(): return lax.ppermute(value, ('zl', 'zh'), pairs)]
    all_to_all x4, starting transfers between devices: 26.2 us -> 23 us  [exchange(): return lax.all_to_all(blocks, axes, 0, 0, tiled=True)]
  transfers between devices with their start and end apart: 15 -> 15, of which waited for: 8 -> 9; matrix products, arithmetic and copies ran while one was open for 1% -> 1% of each run, Pallas kernels for 0% -> 0%
where the time goes in v6:
time: 197 us; the launch traced here: 196 us
  starting transfers between devices  94.3 us (48%)
  waiting for transfers between devices  57.8 us (29%)
  blocking collectives  26.2 us (13%)
  local copies, waits for them, and re-layouts  6.61 us (3%)
  matrix products  4.14 us (2%)
  Pallas kernels  2.88 us (1%)
  between operations  2.38 us (1%)
  other arithmetic  2.12 us (1%)
    ppermute x7, starting transfers between devices, shifted(): lax.ppermute(value, axis, [(i, (i + by) % size) for i in range(size)])  47.5 us
    all_to_all x4, waiting for transfers between devices, exchange(): return lax.all_to_all(blocks, axes, 0, 0, tiled=True)  33.7 us
    all_to_all x1, blocking collectives, exchange(): return lax.all_to_all(blocks, axes, 0, 0, tiled=True)  26.2 us
    ppermute x4, starting transfers between devices, along_z(): return lax.ppermute(value, ('zl', 'zh'), pairs)  23.8 us
    all_to_all x4, starting transfers between devices, exchange(): return lax.all_to_all(blocks, axes, 0, 0, tiled=True)  23 us
    ppermute x7, waiting for transfers between devices, shifted(): lax.ppermute(value, axis, [(i, (i + by) % size) for i in range(size)])  16.4 us
    ppermute x4, waiting for transfers between devices, along_z(): return lax.ppermute(value, ('zl', 'zh'), pairs)  7.72 us
    dot_general x4, matrix products, dot(): return lax.dot_general(a, b, (dims, ((), ())), preferred_element_type=F32)  4.14 us
  transfers between devices with their start and end apart: 15, of which 9 were waited for; matrix products, arithmetic and copies ran while one was open for 1% of the time, Pallas kernels for 0%

profile of v6, /device:TPU:1, one launch (start us, length us, event | category | flops | bytes accessed | tf_op | source)
XLA Modules:
  0.0 196.4 jit_solution(14106215105044790338)
XLA Ops:
  0.6 1.2 convolution_convert_fusion.1
  1.8 1.2 convolution_convert_fusion
  3.8 4.8 %all-to-all-start = ((bf16[4,32,1152]{2,1,0:T(8,128)(2,1)}), bf16[4,32,1152]{2,1,0:T(8,128)(2,1)S(1)}, u32[]{:S(2)}, u32[]{:S(2)}) async-start(bf16[4,32,1152]{2,1,0:T(8,128)(2,1)} %pad_maximum_fusion), calls=%async_computation | async-start | bytes 589824 | tf_op jit(solution)/shard_map/embed/all_to_all | solution.py:24
  8.7 5.6 %all-to-all-done = bf16[4,32,1152]{2,1,0:T(8,128)(2,1)S(1)} async-done(((bf16[4,32,1152]{2,1,0:T(8,128)(2,1)}), bf16[4,32,1152]{2,1,0:T(8,128)(2,1)S(1)}, u32[]{:S(2)}, u32[]{:S(2)}) %all-to-all-start) | async-done | bytes 294944 | tf_op jit(solution)/shard_map/embed/all_to_all | solution.py:24
  14.3 19.2 %collective-permute-start = (f32[32,1152]{1,0:T(8,128)S(1)}, f32[32,1152]{1,0:T(8,128)S(1)}, u32[]{:S(2)}, u32[]{:S(2)}) collective-permute-start(f32[32,1152]{1,0:T(8,128)S(1)} %convert_reduce_fusion.2), channel_id=1, source_target_pairs={{0,4},{4,0},{1,5},{5,1},{2,6},{6,2},{3,7},{7,3},{8,12},{12,8},{9,1... | collective-permute-start | bytes 442376 | tf_op jit(solution)/shard_map/embed/ppermute | solution.py:33
  33.6 2.8 %collective-permute-done = f32[32,1152]{1,0:T(8,128)S(1)} collective-permute-done((f32[32,1152]{1,0:T(8,128)S(1)}, f32[32,1152]{1,0:T(8,128)S(1)}, u32[]{:S(2)}, u32[]{:S(2)}) %collective-permute-start) | collective-permute-done | bytes 147488 | tf_op jit(solution)/shard_map/embed/ppermute | solution.py:33
  36.6 10.8 %collective-permute-start.2 = (bf16[32,1152]{1,0:T(8,128)(2,1)S(1)}, bf16[32,1152]{1,0:T(8,128)(2,1)S(1)}, u32[]{:S(2)}, u32[]{:S(2)}) collective-permute-start(bf16[32,1152]{1,0:T(8,128)(2,1)S(1)} %get-tuple-element.9), channel_id=1, source_target_pairs={{0,512},{128,640},{256,768},{384,896},{512,4},{640,132},{768,260},... | collective-permute-start | bytes 221192 | tf_op jit(solution)/shard_map/gather_others/ppermute | solution.py:40
  47.4 0.9 broadcast_in_dim.39
  48.3 8.4 %all-to-all-start.1 = ((bf16[8,32,1152]{2,1,0:T(8,128)(2,1)}), bf16[8,32,1152]{2,1,0:T(8,128)(2,1)S(1)}, u32[]{:S(2)}, u32[]{:S(2)}) async-start(bf16[8,32,1152]{2,1,0:T(8,128)(2,1)} %broadcast_in_dim.39), calls=%async_computation.1 | async-start | bytes 1179648 | tf_op jit(solution)/shard_map/gather_own/all_to_all | solution.py:24
  56.7 1.5 collective-permute-done.2
  58.2 1.9 collective-permute-start.3
  60.1 4.6 %collective-permute-start.4 = (bf16[64,1152]{1,0:T(8,128)(2,1)S(1)}, bf16[64,1152]{1,0:T(8,128)(2,1)S(1)}, u32[]{:S(2)}, u32[]{:S(2)}) collective-permute-start(bf16[64,1152]{1,0:T(8,128)(2,1)S(1)} %pad_maximum_fusion.1), channel_id=1, source_target_pairs={{0,900},{128,0},{256,128},{384,256},{512,384},{640,512},{768,640},... | collective-permute-start | bytes 442376 | tf_op jit(solution)/shard_map/gather_others/ppermute | solution.py:40
  64.7 6.5 %collective-permute-start.5 = (bf16[64,1152]{1,0:T(8,128)(2,1)S(1)}, bf16[64,1152]{1,0:T(8,128)(2,1)S(1)}, u32[]{:S(2)}, u32[]{:S(2)}) collective-permute-start(bf16[64,1152]{1,0:T(8,128)(2,1)S(1)} %pad_maximum_fusion.1), channel_id=1, source_target_pairs={{0,256},{128,384},{256,512},{384,640},{512,768},{640,896},{768,4},... | collective-permute-start | bytes 442376 | tf_op jit(solution)/shard_map/gather_others/ppermute | solution.py:40
  71.3 6.2 %collective-permute-done.5 = bf16[64,1152]{1,0:T(8,128)(2,1)S(1)} collective-permute-done((bf16[64,1152]{1,0:T(8,128)(2,1)S(1)}, bf16[64,1152]{1,0:T(8,128)(2,1)S(1)}, u32[]{:S(2)}, u32[]{:S(2)}) %collective-permute-start.5) | collective-permute-done | bytes 147488 | tf_op jit(solution)/shard_map/gather_others/ppermute | solution.py:40
  77.5 2.2 %collective-permute-start.6 = (bf16[256,1152]{1,0:T(8,128)(2,1)S(1)}, bf16[256,1152]{1,0:T(8,128)(2,1)S(1)}, u32[]{:S(2)}, u32[]{:S(2)}) collective-permute-start(bf16[256,1152]{1,0:T(8,128)(2,1)S(1)} %constant_dynamic-update-slice_fusion.refs_0_), channel_id=1, source_target_pairs={{0,1},{1,2},{2,3},{3,0},{4,5},{5,6},{6,7},{7,4},{8,9},{9,10},{10,1... | collective-permute-start | bytes 1769480 | tf_op jit(solution)/shard_map/gather_others/ppermute | solution.py:33
  79.7 4.3 %collective-permute-start.7 = (bf16[256,1152]{1,0:T(8,128)(2,1)S(1)}, bf16[256,1152]{1,0:T(8,128)(2,1)S(1)}, u32[]{:S(2)}, u32[]{:S(2)}) collective-permute-start(bf16[256,1152]{1,0:T(8,128)(2,1)S(1)} %constant_dynamic-update-slice_fusion.refs_0_), channel_id=1, source_target_pairs={{0,3},{1,0},{2,1},{3,2},{4,7},{5,4},{6,5},{7,6},{8,11},{9,8},{10,9... | collective-permute-start | bytes 1769480 | tf_op jit(solution)/shard_map/gather_others/ppermute | solution.py:33
  84.0 2.0 %collective-permute-start.8 = (bf16[256,1152]{1,0:T(8,128)(2,1)S(1)}, bf16[256,1152]{1,0:T(8,128)(2,1)S(1)}, u32[]{:S(2)}, u32[]{:S(2)}) collective-permute-start(bf16[256,1152]{1,0:T(8,128)(2,1)S(1)} %constant_dynamic-update-slice_fusion.refs_0_), channel_id=1, source_target_pairs={{0,2},{1,3},{2,0},{3,1},{4,6},{5,7},{6,4},{7,5},{8,10},{9,11},{10,... | collective-permute-start | bytes 1769480 | tf_op jit(solution)/shard_map/gather_others/ppermute | solution.py:33
  86.0 7.1 %collective-permute-start.1 = (bf16[256,1152]{1,0:T(8,128)(2,1)S(1)}, bf16[256,1152]{1,0:T(8,128)(2,1)}, u32[]{:S(2)}, u32[]{:S(2)}) collective-permute-start(bf16[256,1152]{1,0:T(8,128)(2,1)S(1)} %bitcast.26), channel_id=1, source_target_pairs={{0,8},{8,0},{1,9},{9,1},{2,10},{10,2},{3,11},{11,3},{4,12},{12,4},... | collective-permute-start | bytes 1769480 | tf_op jit(solution)/shard_map/gather_own/ppermute | solution.py:33
  94.9 9.3 %collective-permute-done.8.refs_3_ = bf16[256,1152]{1,0:T(8,128)(2,1)S(1)} collective-permute-done((bf16[256,1152]{1,0:T(8,128)(2,1)S(1)}, bf16[256,1152]{1,0:T(8,128)(2,1)S(1)}, u32[]{:S(2)}, u32[]{:S(2)}) %collective-permute-start.8) | collective-permute-done | bytes 589856 | tf_op jit(solution)/shard_map/gather_others/ppermute | solution.py:33
  104.2 2.9 %pairs.1 = (f32[256,1152]{1,0:T(8,128)S(1)}, f32[256,1152]{1,0:T(8,128)S(1)}) custom-call(f32[2]{0:T(128)S(1)} %pad_maximum_fusion.2.factors, s32[256,1]{1,0:T(8,128)S(1)} %reshape.160.own_ids, s32[1,512]{1,0:T(1,128)S(1)} %bitcast.28, bf16[256,1152]{1,0:T(8,128)(2,1)S(1)} %bitcast.27, bf16[256,1152]{1,0:T(8,128)(2,1)} %collective-permute-done.1.theirs, ...), custom_call_target="tpu_custom_call" | custom-call | flops 1207959552 | bytes 5898240 | tf_op jit(solution)/shard_map/pairs/pallas_call | solution.py:75
  107.1 7.9 %collective-permute-start.9 = (f32[256,1152]{1,0:T(8,128)S(1)}, f32[256,1152]{1,0:T(8,128)S(1)}, u32[]{:S(2)}, u32[]{:S(2)}) collective-permute-start(f32[256,1152]{1,0:T(8,128)S(1)} %get-tuple-element.7), channel_id=1, source_target_pairs={{0,8},{8,0},{1,9},{9,1},{2,10},{10,2},{3,11},{11,3},{4,12},{12,4},... | collective-permute-start | bytes 3538952 | tf_op jit(solution)/shard_map/reduce_pairs/ppermute | solution.py:33
  115.0 2.5 %collective-permute-done.9 = f32[256,1152]{1,0:T(8,128)S(1)} collective-permute-done((f32[256,1152]{1,0:T(8,128)S(1)}, f32[256,1152]{1,0:T(8,128)S(1)}, u32[]{:S(2)}, u32[]{:S(2)}) %collective-permute-start.9) | collective-permute-done | bytes 1179680 | tf_op jit(solution)/shard_map/reduce_pairs/ppermute | solution.py:33
  117.7 26.2 %all_to_all.25 = bf16[8,32,1152]{2,1,0:T(8,128)(2,1)S(1)} all-to-all(bf16[8,32,1152]{2,1,0:T(8,128)(2,1)S(1)} %bitcast.29), channel_id=1, replica_groups=mesh['zl'=8,'y'=8,'c'=2,'zh'=2,'x'=4] {'y'}, dimensions={0} | all-to-all | bytes 1179648 | tf_op jit(solution)/shard_map/reduce_pairs/all_to_all | solution.py:24
  145.0 4.6 %all-to-all-start.3 = ((bf16[4,32,1152]{2,1,0:T(8,128)(2,1)}), bf16[4,32,1152]{2,1,0:T(8,128)(2,1)S(1)}, u32[]{:S(2)}, u32[]{:S(2)}) async-start(bf16[4,32,1152]{2,1,0:T(8,128)(2,1)} %broadcast_in_dim.40), calls=%async_computation.3 | async-start | bytes 589824 | tf_op jit(solution)/shard_map/back/all_to_all | solution.py:24
  149.9 5.4 %all-to-all-done.3 = bf16[4,32,1152]{2,1,0:T(8,128)(2,1)S(1)} async-done(((bf16[4,32,1152]{2,1,0:T(8,128)(2,1)}), bf16[4,32,1152]{2,1,0:T(8,128)(2,1)S(1)}, u32[]{:S(2)}, u32[]{:S(2)}) %all-to-all-start.3) | async-done | bytes 294944 | tf_op jit(solution)/shard_map/back/all_to_all | solution.py:24
  155.3 1.4 fusion.3
  156.9 4.8 %collective-permute-start.10 = (f32[576,288]{0,1:T(8,128)S(1)}, f32[576,288]{0,1:T(8,128)S(1)}, u32[]{:S(2)}, u32[]{:S(2)}) collective-permute-start(f32[576,288]{0,1:T(8,128)S(1)} %slice.25), channel_id=1, source_target_pairs={{0,8},{8,0},{1,9},{9,1},{2,10},{10,2},{3,11},{11,3},{4,12},{12,4},... | collective-permute-start | bytes 1990664 | tf_op jit(solution)/shard_map/weight_grad/ppermute | solution.py:33
  161.7 1.8 collective-permute-done.10
  164.1 1.6 reshape.161
  165.6 5.1 %all-to-all-start.4 = ((bf16[64,2,1296]{2,1,0:T(2,128)(2,1)}), bf16[64,2,1296]{2,1,0:T(2,128)(2,1)S(1)}, u32[]{:S(2)}, u32[]{:S(2)}) async-start(bf16[64,2,1296]{2,1,0:T(2,128)(2,1)} %reshape.161), calls=%async_computation.4 | async-start | bytes 720896 | tf_op jit(solution)/shard_map/weight_grad/all_to_all | solution.py:24
  171.9 22.7 %all-to-all-done.4 = bf16[64,2,1296]{2,1,0:T(2,128)(2,1)S(1)} async-done(((bf16[64,2,1296]{2,1,0:T(2,128)(2,1)}), bf16[64,2,1296]{2,1,0:T(2,128)(2,1)S(1)}, u32[]{:S(2)}, u32[]{:S(2)}) %all-to-all-start.4) | async-done | bytes 331808 | tf_op jit(solution)/shard_map/weight_grad/all_to_all | solution.py:24
  194.6 0.9 reshape.162
  (60 shorter events, 5.8 us)
Async XLA Ops:
  3.8 10.5 %all-to-all-start = ((bf16[4,32,1152]{2,1,0:T(8,128)(2,1)}), bf16[4,32,1152]{2,1,0:T(8,128)(2,1)S(1)}, u32[]{:S(2)}, u32[]{:S(2)}) async-start(bf16[4,32,1152]{2,1,0:T(8,128)(2,1)} %pad_maximum_fusion), calls=%async_computation | async-start | bytes 589824 | tf_op jit(solution)/shard_map/embed/all_to_all | solution.py:24
  14.3 22.0 %collective-permute-start = (f32[32,1152]{1,0:T(8,128)S(1)}, f32[32,1152]{1,0:T(8,128)S(1)}, u32[]{:S(2)}, u32[]{:S(2)}) collective-permute-start(f32[32,1152]{1,0:T(8,128)S(1)} %convert_reduce_fusion.2), channel_id=1, source_target_pairs={{0,4},{4,0},{1,5},{5,1},{2,6},{6,2},{3,7},{7,3},{8,12},{12,8},{9,1... | collective-permute-start | bytes 442376 | tf_op jit(solution)/shard_map/embed/ppermute | solution.py:33
  36.6 21.6 %collective-permute-start.2 = (bf16[32,1152]{1,0:T(8,128)(2,1)S(1)}, bf16[32,1152]{1,0:T(8,128)(2,1)S(1)}, u32[]{:S(2)}, u32[]{:S(2)}) collective-permute-start(bf16[32,1152]{1,0:T(8,128)(2,1)S(1)} %get-tuple-element.9), channel_id=1, source_target_pairs={{0,512},{128,640},{256,768},{384,896},{512,4},{640,132},{768,260},... | collective-permute-start | bytes 221192 | tf_op jit(solution)/shard_map/gather_others/ppermute | solution.py:40
  48.3 37.8 %all-to-all-start.1 = ((bf16[8,32,1152]{2,1,0:T(8,128)(2,1)}), bf16[8,32,1152]{2,1,0:T(8,128)(2,1)S(1)}, u32[]{:S(2)}, u32[]{:S(2)}) async-start(bf16[8,32,1152]{2,1,0:T(8,128)(2,1)} %broadcast_in_dim.39), calls=%async_computation.1 | async-start | bytes 1179648 | tf_op jit(solution)/shard_map/gather_own/all_to_all | solution.py:24
  58.2 13.0 %collective-permute-start.3 = (bf16[64,1152]{1,0:T(8,128)(2,1)S(1)}, bf16[64,1152]{1,0:T(8,128)(2,1)S(1)}, u32[]{:S(2)}, u32[]{:S(2)}) collective-permute-start(bf16[64,1152]{1,0:T(8,128)(2,1)S(1)} %pad_maximum_fusion.1), channel_id=1, source_target_pairs={{0,128},{128,256},{256,384},{384,512},{512,640},{640,768},{768,896... | collective-permute-start | bytes 442376 | tf_op jit(solution)/shard_map/gather_others/ppermute | solution.py:40
  60.1 11.1 %collective-permute-start.4 = (bf16[64,1152]{1,0:T(8,128)(2,1)S(1)}, bf16[64,1152]{1,0:T(8,128)(2,1)S(1)}, u32[]{:S(2)}, u32[]{:S(2)}) collective-permute-start(bf16[64,1152]{1,0:T(8,128)(2,1)S(1)} %pad_maximum_fusion.1), channel_id=1, source_target_pairs={{0,900},{128,0},{256,128},{384,256},{512,384},{640,512},{768,640},... | collective-permute-start | bytes 442376 | tf_op jit(solution)/shard_map/gather_others/ppermute | solution.py:40
  64.7 12.8 %collective-permute-start.5 = (bf16[64,1152]{1,0:T(8,128)(2,1)S(1)}, bf16[64,1152]{1,0:T(8,128)(2,1)S(1)}, u32[]{:S(2)}, u32[]{:S(2)}) collective-permute-start(bf16[64,1152]{1,0:T(8,128)(2,1)S(1)} %pad_maximum_fusion.1), channel_id=1, source_target_pairs={{0,256},{128,384},{256,512},{384,640},{512,768},{640,896},{768,4},... | collective-permute-start | bytes 442376 | tf_op jit(solution)/shard_map/gather_others/ppermute | solution.py:40
  77.5 17.4 %collective-permute-start.6 = (bf16[256,1152]{1,0:T(8,128)(2,1)S(1)}, bf16[256,1152]{1,0:T(8,128)(2,1)S(1)}, u32[]{:S(2)}, u32[]{:S(2)}) collective-permute-start(bf16[256,1152]{1,0:T(8,128)(2,1)S(1)} %constant_dynamic-update-slice_fusion.refs_0_), channel_id=1, source_target_pairs={{0,1},{1,2},{2,3},{3,0},{4,5},{5,6},{6,7},{7,4},{8,9},{9,10},{10,1... | collective-permute-start | bytes 1769480 | tf_op jit(solution)/shard_map/gather_others/ppermute | solution.py:33
  79.7 15.2 %collective-permute-start.7 = (bf16[256,1152]{1,0:T(8,128)(2,1)S(1)}, bf16[256,1152]{1,0:T(8,128)(2,1)S(1)}, u32[]{:S(2)}, u32[]{:S(2)}) collective-permute-start(bf16[256,1152]{1,0:T(8,128)(2,1)S(1)} %constant_dynamic-update-slice_fusion.refs_0_), channel_id=1, source_target_pairs={{0,3},{1,0},{2,1},{3,2},{4,7},{5,4},{6,5},{7,6},{8,11},{9,8},{10,9... | collective-permute-start | bytes 1769480 | tf_op jit(solution)/shard_map/gather_others/ppermute | solution.py:33
  84.0 20.2 %collective-permute-start.8 = (bf16[256,1152]{1,0:T(8,128)(2,1)S(1)}, bf16[256,1152]{1,0:T(8,128)(2,1)S(1)}, u32[]{:S(2)}, u32[]{:S(2)}) collective-permute-start(bf16[256,1152]{1,0:T(8,128)(2,1)S(1)} %constant_dynamic-update-slice_fusion.refs_0_), channel_id=1, source_target_pairs={{0,2},{1,3},{2,0},{3,1},{4,6},{5,7},{6,4},{7,5},{8,10},{9,11},{10,... | collective-permute-start | bytes 1769480 | tf_op jit(solution)/shard_map/gather_others/ppermute | solution.py:33
  86.0 18.1 %collective-permute-start.1 = (bf16[256,1152]{1,0:T(8,128)(2,1)S(1)}, bf16[256,1152]{1,0:T(8,128)(2,1)}, u32[]{:S(2)}, u32[]{:S(2)}) collective-permute-start(bf16[256,1152]{1,0:T(8,128)(2,1)S(1)} %bitcast.26), channel_id=1, source_target_pairs={{0,8},{8,0},{1,9},{9,1},{2,10},{10,2},{3,11},{11,3},{4,12},{12,4},... | collective-permute-start | bytes 1769480 | tf_op jit(solution)/shard_map/gather_own/ppermute | solution.py:33
  107.1 10.4 %collective-permute-start.9 = (f32[256,1152]{1,0:T(8,128)S(1)}, f32[256,1152]{1,0:T(8,128)S(1)}, u32[]{:S(2)}, u32[]{:S(2)}) collective-permute-start(f32[256,1152]{1,0:T(8,128)S(1)} %get-tuple-element.7), channel_id=1, source_target_pairs={{0,8},{8,0},{1,9},{9,1},{2,10},{10,2},{3,11},{11,3},{4,12},{12,4},... | collective-permute-start | bytes 3538952 | tf_op jit(solution)/shard_map/reduce_pairs/ppermute | solution.py:33
  143.8 6.0 %copy-start.2 = (bf16[64,144]{1,0:T(8,128)(2,1)S(1)}, bf16[64,144]{1,0:T(8,128)(2,1)}, u32[]{:S(2)}) copy-start(bf16[64,144]{1,0:T(8,128)(2,1)} %param.7) | copy-start | bytes 55300
  143.8 6.0 %copy-start.3 = (bf16[64,144]{1,0:T(8,128)(2,1)S(1)}, bf16[64,144]{1,0:T(8,128)(2,1)}, u32[]{:S(2)}) copy-start(bf16[64,144]{1,0:T(8,128)(2,1)} %param.6) | copy-start | bytes 55300
  145.0 10.3 %all-to-all-start.3 = ((bf16[4,32,1152]{2,1,0:T(8,128)(2,1)}), bf16[4,32,1152]{2,1,0:T(8,128)(2,1)S(1)}, u32[]{:S(2)}, u32[]{:S(2)}) async-start(bf16[4,32,1152]{2,1,0:T(8,128)(2,1)} %broadcast_in_dim.40), calls=%async_computation.3 | async-start | bytes 589824 | tf_op jit(solution)/shard_map/back/all_to_all | solution.py:24
  156.9 6.6 %collective-permute-start.10 = (f32[576,288]{0,1:T(8,128)S(1)}, f32[576,288]{0,1:T(8,128)S(1)}, u32[]{:S(2)}, u32[]{:S(2)}) collective-permute-start(f32[576,288]{0,1:T(8,128)S(1)} %slice.25), channel_id=1, source_target_pairs={{0,8},{8,0},{1,9},{9,1},{2,10},{10,2},{3,11},{11,3},{4,12},{12,4},... | collective-permute-start | bytes 1990664 | tf_op jit(solution)/shard_map/weight_grad/ppermute | solution.py:33
  163.9 6.9 %copy-start = (bf16[144,1152]{1,0:T(8,128)(2,1)S(1)}, bf16[144,1152]{1,0:T(8,128)(2,1)}, u32[]{:S(2)}) copy-start(bf16[144,1152]{1,0:T(8,128)(2,1)} %param.9) | copy-start | bytes 995332
  163.9 6.9 %copy-start.1 = (bf16[144,1152]{1,0:T(8,128)(2,1)S(1)}, bf16[144,1152]{1,0:T(8,128)(2,1)}, u32[]{:S(2)}) copy-start(bf16[144,1152]{1,0:T(8,128)(2,1)} %param.8) | copy-start | bytes 995332
  165.6 29.0 %all-to-all-start.4 = ((bf16[64,2,1296]{2,1,0:T(2,128)(2,1)}), bf16[64,2,1296]{2,1,0:T(2,128)(2,1)S(1)}, u32[]{:S(2)}, u32[]{:S(2)}) async-start(bf16[64,2,1296]{2,1,0:T(2,128)(2,1)} %reshape.161), calls=%async_computation.4 | async-start | bytes 720896 | tf_op jit(solution)/shard_map/weight_grad/all_to_all | solution.py:24

commit v7 on v6

--- a/solution.py
+++ b/solution.py
@@ -40,11 +40,20 @@
     return lax.ppermute(value, ("zl", "zh"), pairs)
 
 
+def along_y(value, by):
+    return shifted(value, "y", by)
+
+
+def ring_gather(block, step):
+    pair = jnp.concatenate([block, step(block, 4)])
+    return jnp.concatenate([pair] + [step(pair, by) for by in (1, -1, 2)])
+
+
 def flat(*sizes):
     return [lax.broadcasted_iota(jnp.int32, sizes, i).reshape(-1) for i in range(len(sizes))]
 
 
-def pair_kernel(factors, own_ids, other_ids, mine, theirs, *refs):
+def pair_kernel(factors, places, own_ids, other_ids, mine, theirs, *refs):
     blocks, (mine_sum, theirs_sum, held, partners) = refs[: len(STEPS)], refs[len(STEPS) :]
     run = RUN
     for kind in range(2):
@@ -62,12 +71,12 @@
         coef = jax.nn.sigmoid(logits) - jnp.where(matched, 1.0, 0.0)
         total = dot(coef.astype(BF16), other, ((1,), (0,)))
         for part, out in ((total[:count], mine_sum), (total[count:], theirs_sum)):
-            for at in range(0, count, run):
-                start = 2 * at + kind * run
-                out[start : start + run, :] = part[at : at + run]
-
-
-def pair_sums(factors, own_ids, other_ids, mine, theirs, others):
+            for group in range(len(GROUPS)):
+                start = pl.multiple_of((2 * places[group] + kind) * run, run)
+                out[pl.ds(start, run), :] = part[group * run : (group + 1) * run]
+
+
+def pair_sums(factors, places, own_ids, other_ids, mine, theirs, others):
     count, width = mine.shape
     partners = len(others) * others[0].shape[0]
     whole = pl.BlockSpec(memory_space=pltpu.VMEM)
@@ -75,7 +84,7 @@
     return pl.pallas_call(
         pair_kernel,
         out_shape=(out, out),
-        in_specs=[pl.BlockSpec(memory_space=pltpu.SMEM)] + [whole] * (4 + len(others)),
+        in_specs=[pl.BlockSpec(memory_space=pltpu.SMEM)] * 2 + [whole] * (4 + len(others)),
         out_specs=(whole, whole),
         scratch_shapes=[
             pltpu.VMEM((2, count, width), BF16),
@@ -87,7 +96,7 @@
             bytes_accessed=12 * count * width + 2 * partners * width,
             transcendentals=count * partners,
         ),
-    )(factors, own_ids, other_ids, mine, theirs, *others)
+    )(factors, places, own_ids, other_ids, mine, theirs, *others)
 
 
 def local(image_features, text_features, image_weight, text_weight, log_scale, logit_bias):
@@ -111,19 +120,21 @@
         vec = unit.astype(BF16)
 
     with jax.named_scope("gather_own"):
-        mine = spread(vec, "y", SIZES["y"]).reshape(-1, width)
+        mine = ring_gather(vec, along_y)
         theirs = shifted(mine, "c", 1)
 
     with jax.named_scope("gather_others"):
-        pair = jnp.concatenate([vec, along_z(vec, 4)])
-        column = jnp.concatenate([pair] + [along_z(pair, by) for by in (1, -1, 2)])
+        column = ring_gather(vec, along_z)
         others = [column] + [shifted(column, "x", by) for by in STEPS[1:]]
 
     with jax.named_scope("pairs"):
-        hc, hy, hrow = flat(2, SIZES["y"], own)
-        held_data = (zl * SIZES["y"] + hy) * 2 + jnp.where(hc == 0, c, 1 - c)
-        held_id = held_data * rows + x * own + hrow
         orow = lax.iota(jnp.int32, own)
+        places = [(y + group + SIZES["y"]) % SIZES["y"] for group in GROUPS]
+        held_id = []
+        for core in (c, 1 - c):
+            for place in places:
+                data = (zl * SIZES["y"] + place) * 2 + core
+                held_id.append(data * rows + x * own + orow)
         other_id = []
         for step in STEPS:
             for group in GROUPS:
@@ -132,7 +143,8 @@
                 other_id.append(data * rows + place * own + orow)
         mine_sum, theirs_sum = pair_sums(
             jnp.stack([scale, bias]),
-            held_id[:, None],
+            jnp.stack(places),
+            jnp.concatenate(held_id)[:, None],
             jnp.concatenate(other_id)[None, :],
             mine,
             theirs,

time: 197 us -> 203 us (1.030)
  starting transfers between devices: 94.3 us -> 104 us
  blocking collectives: 26.2 us -> 23 us
    ppermute x7 -> x11, starting transfers between devices: 47.5 us -> 62.7 us  [shifted(): lax.ppermute(value, axis, [(i, (i + by) % size) for i in range(size)])]
    all_to_all x4 -> x3, starting transfers between devices: 23 us -> 15.3 us  [exchange(): return lax.all_to_all(blocks, axes, 0, 0, tiled=True)]
    all_to_all x1, blocking collectives: 26.2 us -> 23 us  [exchange(): return lax.all_to_all(blocks, axes, 0, 0, tiled=True)]
    ppermute x4, starting transfers between devices: 23.8 us -> 26 us  [along_z(): return lax.ppermute(value, ('zl', 'zh'), pairs)]
    ppermute x7 -> x11, waiting for transfers between devices: 16.4 us -> 16.7 us  [shifted(): lax.ppermute(value, axis, [(i, (i + by) % size) for i in range(size)])]
    all_to_all x4 -> x3, waiting for transfers between devices: 33.7 us -> 33.6 us  [exchange(): return lax.all_to_all(blocks, axes, 0, 0, tiled=True)]
  transfers between devices with their start and end apart: 15 -> 18, of which waited for: 9 -> 8; matrix products, arithmetic and copies ran while one was open for 1% -> 1% of each run, Pallas kernels for 0% -> 0%
where the time goes in v7:
time: 203 us; the launch traced here: 202 us
  starting transfers between devices  104 us (51%)
  waiting for transfers between devices  57.1 us (28%)
  blocking collectives  23 us (11%)
  local copies, waits for them, and re-layouts  6.1 us (3%)
  matrix products  4.14 us (2%)
  Pallas kernels  2.96 us (1%)
  between operations  2.55 us (1%)
  other arithmetic  2.1 us (1%)
    ppermute x11, starting transfers between devices, shifted(): lax.ppermute(value, axis, [(i, (i + by) % size) for i in range(size)])  62.7 us
    all_to_all x3, waiting for transfers between devices, exchange(): return lax.all_to_all(blocks, axes, 0, 0, tiled=True)  33.6 us
    ppermute x4, starting transfers between devices, along_z(): return lax.ppermute(value, ('zl', 'zh'), pairs)  26 us
    all_to_all x1, blocking collectives, exchange(): return lax.all_to_all(blocks, axes, 0, 0, tiled=True)  23 us
    ppermute x11, waiting for transfers between devices, shifted(): lax.ppermute(value, axis, [(i, (i + by) % size) for i in range(size)])  16.7 us
    all_to_all x3, starting transfers between devices, exchange(): return lax.all_to_all(blocks, axes, 0, 0, tiled=True)  15.3 us
    ppermute x4, waiting for transfers between devices, along_z(): return lax.ppermute(value, ('zl', 'zh'), pairs)  6.77 us
    dot_general x4, matrix products, dot(): return lax.dot_general(a, b, (dims, ((), ())), preferred_element_type=F32)  4.14 us
  transfers between devices with their start and end apart: 18, of which 8 were waited for; matrix products, arithmetic and copies ran while one was open for 1% of the time, Pallas kernels for 0%

profile of v7, /device:TPU:1, one launch (start us, length us, event | category | flops | bytes accessed | tf_op | source)
XLA Modules:
  0.0 201.9 jit_solution(11332838291743453201)
XLA Ops:
  0.6 1.2 convolution_convert_fusion.1
  1.8 1.2 convolution_convert_fusion
  3.7 4.8 %all-to-all-start = ((bf16[4,32,1152]{2,1,0:T(8,128)(2,1)}), bf16[4,32,1152]{2,1,0:T(8,128)(2,1)S(1)}, u32[]{:S(2)}, u32[]{:S(2)}) async-start(bf16[4,32,1152]{2,1,0:T(8,128)(2,1)} %pad_maximum_fusion), calls=%async_computation | async-start | bytes 589824 | tf_op jit(solution)/shard_map/embed/all_to_all | solution.py:24
  8.8 5.5 %all-to-all-done = bf16[4,32,1152]{2,1,0:T(8,128)(2,1)S(1)} async-done(((bf16[4,32,1152]{2,1,0:T(8,128)(2,1)}), bf16[4,32,1152]{2,1,0:T(8,128)(2,1)S(1)}, u32[]{:S(2)}, u32[]{:S(2)}) %all-to-all-start) | async-done | bytes 294944 | tf_op jit(solution)/shard_map/embed/all_to_all | solution.py:24
  14.3 19.2 %collective-permute-start = (f32[32,1152]{1,0:T(8,128)S(1)}, f32[32,1152]{1,0:T(8,128)S(1)}, u32[]{:S(2)}, u32[]{:S(2)}) collective-permute-start(f32[32,1152]{1,0:T(8,128)S(1)} %convert_reduce_fusion.2), channel_id=1, source_target_pairs={{0,4},{4,0},{1,5},{5,1},{2,6},{6,2},{3,7},{7,3},{8,12},{12,8},{9,1... | collective-permute-start | bytes 442376 | tf_op jit(solution)/shard_map/embed/ppermute | solution.py:33
  33.6 2.8 %collective-permute-done = f32[32,1152]{1,0:T(8,128)S(1)} collective-permute-done((f32[32,1152]{1,0:T(8,128)S(1)}, f32[32,1152]{1,0:T(8,128)S(1)}, u32[]{:S(2)}, u32[]{:S(2)}) %collective-permute-start) | collective-permute-done | bytes 147488 | tf_op jit(solution)/shard_map/embed/ppermute | solution.py:33
  36.6 7.5 %collective-permute-start.1 = (bf16[32,1152]{1,0:T(8,128)(2,1)S(1)}, bf16[32,1152]{1,0:T(8,128)(2,1)S(1)}, u32[]{:S(2)}, u32[]{:S(2)}) collective-permute-start(bf16[32,1152]{1,0:T(8,128)(2,1)S(1)} %get-tuple-element.9), channel_id=1, source_target_pairs={{0,64},{16,80},{32,96},{48,112},{64,0},{80,16},{96,32},{112,48},{1... | collective-permute-start | bytes 221192 | tf_op jit(solution)/shard_map/gather_own/ppermute | solution.py:33
  44.0 12.4 %collective-permute-start.6 = (bf16[32,1152]{1,0:T(8,128)(2,1)S(1)}, bf16[32,1152]{1,0:T(8,128)(2,1)S(1)}, u32[]{:S(2)}, u32[]{:S(2)}) collective-permute-start(bf16[32,1152]{1,0:T(8,128)(2,1)S(1)} %get-tuple-element.9), channel_id=1, source_target_pairs={{0,512},{128,640},{256,768},{384,896},{512,4},{640,132},{768,260},... | collective-permute-start | bytes 221192 | tf_op jit(solution)/shard_map/gather_others/ppermute | solution.py:40
  56.5 6.8 %collective-permute-done.6 = bf16[32,1152]{1,0:T(8,128)(2,1)S(1)} collective-permute-done((bf16[32,1152]{1,0:T(8,128)(2,1)S(1)}, bf16[32,1152]{1,0:T(8,128)(2,1)S(1)}, u32[]{:S(2)}, u32[]{:S(2)}) %collective-permute-start.6) | collective-permute-done | bytes 73760 | tf_op jit(solution)/shard_map/gather_others/ppermute | solution.py:40
  63.3 1.9 collective-permute-start.7
  65.2 4.6 %collective-permute-start.8 = (bf16[64,1152]{1,0:T(8,128)(2,1)S(1)}, bf16[64,1152]{1,0:T(8,128)(2,1)S(1)}, u32[]{:S(2)}, u32[]{:S(2)}) collective-permute-start(bf16[64,1152]{1,0:T(8,128)(2,1)S(1)} %get-tuple-element.14), channel_id=1, source_target_pairs={{0,900},{128,0},{256,128},{384,256},{512,384},{640,512},{768,640},... | collective-permute-start | bytes 442376 | tf_op jit(solution)/shard_map/gather_others/ppermute | solution.py:40
  69.8 7.1 %collective-permute-start.9 = (bf16[64,1152]{1,0:T(8,128)(2,1)S(1)}, bf16[64,1152]{1,0:T(8,128)(2,1)S(1)}, u32[]{:S(2)}, u32[]{:S(2)}) collective-permute-start(bf16[64,1152]{1,0:T(8,128)(2,1)S(1)} %get-tuple-element.14), channel_id=1, source_target_pairs={{0,256},{128,384},{256,512},{384,640},{512,768},{640,896},{768,4},... | collective-permute-start | bytes 442376 | tf_op jit(solution)/shard_map/gather_others/ppermute | solution.py:40
  76.9 2.3 %collective-permute-start.2 = (bf16[64,1152]{1,0:T(8,128)(2,1)S(1)}, bf16[64,1152]{1,0:T(8,128)(2,1)S(1)}, u32[]{:S(2)}, u32[]{:S(2)}) collective-permute-start(bf16[64,1152]{1,0:T(8,128)(2,1)S(1)} %get-tuple-element.15), channel_id=1, source_target_pairs={{0,16},{16,32},{32,48},{48,64},{64,80},{80,96},{96,112},{112,0},{1... | collective-permute-start | bytes 442376 | tf_op jit(solution)/shard_map/gather_own/ppermute | solution.py:33
  79.2 4.2 %collective-permute-start.3 = (bf16[64,1152]{1,0:T(8,128)(2,1)S(1)}, bf16[64,1152]{1,0:T(8,128)(2,1)S(1)}, u32[]{:S(2)}, u32[]{:S(2)}) collective-permute-start(bf16[64,1152]{1,0:T(8,128)(2,1)S(1)} %get-tuple-element.15), channel_id=1, source_target_pairs={{0,112},{16,0},{32,16},{48,32},{64,48},{80,64},{96,80},{112,96},{1... | collective-permute-start | bytes 442376 | tf_op jit(solution)/shard_map/gather_own/ppermute | solution.py:33
  83.5 1.9 collective-permute-start.4
  85.5 2.2 %collective-permute-start.10 = (bf16[256,1152]{1,0:T(8,128)(2,1)S(1)}, bf16[256,1152]{1,0:T(8,128)(2,1)S(1)}, u32[]{:S(2)}, u32[]{:S(2)}) collective-permute-start(bf16[256,1152]{1,0:T(8,128)(2,1)S(1)} %constant_dynamic-update-slice_fusion.5.refs_0_), channel_id=1, source_target_pairs={{0,1},{1,2},{2,3},{3,0},{4,5},{5,6},{6,7},{7,4},{8,9},{9,10},{10,1... | collective-permute-start | bytes 1769480 | tf_op jit(solution)/shard_map/gather_others/ppermute | solution.py:33
  87.7 4.3 %collective-permute-start.11 = (bf16[256,1152]{1,0:T(8,128)(2,1)S(1)}, bf16[256,1152]{1,0:T(8,128)(2,1)S(1)}, u32[]{:S(2)}, u32[]{:S(2)}) collective-permute-start(bf16[256,1152]{1,0:T(8,128)(2,1)S(1)} %constant_dynamic-update-slice_fusion.5.refs_0_), channel_id=1, source_target_pairs={{0,3},{1,0},{2,1},{3,2},{4,7},{5,4},{6,5},{7,6},{8,11},{9,8},{10,9... | collective-permute-start | bytes 1769480 | tf_op jit(solution)/shard_map/gather_others/ppermute | solution.py:33
  92.0 2.9 %collective-permute-start.12 = (bf16[256,1152]{1,0:T(8,128)(2,1)S(1)}, bf16[256,1152]{1,0:T(8,128)(2,1)S(1)}, u32[]{:S(2)}, u32[]{:S(2)}) collective-permute-start(bf16[256,1152]{1,0:T(8,128)(2,1)S(1)} %constant_dynamic-update-slice_fusion.5.refs_0_), channel_id=1, source_target_pairs={{0,2},{1,3},{2,0},{3,1},{4,6},{5,7},{6,4},{7,5},{8,10},{9,11},{10,... | collective-permute-start | bytes 1769480 | tf_op jit(solution)/shard_map/gather_others/ppermute | solution.py:33
  95.0 5.3 %collective-permute-start.5 = (bf16[256,1152]{1,0:T(8,128)(2,1)S(1)}, bf16[256,1152]{1,0:T(8,128)(2,1)}, u32[]{:S(2)}, u32[]{:S(2)}) collective-permute-start(bf16[256,1152]{1,0:T(8,128)(2,1)S(1)} %constant_dynamic-update-slice_fusion.mine), channel_id=1, source_target_pairs={{0,8},{8,0},{1,9},{9,1},{2,10},{10,2},{3,11},{11,3},{4,12},{12,4},... | collective-permute-start | bytes 1769480 | tf_op jit(solution)/shard_map/gather_own/ppermute | solution.py:33
  102.2 9.7 %collective-permute-done.12.refs_3_ = bf16[256,1152]{1,0:T(8,128)(2,1)S(1)} collective-permute-done((bf16[256,1152]{1,0:T(8,128)(2,1)S(1)}, bf16[256,1152]{1,0:T(8,128)(2,1)S(1)}, u32[]{:S(2)}, u32[]{:S(2)}) %collective-permute-start.12) | collective-permute-done | bytes 589856 | tf_op jit(solution)/shard_map/gather_others/ppermute | solution.py:33
  111.9 3.0 %pairs.1 = (f32[256,1152]{1,0:T(8,128)S(1)}, f32[256,1152]{1,0:T(8,128)S(1)}) custom-call(f32[2]{0:T(128)S(1)} %pad_maximum_fusion.3.factors, s32[8]{0:T(128)S(1)} %stack.40.places, s32[256,1]{1,0:T(8,128)S(1)} %copy.10.own_ids, s32[1,512]{1,0:T(1,128)S(1)} %bitcast.34, bf16[256,1152]{1,0:T(8,128)(2,1)S(1)} %constant_dynamic-update-slice_fusion.mine, ...), custom_call_target="tpu_custom_call" | custom-call | flops 1207959552 | bytes 5898240 | tf_op jit(solution)/shard_map/pairs/pallas_call | solution.py:84
  114.9 8.2 %collective-permute-start.13 = (f32[256,1152]{1,0:T(8,128)S(1)}, f32[256,1152]{1,0:T(8,128)S(1)}, u32[]{:S(2)}, u32[]{:S(2)}) collective-permute-start(f32[256,1152]{1,0:T(8,128)S(1)} %get-tuple-element.7), channel_id=1, source_target_pairs={{0,8},{8,0},{1,9},{9,1},{2,10},{10,2},{3,11},{11,3},{4,12},{12,4},... | collective-permute-start | bytes 3538952 | tf_op jit(solution)/shard_map/reduce_pairs/ppermute | solution.py:33
  123.1 2.5 %collective-permute-done.13 = f32[256,1152]{1,0:T(8,128)S(1)} collective-permute-done((f32[256,1152]{1,0:T(8,128)S(1)}, f32[256,1152]{1,0:T(8,128)S(1)}, u32[]{:S(2)}, u32[]{:S(2)}) %collective-permute-start.13) | collective-permute-done | bytes 1179680 | tf_op jit(solution)/shard_map/reduce_pairs/ppermute | solution.py:33
  125.7 23.0 %all_to_all.20 = bf16[8,32,1152]{2,1,0:T(8,128)(2,1)S(1)} all-to-all(bf16[8,32,1152]{2,1,0:T(8,128)(2,1)S(1)} %bitcast.35), channel_id=1, replica_groups=mesh['zl'=8,'y'=8,'c'=2,'zh'=2,'x'=4] {'y'}, dimensions={0} | all-to-all | bytes 1179648 | tf_op jit(solution)/shard_map/reduce_pairs/all_to_all | solution.py:24
  149.8 4.6 %all-to-all-start.2 = ((bf16[4,32,1152]{2,1,0:T(8,128)(2,1)}), bf16[4,32,1152]{2,1,0:T(8,128)(2,1)S(1)}, u32[]{:S(2)}, u32[]{:S(2)}) async-start(bf16[4,32,1152]{2,1,0:T(8,128)(2,1)} %broadcast_in_dim.26), calls=%async_computation.2 | async-start | bytes 589824 | tf_op jit(solution)/shard_map/back/all_to_all | solution.py:24
  154.8 5.4 %all-to-all-done.2 = bf16[4,32,1152]{2,1,0:T(8,128)(2,1)S(1)} async-done(((bf16[4,32,1152]{2,1,0:T(8,128)(2,1)}), bf16[4,32,1152]{2,1,0:T(8,128)(2,1)S(1)}, u32[]{:S(2)}, u32[]{:S(2)}) %all-to-all-start.2) | async-done | bytes 294944 | tf_op jit(solution)/shard_map/back/all_to_all | solution.py:24
  160.1 1.4 fusion.3
  161.8 4.8 %collective-permute-start.14 = (f32[576,288]{0,1:T(8,128)S(1)}, f32[576,288]{0,1:T(8,128)S(1)}, u32[]{:S(2)}, u32[]{:S(2)}) collective-permute-start(f32[576,288]{0,1:T(8,128)S(1)} %slice.25), channel_id=1, source_target_pairs={{0,8},{8,0},{1,9},{9,1},{2,10},{10,2},{3,11},{11,3},{4,12},{12,4},... | collective-permute-start | bytes 1990664 | tf_op jit(solution)/shard_map/weight_grad/ppermute | solution.py:33
  166.6 1.8 collective-permute-done.14
  168.9 1.6 reshape.89
  170.5 5.8 %all-to-all-start.3 = ((bf16[64,2,1296]{2,1,0:T(2,128)(2,1)}), bf16[64,2,1296]{2,1,0:T(2,128)(2,1)S(1)}, u32[]{:S(2)}, u32[]{:S(2)}) async-start(bf16[64,2,1296]{2,1,0:T(2,128)(2,1)} %reshape.89), calls=%async_computation.3 | async-start | bytes 720896 | tf_op jit(solution)/shard_map/weight_grad/all_to_all | solution.py:24
  177.4 22.7 %all-to-all-done.3 = bf16[64,2,1296]{2,1,0:T(2,128)(2,1)S(1)} async-done(((bf16[64,2,1296]{2,1,0:T(2,128)(2,1)}), bf16[64,2,1296]{2,1,0:T(2,128)(2,1)S(1)}, u32[]{:S(2)}, u32[]{:S(2)}) %all-to-all-start.3) | async-done | bytes 331808 | tf_op jit(solution)/shard_map/weight_grad/all_to_all | solution.py:24
  (79 shorter events, 7.1 us)
Async XLA Ops:
  3.7 10.5 %all-to-all-start = ((bf16[4,32,1152]{2,1,0:T(8,128)(2,1)}), bf16[4,32,1152]{2,1,0:T(8,128)(2,1)S(1)}, u32[]{:S(2)}, u32[]{:S(2)}) async-start(bf16[4,32,1152]{2,1,0:T(8,128)(2,1)} %pad_maximum_fusion), calls=%async_computation | async-start | bytes 589824 | tf_op jit(solution)/shard_map/embed/all_to_all | solution.py:24
  14.3 22.0 %collective-permute-start = (f32[32,1152]{1,0:T(8,128)S(1)}, f32[32,1152]{1,0:T(8,128)S(1)}, u32[]{:S(2)}, u32[]{:S(2)}) collective-permute-start(f32[32,1152]{1,0:T(8,128)S(1)} %convert_reduce_fusion.2), channel_id=1, source_target_pairs={{0,4},{4,0},{1,5},{5,1},{2,6},{6,2},{3,7},{7,3},{8,12},{12,8},{9,1... | collective-permute-start | bytes 442376 | tf_op jit(solution)/shard_map/embed/ppermute | solution.py:33
  36.6 19.9 %collective-permute-start.1 = (bf16[32,1152]{1,0:T(8,128)(2,1)S(1)}, bf16[32,1152]{1,0:T(8,128)(2,1)S(1)}, u32[]{:S(2)}, u32[]{:S(2)}) collective-permute-start(bf16[32,1152]{1,0:T(8,128)(2,1)S(1)} %get-tuple-element.9), channel_id=1, source_target_pairs={{0,64},{16,80},{32,96},{48,112},{64,0},{80,16},{96,32},{112,48},{1... | collective-permute-start | bytes 221192 | tf_op jit(solution)/shard_map/gather_own/ppermute | solution.py:33
  44.0 19.2 %collective-permute-start.6 = (bf16[32,1152]{1,0:T(8,128)(2,1)S(1)}, bf16[32,1152]{1,0:T(8,128)(2,1)S(1)}, u32[]{:S(2)}, u32[]{:S(2)}) collective-permute-start(bf16[32,1152]{1,0:T(8,128)(2,1)S(1)} %get-tuple-element.9), channel_id=1, source_target_pairs={{0,512},{128,640},{256,768},{384,896},{512,4},{640,132},{768,260},... | collective-permute-start | bytes 221192 | tf_op jit(solution)/shard_map/gather_others/ppermute | solution.py:40
  63.3 20.2 %collective-permute-start.7 = (bf16[64,1152]{1,0:T(8,128)(2,1)S(1)}, bf16[64,1152]{1,0:T(8,128)(2,1)S(1)}, u32[]{:S(2)}, u32[]{:S(2)}) collective-permute-start(bf16[64,1152]{1,0:T(8,128)(2,1)S(1)} %get-tuple-element.14), channel_id=1, source_target_pairs={{0,128},{128,256},{256,384},{384,512},{512,640},{640,768},{768,896... | collective-permute-start | bytes 442376 | tf_op jit(solution)/shard_map/gather_others/ppermute | solution.py:40
  65.2 20.2 %collective-permute-start.8 = (bf16[64,1152]{1,0:T(8,128)(2,1)S(1)}, bf16[64,1152]{1,0:T(8,128)(2,1)S(1)}, u32[]{:S(2)}, u32[]{:S(2)}) collective-permute-start(bf16[64,1152]{1,0:T(8,128)(2,1)S(1)} %get-tuple-element.14), channel_id=1, source_target_pairs={{0,900},{128,0},{256,128},{384,256},{512,384},{640,512},{768,640},... | collective-permute-start | bytes 442376 | tf_op jit(solution)/shard_map/gather_others/ppermute | solution.py:40
  69.8 15.7 %collective-permute-start.9 = (bf16[64,1152]{1,0:T(8,128)(2,1)S(1)}, bf16[64,1152]{1,0:T(8,128)(2,1)S(1)}, u32[]{:S(2)}, u32[]{:S(2)}) collective-permute-start(bf16[64,1152]{1,0:T(8,128)(2,1)S(1)} %get-tuple-element.14), channel_id=1, source_target_pairs={{0,256},{128,384},{256,512},{384,640},{512,768},{640,896},{768,4},... | collective-permute-start | bytes 442376 | tf_op jit(solution)/shard_map/gather_others/ppermute | solution.py:40
  76.9 15.1 %collective-permute-start.2 = (bf16[64,1152]{1,0:T(8,128)(2,1)S(1)}, bf16[64,1152]{1,0:T(8,128)(2,1)S(1)}, u32[]{:S(2)}, u32[]{:S(2)}) collective-permute-start(bf16[64,1152]{1,0:T(8,128)(2,1)S(1)} %get-tuple-element.15), channel_id=1, source_target_pairs={{0,16},{16,32},{32,48},{48,64},{64,80},{80,96},{96,112},{112,0},{1... | collective-permute-start | bytes 442376 | tf_op jit(solution)/shard_map/gather_own/ppermute | solution.py:33
  79.2 15.7 %collective-permute-start.3 = (bf16[64,1152]{1,0:T(8,128)(2,1)S(1)}, bf16[64,1152]{1,0:T(8,128)(2,1)S(1)}, u32[]{:S(2)}, u32[]{:S(2)}) collective-permute-start(bf16[64,1152]{1,0:T(8,128)(2,1)S(1)} %get-tuple-element.15), channel_id=1, source_target_pairs={{0,112},{16,0},{32,16},{48,32},{64,48},{80,64},{96,80},{112,96},{1... | collective-permute-start | bytes 442376 | tf_op jit(solution)/shard_map/gather_own/ppermute | solution.py:33
  83.5 11.5 %collective-permute-start.4 = (bf16[64,1152]{1,0:T(8,128)(2,1)S(1)}, bf16[64,1152]{1,0:T(8,128)(2,1)S(1)}, u32[]{:S(2)}, u32[]{:S(2)}) collective-permute-start(bf16[64,1152]{1,0:T(8,128)(2,1)S(1)} %get-tuple-element.15), channel_id=1, source_target_pairs={{0,32},{16,48},{32,64},{48,80},{64,96},{80,112},{96,0},{112,16},{1... | collective-permute-start | bytes 442376 | tf_op jit(solution)/shard_map/gather_own/ppermute | solution.py:33
  85.5 16.8 %collective-permute-start.10 = (bf16[256,1152]{1,0:T(8,128)(2,1)S(1)}, bf16[256,1152]{1,0:T(8,128)(2,1)S(1)}, u32[]{:S(2)}, u32[]{:S(2)}) collective-permute-start(bf16[256,1152]{1,0:T(8,128)(2,1)S(1)} %constant_dynamic-update-slice_fusion.5.refs_0_), channel_id=1, source_target_pairs={{0,1},{1,2},{2,3},{3,0},{4,5},{5,6},{6,7},{7,4},{8,9},{9,10},{10,1... | collective-permute-start | bytes 1769480 | tf_op jit(solution)/shard_map/gather_others/ppermute | solution.py:33
  87.7 14.6 %collective-permute-start.11 = (bf16[256,1152]{1,0:T(8,128)(2,1)S(1)}, bf16[256,1152]{1,0:T(8,128)(2,1)S(1)}, u32[]{:S(2)}, u32[]{:S(2)}) collective-permute-start(bf16[256,1152]{1,0:T(8,128)(2,1)S(1)} %constant_dynamic-update-slice_fusion.5.refs_0_), channel_id=1, source_target_pairs={{0,3},{1,0},{2,1},{3,2},{4,7},{5,4},{6,5},{7,6},{8,11},{9,8},{10,9... | collective-permute-start | bytes 1769480 | tf_op jit(solution)/shard_map/gather_others/ppermute | solution.py:33
  92.0 19.9 %collective-permute-start.12 = (bf16[256,1152]{1,0:T(8,128)(2,1)S(1)}, bf16[256,1152]{1,0:T(8,128)(2,1)S(1)}, u32[]{:S(2)}, u32[]{:S(2)}) collective-permute-start(bf16[256,1152]{1,0:T(8,128)(2,1)S(1)} %constant_dynamic-update-slice_fusion.5.refs_0_), channel_id=1, source_target_pairs={{0,2},{1,3},{2,0},{3,1},{4,6},{5,7},{6,4},{7,5},{8,10},{9,11},{10,... | collective-permute-start | bytes 1769480 | tf_op jit(solution)/shard_map/gather_others/ppermute | solution.py:33
  95.0 17.0 %collective-permute-start.5 = (bf16[256,1152]{1,0:T(8,128)(2,1)S(1)}, bf16[256,1152]{1,0:T(8,128)(2,1)}, u32[]{:S(2)}, u32[]{:S(2)}) collective-permute-start(bf16[256,1152]{1,0:T(8,128)(2,1)S(1)} %constant_dynamic-update-slice_fusion.mine), channel_id=1, source_target_pairs={{0,8},{8,0},{1,9},{9,1},{2,10},{10,2},{3,11},{11,3},{4,12},{12,4},... | collective-permute-start | bytes 1769480 | tf_op jit(solution)/shard_map/gather_own/ppermute | solution.py:33
  114.9 10.6 %collective-permute-start.13 = (f32[256,1152]{1,0:T(8,128)S(1)}, f32[256,1152]{1,0:T(8,128)S(1)}, u32[]{:S(2)}, u32[]{:S(2)}) collective-permute-start(f32[256,1152]{1,0:T(8,128)S(1)} %get-tuple-element.7), channel_id=1, source_target_pairs={{0,8},{8,0},{1,9},{9,1},{2,10},{10,2},{3,11},{11,3},{4,12},{12,4},... | collective-permute-start | bytes 3538952 | tf_op jit(solution)/shard_map/reduce_pairs/ppermute | solution.py:33
  148.7 6.0 %copy-start.2 = (bf16[64,144]{1,0:T(8,128)(2,1)S(1)}, bf16[64,144]{1,0:T(8,128)(2,1)}, u32[]{:S(2)}) copy-start(bf16[64,144]{1,0:T(8,128)(2,1)} %param.7) | copy-start | bytes 55300
  148.7 6.0 %copy-start.3 = (bf16[64,144]{1,0:T(8,128)(2,1)S(1)}, bf16[64,144]{1,0:T(8,128)(2,1)}, u32[]{:S(2)}) copy-start(bf16[64,144]{1,0:T(8,128)(2,1)} %param.6) | copy-start | bytes 55300
  149.8 10.4 %all-to-all-start.2 = ((bf16[4,32,1152]{2,1,0:T(8,128)(2,1)}), bf16[4,32,1152]{2,1,0:T(8,128)(2,1)S(1)}, u32[]{:S(2)}, u32[]{:S(2)}) async-start(bf16[4,32,1152]{2,1,0:T(8,128)(2,1)} %broadcast_in_dim.26), calls=%async_computation.2 | async-start | bytes 589824 | tf_op jit(solution)/shard_map/back/all_to_all | solution.py:24
  161.8 6.6 %collective-permute-start.14 = (f32[576,288]{0,1:T(8,128)S(1)}, f32[576,288]{0,1:T(8,128)S(1)}, u32[]{:S(2)}, u32[]{:S(2)}) collective-permute-start(f32[576,288]{0,1:T(8,128)S(1)} %slice.25), channel_id=1, source_target_pairs={{0,8},{8,0},{1,9},{9,1},{2,10},{10,2},{3,11},{11,3},{4,12},{12,4},... | collective-permute-start | bytes 1990664 | tf_op jit(solution)/shard_map/weight_grad/ppermute | solution.py:33
  168.7 7.6 %copy-start = (bf16[144,1152]{1,0:T(8,128)(2,1)S(1)}, bf16[144,1152]{1,0:T(8,128)(2,1)}, u32[]{:S(2)}) copy-start(bf16[144,1152]{1,0:T(8,128)(2,1)} %param.9) | copy-start | bytes 995332
  168.7 7.6 %copy-start.1 = (bf16[144,1152]{1,0:T(8,128)(2,1)S(1)}, bf16[144,1152]{1,0:T(8,128)(2,1)}, u32[]{:S(2)}) copy-start(bf16[144,1152]{1,0:T(8,128)(2,1)} %param.8) | copy-start | bytes 995332
  170.5 29.7 %all-to-all-start.3 = ((bf16[64,2,1296]{2,1,0:T(2,128)(2,1)}), bf16[64,2,1296]{2,1,0:T(2,128)(2,1)S(1)}, u32[]{:S(2)}, u32[]{:S(2)}) async-start(bf16[64,2,1296]{2,1,0:T(2,128)(2,1)} %reshape.89), calls=%async_computation.3 | async-start | bytes 720896 | tf_op jit(solution)/shard_map/weight_grad/all_to_all | solution.py:24

commit v8 on v6

--- a/solution.py
+++ b/solution.py
@@ -11,7 +11,6 @@
 SIZES = {"zl": 8, "y": 8, "c": 2, "zh": 2, "x": 4}
 STEPS = (0, 1, 3, 2)
 GROUPS = (0, -4, -1, -5, 1, -3, -2, -6)
-RUN = 16
 F32 = jnp.float32
 BF16 = jnp.bfloat16
 
@@ -46,25 +45,17 @@
 
 def pair_kernel(factors, own_ids, other_ids, mine, theirs, *refs):
     blocks, (mine_sum, theirs_sum, held, partners) = refs[: len(STEPS)], refs[len(STEPS) :]
-    run = RUN
-    for kind in range(2):
-        for target, sources in ((held, (mine, theirs)), (partners, blocks)):
-            at = 0
-            for source in sources:
-                for start in range(kind * run, source.shape[0], 2 * run):
-                    target[kind, at : at + run, :] = source[start : start + run, :]
-                    at += run
-    matched = own_ids[...] == other_ids[...]
-    count = held.shape[1] // 2
-    for kind in range(2):
-        other = partners[1 - kind]
-        logits = factors[0] * dot(held[kind], other, ((1,), (1,))) + factors[1]
-        coef = jax.nn.sigmoid(logits) - jnp.where(matched, 1.0, 0.0)
-        total = dot(coef.astype(BF16), other, ((1,), (0,)))
-        for part, out in ((total[:count], mine_sum), (total[count:], theirs_sum)):
-            for at in range(0, count, run):
-                start = 2 * at + kind * run
-                out[start : start + run, :] = part[at : at + run]
+    for target, sources in ((held, (mine, theirs)), (partners, blocks)):
+        size = sources[0].shape[0]
+        for i, source in enumerate(sources):
+            target[i * size : (i + 1) * size, :] = source[...]
+    other = partners[...]
+    logits = factors[0] * dot(held[...], other, ((1,), (1,))) + factors[1]
+    coef = jax.nn.sigmoid(logits) - jnp.where(own_ids[...] == other_ids[...], 1.0, 0.0)
+    total = dot(coef.astype(BF16), other, ((1,), (0,)))
+    count = mine.shape[0]
+    mine_sum[...] = total[:count]
+    theirs_sum[...] = total[count:]
 
 
 def pair_sums(factors, own_ids, other_ids, mine, theirs, others):
@@ -77,15 +68,12 @@
         out_shape=(out, out),
         in_specs=[pl.BlockSpec(memory_space=pltpu.SMEM)] + [whole] * (4 + len(others)),
         out_specs=(whole, whole),
-        scratch_shapes=[
-            pltpu.VMEM((2, count, width), BF16),
-            pltpu.VMEM((2, partners // 2, width), BF16),
-        ],
-        compiler_params=pltpu.CompilerParams(vmem_limit_bytes=28 * 2**20),
+        scratch_shapes=[pltpu.VMEM((2 * count, width), BF16), pltpu.VMEM((partners, width), BF16)],
+        compiler_params=pltpu.CompilerParams(vmem_limit_bytes=24 * 2**20),
         cost_estimate=pl.CostEstimate(
-            flops=4 * count * partners * width,
+            flops=8 * count * partners * width,
             bytes_accessed=12 * count * width + 2 * partners * width,
-            transcendentals=count * partners,
+            transcendentals=2 * count * partners,
         ),
     )(factors, own_ids, other_ids, mine, theirs, *others)
 
@@ -93,7 +81,7 @@
 def local(image_features, text_features, image_weight, text_weight, log_scale, logit_bias):
     scale = jnp.exp(log_scale[0])
     bias = logit_bias[0]
-    zl, y, c, x = (lax.axis_index(axis) for axis in ("zl", "y", "c", "x"))
+    zl, y, c, zh, x = (lax.axis_index(axis) for axis in ("zl", "y", "c", "zh", "x"))
     rows, depth = image_features.shape
     width = image_weight.shape[1]
     own = rows // SIZES["x"]
@@ -109,14 +97,23 @@
         inverse = lax.rsqrt(jnp.sum(embed * embed, axis=-1, keepdims=True) + EPS)
         unit = embed * inverse
         vec = unit.astype(BF16)
+        kinds = vec.reshape(2, own, width)
 
     with jax.named_scope("gather_own"):
-        mine = spread(vec, "y", SIZES["y"]).reshape(-1, width)
+        own_vec = lax.dynamic_index_in_dim(kinds, zh, 0, keepdims=False)
+        mine = spread(own_vec, "y", SIZES["y"]).reshape(-1, width)
         theirs = shifted(mine, "c", 1)
 
     with jax.named_scope("gather_others"):
-        pair = jnp.concatenate([vec, along_z(vec, 4)])
-        column = jnp.concatenate([pair] + [along_z(pair, by) for by in (1, -1, 2)])
+        pair = jnp.stack([kinds, along_z(vec, 4).reshape(2, own, width)], axis=1)
+        pair = pair.reshape(2, 2 * own, width)
+        at = zh * SIZES["zl"] + zl
+        column = []
+        for by in (0, 1, -1, 2):
+            half = (at + by + 2 * SIZES["zl"]) // SIZES["zl"] % 2
+            block = jnp.where(half == 0, pair[1], pair[0])
+            column.append(along_z(block, by) if by else block)
+        column = jnp.concatenate(column)
         others = [column] + [shifted(column, "x", by) for by in STEPS[1:]]
 
     with jax.named_scope("pairs"):
@@ -141,12 +138,18 @@
 
     with jax.named_scope("reduce_pairs"):
         direction = mine_sum + shifted(theirs_sum, "c", 1)
-        direction = exchange(direction.astype(BF16).reshape(SIZES["y"], 2 * own, width), "y")
+        direction = exchange(direction.astype(BF16).reshape(SIZES["y"], own, width), "y")
         direction = scale * jnp.sum(direction.astype(F32), axis=0)
 
     with jax.named_scope("back"):
+        unit = lax.dynamic_index_in_dim(unit.reshape(2, own, width), zh, 0, keepdims=False)
+        inverse = lax.dynamic_index_in_dim(inverse.reshape(2, own, 1), zh, 0, keepdims=False)
         inner = jnp.sum(unit * direction, axis=-1, keepdims=True)
         back = (inverse * (direction - unit * inner)).astype(BF16)
+        swapped = shifted(back, "zh", 1)
+        back = jnp.concatenate(
+            [jnp.where(zh == 0, back, swapped), jnp.where(zh == 0, swapped, back)]
+        )
         back = spread(back, "x", SIZES["x"]).reshape(-1, width)
 
     with jax.named_scope("feature_grad"):

time: 197 us -> 191 us (0.970)
  blocking collectives: 26.2 us -> 0 us
  starting transfers between devices: 94.3 us -> 112 us
  waiting for transfers between devices: 57.8 us -> 61.4 us
    all_to_all x1 -> x0, blocking collectives: 26.2 us -> none  [exchange(): return lax.all_to_all(blocks, axes, 0, 0, tiled=True)]
    all_to_all x4 -> x5, waiting for transfers between devices: 33.7 us -> 46 us  [exchange(): return lax.all_to_all(blocks, axes, 0, 0, tiled=True)]
    ppermute x7 -> x8, starting transfers between devices: 47.5 us -> 56.8 us  [shifted(): lax.ppermute(value, axis, [(i, (i + by) % size) for i in range(size)])]
    all_to_all x4 -> x5, starting transfers between devices: 23 us -> 31.1 us  [exchange(): return lax.all_to_all(blocks, axes, 0, 0, tiled=True)]
    ppermute x7 -> x8, waiting for transfers between devices: 16.4 us -> 9.6 us  [shifted(): lax.ppermute(value, axis, [(i, (i + by) % size) for i in range(size)])]
  transfers between devices with their start and end apart: 15 -> 17, of which waited for: 9 -> 12; matrix products, arithmetic and copies ran while one was open for 1% -> 1% of each run, Pallas kernels for 0% -> 0%
where the time goes in v8:
time: 191 us; the launch traced here: 190 us
  starting transfers between devices  112 us (59%)
  waiting for transfers between devices  61.4 us (32%)
  local copies, waits for them, and re-layouts  6.5 us (3%)
  matrix products  4.15 us (2%)
  other arithmetic  2.7 us (1%)
  between operations  2.47 us (1%)
    ppermute x8, starting transfers between devices, shifted(): lax.ppermute(value, axis, [(i, (i + by) % size) for i in range(size)])  56.8 us
    all_to_all x5, waiting for transfers between devices, exchange(): return lax.all_to_all(blocks, axes, 0, 0, tiled=True)  46 us
    all_to_all x5, starting transfers between devices, exchange(): return lax.all_to_all(blocks, axes, 0, 0, tiled=True)  31.1 us
    ppermute x4, starting transfers between devices, along_z(): return lax.ppermute(value, ('zl', 'zh'), pairs)  23.8 us
    ppermute x8, waiting for transfers between devices, shifted(): lax.ppermute(value, axis, [(i, (i + by) % size) for i in range(size)])  9.6 us
    ppermute x4, waiting for transfers between devices, along_z(): return lax.ppermute(value, ('zl', 'zh'), pairs)  5.78 us
    dot_general x4, matrix products, dot(): return lax.dot_general(a, b, (dims, ((), ())), preferred_element_type=F32)  4.15 us
  transfers between devices with their start and end apart: 17, of which 12 were waited for; matrix products, arithmetic and copies ran while one was open for 1% of the time, Pallas kernels for 0%

profile of v8, /device:TPU:1, one launch (start us, length us, event | category | flops | bytes accessed | tf_op | source)
XLA Modules:
  0.0 190.4 jit_solution(4771842298099909595)
XLA Ops:
  0.6 1.2 convolution_convert_fusion.1
  1.8 1.2 convolution_convert_fusion
  3.7 4.8 %all-to-all-start = ((bf16[4,32,1152]{2,1,0:T(8,128)(2,1)}), bf16[4,32,1152]{2,1,0:T(8,128)(2,1)S(1)}, u32[]{:S(2)}, u32[]{:S(2)}) async-start(bf16[4,32,1152]{2,1,0:T(8,128)(2,1)} %pad_maximum_fusion), calls=%async_computation | async-start | bytes 589824 | tf_op jit(solution)/shard_map/embed/all_to_all | solution.py:23
  8.8 5.5 %all-to-all-done = bf16[4,32,1152]{2,1,0:T(8,128)(2,1)S(1)} async-done(((bf16[4,32,1152]{2,1,0:T(8,128)(2,1)}), bf16[4,32,1152]{2,1,0:T(8,128)(2,1)S(1)}, u32[]{:S(2)}, u32[]{:S(2)}) %all-to-all-start) | async-done | bytes 294944 | tf_op jit(solution)/shard_map/embed/all_to_all | solution.py:23
  14.3 19.2 %collective-permute-start = (f32[32,1152]{1,0:T(8,128)S(1)}, f32[32,1152]{1,0:T(8,128)S(1)}, u32[]{:S(2)}, u32[]{:S(2)}) collective-permute-start(f32[32,1152]{1,0:T(8,128)S(1)} %convert_reduce_fusion.2), channel_id=1, source_target_pairs={{0,4},{4,0},{1,5},{5,1},{2,6},{6,2},{3,7},{7,3},{8,12},{12,8},{9,1... | collective-permute-start | bytes 442376 | tf_op jit(solution)/shard_map/embed/ppermute | solution.py:32
  35.1 1.2 collective-permute-done
  36.6 10.8 %collective-permute-start.2 = (bf16[32,1152]{1,0:T(8,128)(2,1)S(1)}, bf16[32,1152]{1,0:T(8,128)(2,1)S(1)}, u32[]{:S(2)}, u32[]{:S(2)}) collective-permute-start(bf16[32,1152]{1,0:T(8,128)(2,1)S(1)} %get-tuple-element.11), channel_id=1, source_target_pairs={{0,512},{128,640},{256,768},{384,896},{512,4},{640,132},{768,260},... | collective-permute-start | bytes 221192 | tf_op jit(solution)/shard_map/gather_others/ppermute | solution.py:39
  48.1 8.4 %all-to-all-start.1 = ((bf16[8,16,1152]{2,1,0:T(8,128)(2,1)}), bf16[8,16,1152]{2,1,0:T(8,128)(2,1)S(1)}, u32[]{:S(2)}, u32[]{:S(2)}) async-start(bf16[8,16,1152]{2,1,0:T(8,128)(2,1)} %broadcast_in_dim.42), calls=%async_computation.1 | async-start | bytes 589824 | tf_op jit(solution)/shard_map/gather_own/all_to_all | solution.py:23
  56.5 1.6 collective-permute-done.2
  58.2 1.9 %collective-permute-start.3 = (bf16[32,1152]{1,0:T(8,128)(2,1)S(1)}, bf16[32,1152]{1,0:T(8,128)(2,1)S(1)}, u32[]{:S(2)}, u32[]{:S(2)}) collective-permute-start(bf16[32,1152]{1,0:T(8,128)(2,1)S(1)} %bitcast.67), channel_id=1, source_target_pairs={{0,128},{128,256},{256,384},{384,512},{512,640},{640,768},{768,896... | collective-permute-start | bytes 221192 | tf_op jit(solution)/shard_map/gather_others/ppermute | solution.py:39
  60.1 4.6 %collective-permute-start.4 = (bf16[32,1152]{1,0:T(8,128)(2,1)S(1)}, bf16[32,1152]{1,0:T(8,128)(2,1)S(1)}, u32[]{:S(2)}, u32[]{:S(2)}) collective-permute-start(bf16[32,1152]{1,0:T(8,128)(2,1)S(1)} %bitcast.66), channel_id=1, source_target_pairs={{0,900},{128,0},{256,128},{384,256},{512,384},{640,512},{768,640},... | collective-permute-start | bytes 221192 | tf_op jit(solution)/shard_map/gather_others/ppermute | solution.py:39
  64.7 6.5 %collective-permute-start.5 = (bf16[32,1152]{1,0:T(8,128)(2,1)S(1)}, bf16[32,1152]{1,0:T(8,128)(2,1)S(1)}, u32[]{:S(2)}, u32[]{:S(2)}) collective-permute-start(bf16[32,1152]{1,0:T(8,128)(2,1)S(1)} %bitcast.65), channel_id=1, source_target_pairs={{0,256},{128,384},{256,512},{384,640},{512,768},{640,896},{768,4},... | collective-permute-start | bytes 221192 | tf_op jit(solution)/shard_map/gather_others/ppermute | solution.py:39
  71.3 4.2 %collective-permute-done.5 = bf16[32,1152]{1,0:T(8,128)(2,1)S(1)} collective-permute-done((bf16[32,1152]{1,0:T(8,128)(2,1)S(1)}, bf16[32,1152]{1,0:T(8,128)(2,1)S(1)}, u32[]{:S(2)}, u32[]{:S(2)}) %collective-permute-start.5) | collective-permute-done | bytes 73760 | tf_op jit(solution)/shard_map/gather_others/ppermute | solution.py:39
  75.5 2.2 %collective-permute-start.6 = (bf16[128,1152]{1,0:T(8,128)(2,1)S(1)}, bf16[128,1152]{1,0:T(8,128)(2,1)S(1)}, u32[]{:S(2)}, u32[]{:S(2)}) collective-permute-start(bf16[128,1152]{1,0:T(8,128)(2,1)S(1)} %pad_maximum_fusion.1.refs_0_), channel_id=1, source_target_pairs={{0,1},{1,2},{2,3},{3,0},{4,5},{5,6},{6,7},{7,4},{8,9},{9,10},{10,1... | collective-permute-start | bytes 884744 | tf_op jit(solution)/shard_map/gather_others/ppermute | solution.py:32
  77.7 4.3 %collective-permute-start.7 = (bf16[128,1152]{1,0:T(8,128)(2,1)S(1)}, bf16[128,1152]{1,0:T(8,128)(2,1)S(1)}, u32[]{:S(2)}, u32[]{:S(2)}) collective-permute-start(bf16[128,1152]{1,0:T(8,128)(2,1)S(1)} %pad_maximum_fusion.1.refs_0_), channel_id=1, source_target_pairs={{0,3},{1,0},{2,1},{3,2},{4,7},{5,4},{6,5},{7,6},{8,11},{9,8},{10,9... | collective-permute-start | bytes 884744 | tf_op jit(solution)/shard_map/gather_others/ppermute | solution.py:32
  82.0 1.9 %collective-permute-start.8 = (bf16[128,1152]{1,0:T(8,128)(2,1)S(1)}, bf16[128,1152]{1,0:T(8,128)(2,1)S(1)}, u32[]{:S(2)}, u32[]{:S(2)}) collective-permute-start(bf16[128,1152]{1,0:T(8,128)(2,1)S(1)} %pad_maximum_fusion.1.refs_0_), channel_id=1, source_target_pairs={{0,2},{1,3},{2,0},{3,1},{4,6},{5,7},{6,4},{7,5},{8,10},{9,11},{10,... | collective-permute-start | bytes 884744 | tf_op jit(solution)/shard_map/gather_others/ppermute | solution.py:32
  83.9 7.1 %collective-permute-start.1 = (bf16[128,1152]{1,0:T(8,128)(2,1)S(1)}, bf16[128,1152]{1,0:T(8,128)(2,1)S(1)}, u32[]{:S(2)}, u32[]{:S(2)}) collective-permute-start(bf16[128,1152]{1,0:T(8,128)(2,1)S(1)} %bitcast.49), channel_id=1, source_target_pairs={{0,8},{8,0},{1,9},{9,1},{2,10},{10,2},{3,11},{11,3},{4,12},{12,4},... | collective-permute-start | bytes 884744 | tf_op jit(solution)/shard_map/gather_own/ppermute | solution.py:32
  92.2 1.6 pairs.1
  93.8 7.0 %collective-permute-start.9 = (f32[128,1152]{1,0:T(8,128)S(1)}, f32[128,1152]{1,0:T(8,128)S(1)}, u32[]{:S(2)}, u32[]{:S(2)}) collective-permute-start(f32[128,1152]{1,0:T(8,128)S(1)} %get-tuple-element.7), channel_id=1, source_target_pairs={{0,8},{8,0},{1,9},{9,1},{2,10},{10,2},{3,11},{11,3},{4,12},{12,4},... | collective-permute-start | bytes 1769480 | tf_op jit(solution)/shard_map/reduce_pairs/ppermute | solution.py:32
  100.8 1.6 collective-permute-done.9
  103.2 5.6 %all-to-all-start.2 = ((bf16[8,16,1152]{2,1,0:T(8,128)(2,1)}), bf16[8,16,1152]{2,1,0:T(8,128)(2,1)S(1)}, u32[]{:S(2)}, u32[]{:S(2)}) async-start(bf16[8,16,1152]{2,1,0:T(8,128)(2,1)} %bitcast.14), calls=%async_computation.2 | async-start | bytes 589824 | tf_op jit(solution)/shard_map/reduce_pairs/all_to_all | solution.py:23
  108.9 12.3 %all-to-all-done.2 = bf16[8,16,1152]{2,1,0:T(8,128)(2,1)S(1)} async-done(((bf16[8,16,1152]{2,1,0:T(8,128)(2,1)}), bf16[8,16,1152]{2,1,0:T(8,128)(2,1)S(1)}, u32[]{:S(2)}, u32[]{:S(2)}) %all-to-all-start.2) | async-done | bytes 294944 | tf_op jit(solution)/shard_map/reduce_pairs/all_to_all | solution.py:23
  121.4 9.5 %collective-permute-start.10 = (bf16[16,1152]{1,0:T(8,128)(2,1)S(1)}, bf16[16,1152]{1,0:T(8,128)(2,1)S(1)}, u32[]{:S(2)}, u32[]{:S(2)}) collective-permute-start(bf16[16,1152]{1,0:T(8,128)(2,1)S(1)} %fusion.15), channel_id=1, source_target_pairs={{0,4},{4,0},{1,5},{5,1},{2,6},{6,2},{3,7},{7,3},{8,12},{12,8},{9,1... | collective-permute-start | bytes 110600 | tf_op jit(solution)/shard_map/back/ppermute | solution.py:32
  130.9 3.9 %collective-permute-done.10 = bf16[16,1152]{1,0:T(8,128)(2,1)S(1)} collective-permute-done((bf16[16,1152]{1,0:T(8,128)(2,1)S(1)}, bf16[16,1152]{1,0:T(8,128)(2,1)S(1)}, u32[]{:S(2)}, u32[]{:S(2)}) %collective-permute-start.10) | collective-permute-done | bytes 36896 | tf_op jit(solution)/shard_map/back/ppermute | solution.py:32
  135.6 4.6 %all-to-all-start.3 = ((bf16[4,32,1152]{2,1,0:T(8,128)(2,1)}), bf16[4,32,1152]{2,1,0:T(8,128)(2,1)S(1)}, u32[]{:S(2)}, u32[]{:S(2)}) async-start(bf16[4,32,1152]{2,1,0:T(8,128)(2,1)} %broadcast_in_dim.43), calls=%async_computation.3 | async-start | bytes 589824 | tf_op jit(solution)/shard_map/back/all_to_all | solution.py:23
  140.6 5.4 %all-to-all-done.3 = bf16[4,32,1152]{2,1,0:T(8,128)(2,1)S(1)} async-done(((bf16[4,32,1152]{2,1,0:T(8,128)(2,1)}), bf16[4,32,1152]{2,1,0:T(8,128)(2,1)S(1)}, u32[]{:S(2)}, u32[]{:S(2)}) %all-to-all-start.3) | async-done | bytes 294944 | tf_op jit(solution)/shard_map/back/all_to_all | solution.py:23
  146.0 1.4 fusion.3
  147.6 5.6 %collective-permute-start.11 = (f32[576,288]{0,1:T(8,128)S(1)}, f32[576,288]{0,1:T(8,128)S(1)}, u32[]{:S(2)}, u32[]{:S(2)}) collective-permute-start(f32[576,288]{0,1:T(8,128)S(1)} %slice.43), channel_id=1, source_target_pairs={{0,8},{8,0},{1,9},{9,1},{2,10},{10,2},{3,11},{11,3},{4,12},{12,4},... | collective-permute-start | bytes 1990664 | tf_op jit(solution)/shard_map/weight_grad/ppermute | solution.py:32
  153.2 1.8 collective-permute-done.11
  155.6 1.5 reshape.207
  157.1 7.6 %all-to-all-start.4 = ((bf16[64,2,1296]{2,1,0:T(2,128)(2,1)}), bf16[64,2,1296]{2,1,0:T(2,128)(2,1)S(1)}, u32[]{:S(2)}, u32[]{:S(2)}) async-start(bf16[64,2,1296]{2,1,0:T(2,128)(2,1)} %reshape.207), calls=%async_computation.4 | async-start | bytes 720896 | tf_op jit(solution)/shard_map/weight_grad/all_to_all | solution.py:23
  165.9 22.7 %all-to-all-done.4 = bf16[64,2,1296]{2,1,0:T(2,128)(2,1)S(1)} async-done(((bf16[64,2,1296]{2,1,0:T(2,128)(2,1)}), bf16[64,2,1296]{2,1,0:T(2,128)(2,1)S(1)}, u32[]{:S(2)}, u32[]{:S(2)}) %all-to-all-start.4) | async-done | bytes 331808 | tf_op jit(solution)/shard_map/weight_grad/all_to_all | solution.py:23
  (66 shorter events, 9.0 us)
Async XLA Ops:
  3.7 10.5 %all-to-all-start = ((bf16[4,32,1152]{2,1,0:T(8,128)(2,1)}), bf16[4,32,1152]{2,1,0:T(8,128)(2,1)S(1)}, u32[]{:S(2)}, u32[]{:S(2)}) async-start(bf16[4,32,1152]{2,1,0:T(8,128)(2,1)} %pad_maximum_fusion), calls=%async_computation | async-start | bytes 589824 | tf_op jit(solution)/shard_map/embed/all_to_all | solution.py:23
  14.3 22.0 %collective-permute-start = (f32[32,1152]{1,0:T(8,128)S(1)}, f32[32,1152]{1,0:T(8,128)S(1)}, u32[]{:S(2)}, u32[]{:S(2)}) collective-permute-start(f32[32,1152]{1,0:T(8,128)S(1)} %convert_reduce_fusion.2), channel_id=1, source_target_pairs={{0,4},{4,0},{1,5},{5,1},{2,6},{6,2},{3,7},{7,3},{8,12},{12,8},{9,1... | collective-permute-start | bytes 442376 | tf_op jit(solution)/shard_map/embed/ppermute | solution.py:32
  36.6 21.6 %collective-permute-start.2 = (bf16[32,1152]{1,0:T(8,128)(2,1)S(1)}, bf16[32,1152]{1,0:T(8,128)(2,1)S(1)}, u32[]{:S(2)}, u32[]{:S(2)}) collective-permute-start(bf16[32,1152]{1,0:T(8,128)(2,1)S(1)} %get-tuple-element.11), channel_id=1, source_target_pairs={{0,512},{128,640},{256,768},{384,896},{512,4},{640,132},{768,260},... | collective-permute-start | bytes 221192 | tf_op jit(solution)/shard_map/gather_others/ppermute | solution.py:39
  48.1 35.7 %all-to-all-start.1 = ((bf16[8,16,1152]{2,1,0:T(8,128)(2,1)}), bf16[8,16,1152]{2,1,0:T(8,128)(2,1)S(1)}, u32[]{:S(2)}, u32[]{:S(2)}) async-start(bf16[8,16,1152]{2,1,0:T(8,128)(2,1)} %broadcast_in_dim.42), calls=%async_computation.1 | async-start | bytes 589824 | tf_op jit(solution)/shard_map/gather_own/all_to_all | solution.py:23
  58.2 13.0 %collective-permute-start.3 = (bf16[32,1152]{1,0:T(8,128)(2,1)S(1)}, bf16[32,1152]{1,0:T(8,128)(2,1)S(1)}, u32[]{:S(2)}, u32[]{:S(2)}) collective-permute-start(bf16[32,1152]{1,0:T(8,128)(2,1)S(1)} %bitcast.67), channel_id=1, source_target_pairs={{0,128},{128,256},{256,384},{384,512},{512,640},{640,768},{768,896... | collective-permute-start | bytes 221192 | tf_op jit(solution)/shard_map/gather_others/ppermute | solution.py:39
  60.1 11.1 %collective-permute-start.4 = (bf16[32,1152]{1,0:T(8,128)(2,1)S(1)}, bf16[32,1152]{1,0:T(8,128)(2,1)S(1)}, u32[]{:S(2)}, u32[]{:S(2)}) collective-permute-start(bf16[32,1152]{1,0:T(8,128)(2,1)S(1)} %bitcast.66), channel_id=1, source_target_pairs={{0,900},{128,0},{256,128},{384,256},{512,384},{640,512},{768,640},... | collective-permute-start | bytes 221192 | tf_op jit(solution)/shard_map/gather_others/ppermute | solution.py:39
  64.7 10.7 %collective-permute-start.5 = (bf16[32,1152]{1,0:T(8,128)(2,1)S(1)}, bf16[32,1152]{1,0:T(8,128)(2,1)S(1)}, u32[]{:S(2)}, u32[]{:S(2)}) collective-permute-start(bf16[32,1152]{1,0:T(8,128)(2,1)S(1)} %bitcast.65), channel_id=1, source_target_pairs={{0,256},{128,384},{256,512},{384,640},{512,768},{640,896},{768,4},... | collective-permute-start | bytes 221192 | tf_op jit(solution)/shard_map/gather_others/ppermute | solution.py:39
  75.5 15.8 %collective-permute-start.6 = (bf16[128,1152]{1,0:T(8,128)(2,1)S(1)}, bf16[128,1152]{1,0:T(8,128)(2,1)S(1)}, u32[]{:S(2)}, u32[]{:S(2)}) collective-permute-start(bf16[128,1152]{1,0:T(8,128)(2,1)S(1)} %pad_maximum_fusion.1.refs_0_), channel_id=1, source_target_pairs={{0,1},{1,2},{2,3},{3,0},{4,5},{5,6},{6,7},{7,4},{8,9},{9,10},{10,1... | collective-permute-start | bytes 884744 | tf_op jit(solution)/shard_map/gather_others/ppermute | solution.py:32
  77.7 13.6 %collective-permute-start.7 = (bf16[128,1152]{1,0:T(8,128)(2,1)S(1)}, bf16[128,1152]{1,0:T(8,128)(2,1)S(1)}, u32[]{:S(2)}, u32[]{:S(2)}) collective-permute-start(bf16[128,1152]{1,0:T(8,128)(2,1)S(1)} %pad_maximum_fusion.1.refs_0_), channel_id=1, source_target_pairs={{0,3},{1,0},{2,1},{3,2},{4,7},{5,4},{6,5},{7,6},{8,11},{9,8},{10,9... | collective-permute-start | bytes 884744 | tf_op jit(solution)/shard_map/gather_others/ppermute | solution.py:32
  82.0 9.9 %collective-permute-start.8 = (bf16[128,1152]{1,0:T(8,128)(2,1)S(1)}, bf16[128,1152]{1,0:T(8,128)(2,1)S(1)}, u32[]{:S(2)}, u32[]{:S(2)}) collective-permute-start(bf16[128,1152]{1,0:T(8,128)(2,1)S(1)} %pad_maximum_fusion.1.refs_0_), channel_id=1, source_target_pairs={{0,2},{1,3},{2,0},{3,1},{4,6},{5,7},{6,4},{7,5},{8,10},{9,11},{10,... | collective-permute-start | bytes 884744 | tf_op jit(solution)/shard_map/gather_others/ppermute | solution.py:32
  83.9 8.3 %collective-permute-start.1 = (bf16[128,1152]{1,0:T(8,128)(2,1)S(1)}, bf16[128,1152]{1,0:T(8,128)(2,1)S(1)}, u32[]{:S(2)}, u32[]{:S(2)}) collective-permute-start(bf16[128,1152]{1,0:T(8,128)(2,1)S(1)} %bitcast.49), channel_id=1, source_target_pairs={{0,8},{8,0},{1,9},{9,1},{2,10},{10,2},{3,11},{11,3},{4,12},{12,4},... | collective-permute-start | bytes 884744 | tf_op jit(solution)/shard_map/gather_own/ppermute | solution.py:32
  93.8 8.6 %collective-permute-start.9 = (f32[128,1152]{1,0:T(8,128)S(1)}, f32[128,1152]{1,0:T(8,128)S(1)}, u32[]{:S(2)}, u32[]{:S(2)}) collective-permute-start(f32[128,1152]{1,0:T(8,128)S(1)} %get-tuple-element.7), channel_id=1, source_target_pairs={{0,8},{8,0},{1,9},{9,1},{2,10},{10,2},{3,11},{11,3},{4,12},{12,4},... | collective-permute-start | bytes 1769480 | tf_op jit(solution)/shard_map/reduce_pairs/ppermute | solution.py:32
  103.2 37.3 %copy-start.2 = (bf16[64,144]{1,0:T(8,128)(2,1)S(1)}, bf16[64,144]{1,0:T(8,128)(2,1)}, u32[]{:S(2)}) copy-start(bf16[64,144]{1,0:T(8,128)(2,1)} %param.7) | copy-start | bytes 55300
  103.2 37.3 %copy-start.3 = (bf16[64,144]{1,0:T(8,128)(2,1)S(1)}, bf16[64,144]{1,0:T(8,128)(2,1)}, u32[]{:S(2)}) copy-start(bf16[64,144]{1,0:T(8,128)(2,1)} %param.6) | copy-start | bytes 55300
  103.2 18.0 %all-to-all-start.2 = ((bf16[8,16,1152]{2,1,0:T(8,128)(2,1)}), bf16[8,16,1152]{2,1,0:T(8,128)(2,1)S(1)}, u32[]{:S(2)}, u32[]{:S(2)}) async-start(bf16[8,16,1152]{2,1,0:T(8,128)(2,1)} %bitcast.14), calls=%async_computation.2 | async-start | bytes 589824 | tf_op jit(solution)/shard_map/reduce_pairs/all_to_all | solution.py:23
  121.4 13.4 %collective-permute-start.10 = (bf16[16,1152]{1,0:T(8,128)(2,1)S(1)}, bf16[16,1152]{1,0:T(8,128)(2,1)S(1)}, u32[]{:S(2)}, u32[]{:S(2)}) collective-permute-start(bf16[16,1152]{1,0:T(8,128)(2,1)S(1)} %fusion.15), channel_id=1, source_target_pairs={{0,4},{4,0},{1,5},{5,1},{2,6},{6,2},{3,7},{7,3},{8,12},{12,8},{9,1... | collective-permute-start | bytes 110600 | tf_op jit(solution)/shard_map/back/ppermute | solution.py:32
  135.6 10.3 %all-to-all-start.3 = ((bf16[4,32,1152]{2,1,0:T(8,128)(2,1)}), bf16[4,32,1152]{2,1,0:T(8,128)(2,1)S(1)}, u32[]{:S(2)}, u32[]{:S(2)}) async-start(bf16[4,32,1152]{2,1,0:T(8,128)(2,1)} %broadcast_in_dim.43), calls=%async_computation.3 | async-start | bytes 589824 | tf_op jit(solution)/shard_map/back/all_to_all | solution.py:23
  147.6 7.4 %collective-permute-start.11 = (f32[576,288]{0,1:T(8,128)S(1)}, f32[576,288]{0,1:T(8,128)S(1)}, u32[]{:S(2)}, u32[]{:S(2)}) collective-permute-start(f32[576,288]{0,1:T(8,128)S(1)} %slice.43), channel_id=1, source_target_pairs={{0,8},{8,0},{1,9},{9,1},{2,10},{10,2},{3,11},{11,3},{4,12},{12,4},... | collective-permute-start | bytes 1990664 | tf_op jit(solution)/shard_map/weight_grad/ppermute | solution.py:32
  155.4 9.4 %copy-start = (bf16[144,1152]{1,0:T(8,128)(2,1)S(1)}, bf16[144,1152]{1,0:T(8,128)(2,1)}, u32[]{:S(2)}) copy-start(bf16[144,1152]{1,0:T(8,128)(2,1)} %param.9) | copy-start | bytes 995332
  155.4 9.4 %copy-start.1 = (bf16[144,1152]{1,0:T(8,128)(2,1)S(1)}, bf16[144,1152]{1,0:T(8,128)(2,1)}, u32[]{:S(2)}) copy-start(bf16[144,1152]{1,0:T(8,128)(2,1)} %param.8) | copy-start | bytes 995332
  157.1 31.5 %all-to-all-start.4 = ((bf16[64,2,1296]{2,1,0:T(2,128)(2,1)}), bf16[64,2,1296]{2,1,0:T(2,128)(2,1)S(1)}, u32[]{:S(2)}, u32[]{:S(2)}) async-start(bf16[64,2,1296]{2,1,0:T(2,128)(2,1)} %reshape.207), calls=%async_computation.4 | async-start | bytes 720896 | tf_op jit(solution)/shard_map/weight_grad/all_to_all | solution.py:23

commit v9 on v8

--- a/solution.py
+++ b/solution.py
@@ -93,11 +93,12 @@
         ]
         parts = exchange(jnp.concatenate(parts, axis=1), "x")
         embed = jnp.sum(parts.astype(F32), axis=0)
-        embed = embed + shifted(embed, "zh", 1)
-        inverse = lax.rsqrt(jnp.sum(embed * embed, axis=-1, keepdims=True) + EPS)
-        unit = embed * inverse
-        vec = unit.astype(BF16)
-        kinds = vec.reshape(2, own, width)
+        other_half, below, above = along_z(embed, 8), along_z(embed, 4), along_z(embed, -4)
+        embeds = jnp.concatenate([embed + other_half, below + above])
+        inverse = lax.rsqrt(jnp.sum(embeds * embeds, axis=-1, keepdims=True) + EPS)
+        unit = embeds * inverse
+        pair = unit.astype(BF16).reshape(2, 2, own, width)
+        unit, inverse, kinds = unit[: 2 * own], inverse[: 2 * own], pair[0]
 
     with jax.named_scope("gather_own"):
         own_vec = lax.dynamic_index_in_dim(kinds, zh, 0, keepdims=False)
@@ -105,8 +106,7 @@
         theirs = shifted(mine, "c", 1)
 
     with jax.named_scope("gather_others"):
-        pair = jnp.stack([kinds, along_z(vec, 4).reshape(2, own, width)], axis=1)
-        pair = pair.reshape(2, 2 * own, width)
+        pair = pair.transpose(1, 0, 2, 3).reshape(2, 2 * own, width)
         at = zh * SIZES["zl"] + zl
         column = []
         for by in (0, 1, -1, 2):

time: 191 us -> 200 us (1.047)
  waiting for transfers between devices: 61.4 us -> 84.9 us
  starting transfers between devices: 112 us -> 96.4 us
    ppermute x8 -> x7, starting transfers between devices: 56.8 us -> 30.7 us  [shifted(): lax.ppermute(value, axis, [(i, (i + by) % size) for i in range(size)])]
    ppermute x4 -> x6, waiting for transfers between devices: 5.78 us -> 26 us  [along_z(): return lax.ppermute(value, ('zl', 'zh'), pairs)]
    ppermute x4 -> x6, starting transfers between devices: 23.8 us -> 35.6 us  [along_z(): return lax.ppermute(value, ('zl', 'zh'), pairs)]
    ppermute x8 -> x7, waiting for transfers between devices: 9.6 us -> 13 us  [shifted(): lax.ppermute(value, axis, [(i, (i + by) % size) for i in range(size)])]
  transfers between devices with their start and end apart: 17 -> 18, of which waited for: 12 -> 12; matrix products, arithmetic and copies ran while one was open for 1% -> 1% of each run, Pallas kernels for 0% -> 0%
where the time goes in v9:
time: 200 us; the launch traced here: 199 us
  starting transfers between devices  96.4 us (48%)
  waiting for transfers between devices  84.9 us (42%)
  local copies, waits for them, and re-layouts  6.6 us (3%)
  matrix products  4.14 us (2%)
  other arithmetic  2.79 us (1%)
  between operations  2.56 us (1%)
    all_to_all x5, waiting for transfers between devices, exchange(): return lax.all_to_all(blocks, axes, 0, 0, tiled=True)  45.9 us
    ppermute x6, starting transfers between devices, along_z(): return lax.ppermute(value, ('zl', 'zh'), pairs)  35.6 us
    ppermute x7, starting transfers between devices, shifted(): lax.ppermute(value, axis, [(i, (i + by) % size) for i in range(size)])  30.7 us
    all_to_all x5, starting transfers between devices, exchange(): return lax.all_to_all(blocks, axes, 0, 0, tiled=True)  30.1 us
    ppermute x6, waiting for transfers between devices, along_z(): return lax.ppermute(value, ('zl', 'zh'), pairs)  26 us
    ppermute x7, waiting for transfers between devices, shifted(): lax.ppermute(value, axis, [(i, (i + by) % size) for i in range(size)])  13 us
    dot_general x4, matrix products, dot(): return lax.dot_general(a, b, (dims, ((), ())), preferred_element_type=F32)  4.14 us
  transfers between devices with their start and end apart: 18, of which 12 were waited for; matrix products, arithmetic and copies ran while one was open for 1% of the time, Pallas kernels for 0%

profile of v9, /device:TPU:1, one launch (start us, length us, event | category | flops | bytes accessed | tf_op | source)
XLA Modules:
  0.0 199.0 jit_solution(13533583546360461049)
XLA Ops:
  3.7 4.8 %all-to-all-start = ((bf16[4,32,1152]{2,1,0:T(8,128)(2,1)}), bf16[4,32,1152]{2,1,0:T(8,128)(2,1)S(1)}, u32[]{:S(2)}, u32[]{:S(2)}) async-start(bf16[4,32,1152]{2,1,0:T(8,128)(2,1)} %pad_maximum_fusion), calls=%async_computation | async-start | bytes 589824 | tf_op jit(solution)/shard_map/embed/all_to_all | solution.py:23
  8.7 5.5 %all-to-all-done = bf16[4,32,1152]{2,1,0:T(8,128)(2,1)S(1)} async-done(((bf16[4,32,1152]{2,1,0:T(8,128)(2,1)}), bf16[4,32,1152]{2,1,0:T(8,128)(2,1)S(1)}, u32[]{:S(2)}, u32[]{:S(2)}) %all-to-all-start) | async-done | bytes 294944 | tf_op jit(solution)/shard_map/embed/all_to_all | solution.py:23
  14.3 18.0 %collective-permute-start.2 = (f32[32,1152]{1,0:T(8,128)S(1)}, f32[32,1152]{1,0:T(8,128)S(1)}, u32[]{:S(2)}, u32[]{:S(2)}) collective-permute-start(f32[32,1152]{1,0:T(8,128)S(1)} %convert_reduce_fusion.2), channel_id=1, source_target_pairs={{0,516},{128,644},{256,772},{384,900},{512,0},{640,128},{768,256},... | collective-permute-start | bytes 442376 | tf_op jit(solution)/shard_map/embed/ppermute | solution.py:39
  32.3 1.9 collective-permute-start.1
  34.3 8.4 %collective-permute-start = (f32[32,1152]{1,0:T(8,128)S(1)}, f32[32,1152]{1,0:T(8,128)S(1)}, u32[]{:S(2)}, u32[]{:S(2)}) collective-permute-start(f32[32,1152]{1,0:T(8,128)S(1)} %convert_reduce_fusion.2), channel_id=1, source_target_pairs={{0,4},{128,132},{256,260},{384,388},{512,516},{640,644},{768,772},... | collective-permute-start | bytes 442376 | tf_op jit(solution)/shard_map/embed/ppermute | solution.py:39
  44.3 20.4 %collective-permute-done = f32[32,1152]{1,0:T(8,128)S(1)} collective-permute-done((f32[32,1152]{1,0:T(8,128)S(1)}, f32[32,1152]{1,0:T(8,128)S(1)}, u32[]{:S(2)}, u32[]{:S(2)}) %collective-permute-start) | collective-permute-done | bytes 147488 | tf_op jit(solution)/shard_map/embed/ppermute | solution.py:39
  65.8 6.9 %all-to-all-start.1 = ((bf16[8,16,1152]{2,1,0:T(8,128)(2,1)}), bf16[8,16,1152]{2,1,0:T(8,128)(2,1)S(1)}, u32[]{:S(2)}, u32[]{:S(2)}) async-start(bf16[8,16,1152]{2,1,0:T(8,128)(2,1)} %broadcast_in_dim.42), calls=%async_computation.1 | async-start | bytes 589824 | tf_op jit(solution)/shard_map/gather_own/all_to_all | solution.py:23
  72.9 1.9 collective-permute-start.5
  74.8 1.9 collective-permute-start.6
  76.7 3.4 %collective-permute-start.4 = (bf16[32,1152]{1,0:T(8,128)(2,1)S(1)}, bf16[32,1152]{1,0:T(8,128)(2,1)S(1)}, u32[]{:S(2)}, u32[]{:S(2)}) collective-permute-start(bf16[32,1152]{1,0:T(8,128)(2,1)S(1)} %bitcast.67), channel_id=1, source_target_pairs={{0,128},{128,256},{256,384},{384,512},{512,640},{640,768},{768,896... | collective-permute-start | bytes 221192 | tf_op jit(solution)/shard_map/gather_others/ppermute | solution.py:39
  80.1 2.1 %collective-permute-done.6 = bf16[32,1152]{1,0:T(8,128)(2,1)S(1)} collective-permute-done((bf16[32,1152]{1,0:T(8,128)(2,1)S(1)}, bf16[32,1152]{1,0:T(8,128)(2,1)S(1)}, u32[]{:S(2)}, u32[]{:S(2)}) %collective-permute-start.6) | collective-permute-done | bytes 73760 | tf_op jit(solution)/shard_map/gather_others/ppermute | solution.py:39
  82.2 3.5 %collective-permute-done.4 = bf16[32,1152]{1,0:T(8,128)(2,1)S(1)} collective-permute-done((bf16[32,1152]{1,0:T(8,128)(2,1)S(1)}, bf16[32,1152]{1,0:T(8,128)(2,1)S(1)}, u32[]{:S(2)}, u32[]{:S(2)}) %collective-permute-start.4) | collective-permute-done | bytes 73760 | tf_op jit(solution)/shard_map/gather_others/ppermute | solution.py:39
  85.8 2.2 %collective-permute-start.9 = (bf16[128,1152]{1,0:T(8,128)(2,1)S(1)}, bf16[128,1152]{1,0:T(8,128)(2,1)S(1)}, u32[]{:S(2)}, u32[]{:S(2)}) collective-permute-start(bf16[128,1152]{1,0:T(8,128)(2,1)S(1)} %pad_maximum_fusion.2.refs_0_), channel_id=1, source_target_pairs={{0,2},{1,3},{2,0},{3,1},{4,6},{5,7},{6,4},{7,5},{8,10},{9,11},{10,... | collective-permute-start | bytes 884744 | tf_op jit(solution)/shard_map/gather_others/ppermute | solution.py:32
  88.0 4.3 %collective-permute-start.8 = (bf16[128,1152]{1,0:T(8,128)(2,1)S(1)}, bf16[128,1152]{1,0:T(8,128)(2,1)S(1)}, u32[]{:S(2)}, u32[]{:S(2)}) collective-permute-start(bf16[128,1152]{1,0:T(8,128)(2,1)S(1)} %pad_maximum_fusion.2.refs_0_), channel_id=1, source_target_pairs={{0,3},{1,0},{2,1},{3,2},{4,7},{5,4},{6,5},{7,6},{8,11},{9,8},{10,9... | collective-permute-start | bytes 884744 | tf_op jit(solution)/shard_map/gather_others/ppermute | solution.py:32
  92.3 1.9 collective-permute-start.7
  94.2 3.8 %collective-permute-start.3 = (bf16[128,1152]{1,0:T(8,128)(2,1)S(1)}, bf16[128,1152]{1,0:T(8,128)(2,1)S(1)}, u32[]{:S(2)}, u32[]{:S(2)}) collective-permute-start(bf16[128,1152]{1,0:T(8,128)(2,1)S(1)} %bitcast.51), channel_id=1, source_target_pairs={{0,8},{8,0},{1,9},{9,1},{2,10},{10,2},{3,11},{11,3},{4,12},{12,4},... | collective-permute-start | bytes 884744 | tf_op jit(solution)/shard_map/gather_own/ppermute | solution.py:32
  98.2 3.2 %collective-permute-done.8.refs_2_ = bf16[128,1152]{1,0:T(8,128)(2,1)S(1)} collective-permute-done((bf16[128,1152]{1,0:T(8,128)(2,1)S(1)}, bf16[128,1152]{1,0:T(8,128)(2,1)S(1)}, u32[]{:S(2)}, u32[]{:S(2)}) %collective-permute-start.8) | collective-permute-done | bytes 294944 | tf_op jit(solution)/shard_map/gather_others/ppermute | solution.py:32
  101.4 1.6 collective-permute-done.7.refs_1_
  103.1 1.5 pairs.1
  104.6 4.2 %collective-permute-start.10 = (f32[128,1152]{1,0:T(8,128)S(1)}, f32[128,1152]{1,0:T(8,128)S(1)}, u32[]{:S(2)}, u32[]{:S(2)}) collective-permute-start(f32[128,1152]{1,0:T(8,128)S(1)} %get-tuple-element.7), channel_id=1, source_target_pairs={{0,8},{8,0},{1,9},{9,1},{2,10},{10,2},{3,11},{11,3},{4,12},{12,4},... | collective-permute-start | bytes 1769480 | tf_op jit(solution)/shard_map/reduce_pairs/ppermute | solution.py:32
  108.8 1.6 collective-permute-done.10
  111.2 6.6 %all-to-all-start.2 = ((bf16[8,16,1152]{2,1,0:T(8,128)(2,1)}), bf16[8,16,1152]{2,1,0:T(8,128)(2,1)S(1)}, u32[]{:S(2)}, u32[]{:S(2)}) async-start(bf16[8,16,1152]{2,1,0:T(8,128)(2,1)} %bitcast.14), calls=%async_computation.2 | async-start | bytes 589824 | tf_op jit(solution)/shard_map/reduce_pairs/all_to_all | solution.py:23
  117.9 12.3 %all-to-all-done.2 = bf16[8,16,1152]{2,1,0:T(8,128)(2,1)S(1)} async-done(((bf16[8,16,1152]{2,1,0:T(8,128)(2,1)}), bf16[8,16,1152]{2,1,0:T(8,128)(2,1)S(1)}, u32[]{:S(2)}, u32[]{:S(2)}) %all-to-all-start.2) | async-done | bytes 294944 | tf_op jit(solution)/shard_map/reduce_pairs/all_to_all | solution.py:23
  130.5 9.0 %collective-permute-start.11 = (bf16[16,1152]{1,0:T(8,128)(2,1)S(1)}, bf16[16,1152]{1,0:T(8,128)(2,1)S(1)}, u32[]{:S(2)}, u32[]{:S(2)}) collective-permute-start(bf16[16,1152]{1,0:T(8,128)(2,1)S(1)} %fusion.15), channel_id=1, source_target_pairs={{0,4},{4,0},{1,5},{5,1},{2,6},{6,2},{3,7},{7,3},{8,12},{12,8},{9,1... | collective-permute-start | bytes 110600 | tf_op jit(solution)/shard_map/back/ppermute | solution.py:32
  139.4 4.7 %collective-permute-done.11 = bf16[16,1152]{1,0:T(8,128)(2,1)S(1)} collective-permute-done((bf16[16,1152]{1,0:T(8,128)(2,1)S(1)}, bf16[16,1152]{1,0:T(8,128)(2,1)S(1)}, u32[]{:S(2)}, u32[]{:S(2)}) %collective-permute-start.11) | collective-permute-done | bytes 36896 | tf_op jit(solution)/shard_map/back/ppermute | solution.py:32
  144.9 3.5 %all-to-all-start.3 = ((bf16[4,32,1152]{2,1,0:T(8,128)(2,1)}), bf16[4,32,1152]{2,1,0:T(8,128)(2,1)S(1)}, u32[]{:S(2)}, u32[]{:S(2)}) async-start(bf16[4,32,1152]{2,1,0:T(8,128)(2,1)} %broadcast_in_dim.43), calls=%async_computation.3 | async-start | bytes 589824 | tf_op jit(solution)/shard_map/back/all_to_all | solution.py:23
  148.7 5.3 %all-to-all-done.3 = bf16[4,32,1152]{2,1,0:T(8,128)(2,1)S(1)} async-done(((bf16[4,32,1152]{2,1,0:T(8,128)(2,1)}), bf16[4,32,1152]{2,1,0:T(8,128)(2,1)S(1)}, u32[]{:S(2)}, u32[]{:S(2)}) %all-to-all-start.3) | async-done | bytes 294944 | tf_op jit(solution)/shard_map/back/all_to_all | solution.py:23
  155.7 5.4 %collective-permute-start.12 = (f32[576,288]{0,1:T(8,128)S(1)}, f32[576,288]{0,1:T(8,128)S(1)}, u32[]{:S(2)}, u32[]{:S(2)}) collective-permute-start(f32[576,288]{0,1:T(8,128)S(1)} %slice.59), channel_id=1, source_target_pairs={{0,8},{8,0},{1,9},{9,1},{2,10},{10,2},{3,11},{11,3},{4,12},{12,4},... | collective-permute-start | bytes 1990664 | tf_op jit(solution)/shard_map/weight_grad/ppermute | solution.py:32
  161.1 1.8 collective-permute-done.12
  163.4 1.6 reshape.206
  165.0 8.3 %all-to-all-start.4 = ((bf16[64,2,1296]{2,1,0:T(2,128)(2,1)}), bf16[64,2,1296]{2,1,0:T(2,128)(2,1)S(1)}, u32[]{:S(2)}, u32[]{:S(2)}) async-start(bf16[64,2,1296]{2,1,0:T(2,128)(2,1)} %reshape.206), calls=%async_computation.4 | async-start | bytes 720896 | tf_op jit(solution)/shard_map/weight_grad/all_to_all | solution.py:23
  174.5 22.7 %all-to-all-done.4 = bf16[64,2,1296]{2,1,0:T(2,128)(2,1)S(1)} async-done(((bf16[64,2,1296]{2,1,0:T(2,128)(2,1)}), bf16[64,2,1296]{2,1,0:T(2,128)(2,1)S(1)}, u32[]{:S(2)}, u32[]{:S(2)}) %all-to-all-start.4) | async-done | bytes 331808 | tf_op jit(solution)/shard_map/weight_grad/all_to_all | solution.py:23
  (73 shorter events, 12.0 us)
Async XLA Ops:
  3.7 10.5 %all-to-all-start = ((bf16[4,32,1152]{2,1,0:T(8,128)(2,1)}), bf16[4,32,1152]{2,1,0:T(8,128)(2,1)S(1)}, u32[]{:S(2)}, u32[]{:S(2)}) async-start(bf16[4,32,1152]{2,1,0:T(8,128)(2,1)} %pad_maximum_fusion), calls=%async_computation | async-start | bytes 589824 | tf_op jit(solution)/shard_map/embed/all_to_all | solution.py:23
  14.3 50.4 %collective-permute-start.2 = (f32[32,1152]{1,0:T(8,128)S(1)}, f32[32,1152]{1,0:T(8,128)S(1)}, u32[]{:S(2)}, u32[]{:S(2)}) collective-permute-start(f32[32,1152]{1,0:T(8,128)S(1)} %convert_reduce_fusion.2), channel_id=1, source_target_pairs={{0,516},{128,644},{256,772},{384,900},{512,0},{640,128},{768,256},... | collective-permute-start | bytes 442376 | tf_op jit(solution)/shard_map/embed/ppermute | solution.py:39
  32.3 32.4 %collective-permute-start.1 = (f32[32,1152]{1,0:T(8,128)S(1)}, f32[32,1152]{1,0:T(8,128)S(1)}, u32[]{:S(2)}, u32[]{:S(2)}) collective-permute-start(f32[32,1152]{1,0:T(8,128)S(1)} %convert_reduce_fusion.2), channel_id=1, source_target_pairs={{0,512},{128,640},{256,768},{384,896},{512,4},{640,132},{768,260},... | collective-permute-start | bytes 442376 | tf_op jit(solution)/shard_map/embed/ppermute | solution.py:39
  34.3 30.4 %collective-permute-start = (f32[32,1152]{1,0:T(8,128)S(1)}, f32[32,1152]{1,0:T(8,128)S(1)}, u32[]{:S(2)}, u32[]{:S(2)}) collective-permute-start(f32[32,1152]{1,0:T(8,128)S(1)} %convert_reduce_fusion.2), channel_id=1, source_target_pairs={{0,4},{128,132},{256,260},{384,388},{512,516},{640,644},{768,772},... | collective-permute-start | bytes 442376 | tf_op jit(solution)/shard_map/embed/ppermute | solution.py:39
  65.8 28.4 %all-to-all-start.1 = ((bf16[8,16,1152]{2,1,0:T(8,128)(2,1)}), bf16[8,16,1152]{2,1,0:T(8,128)(2,1)S(1)}, u32[]{:S(2)}, u32[]{:S(2)}) async-start(bf16[8,16,1152]{2,1,0:T(8,128)(2,1)} %broadcast_in_dim.42), calls=%async_computation.1 | async-start | bytes 589824 | tf_op jit(solution)/shard_map/gather_own/all_to_all | solution.py:23
  72.9 7.2 %collective-permute-start.5 = (bf16[32,1152]{1,0:T(8,128)(2,1)S(1)}, bf16[32,1152]{1,0:T(8,128)(2,1)S(1)}, u32[]{:S(2)}, u32[]{:S(2)}) collective-permute-start(bf16[32,1152]{1,0:T(8,128)(2,1)S(1)} %bitcast.69), channel_id=1, source_target_pairs={{0,900},{128,0},{256,128},{384,256},{512,384},{640,512},{768,640},... | collective-permute-start | bytes 221192 | tf_op jit(solution)/shard_map/gather_others/ppermute | solution.py:39
  74.8 7.4 %collective-permute-start.6 = (bf16[32,1152]{1,0:T(8,128)(2,1)S(1)}, bf16[32,1152]{1,0:T(8,128)(2,1)S(1)}, u32[]{:S(2)}, u32[]{:S(2)}) collective-permute-start(bf16[32,1152]{1,0:T(8,128)(2,1)S(1)} %bitcast.68), channel_id=1, source_target_pairs={{0,256},{128,384},{256,512},{384,640},{512,768},{640,896},{768,4},... | collective-permute-start | bytes 221192 | tf_op jit(solution)/shard_map/gather_others/ppermute | solution.py:39
  76.7 9.0 %collective-permute-start.4 = (bf16[32,1152]{1,0:T(8,128)(2,1)S(1)}, bf16[32,1152]{1,0:T(8,128)(2,1)S(1)}, u32[]{:S(2)}, u32[]{:S(2)}) collective-permute-start(bf16[32,1152]{1,0:T(8,128)(2,1)S(1)} %bitcast.67), channel_id=1, source_target_pairs={{0,128},{128,256},{256,384},{384,512},{512,640},{640,768},{768,896... | collective-permute-start | bytes 221192 | tf_op jit(solution)/shard_map/gather_others/ppermute | solution.py:39
  85.8 12.4 %collective-permute-start.9 = (bf16[128,1152]{1,0:T(8,128)(2,1)S(1)}, bf16[128,1152]{1,0:T(8,128)(2,1)S(1)}, u32[]{:S(2)}, u32[]{:S(2)}) collective-permute-start(bf16[128,1152]{1,0:T(8,128)(2,1)S(1)} %pad_maximum_fusion.2.refs_0_), channel_id=1, source_target_pairs={{0,2},{1,3},{2,0},{3,1},{4,6},{5,7},{6,4},{7,5},{8,10},{9,11},{10,... | collective-permute-start | bytes 884744 | tf_op jit(solution)/shard_map/gather_others/ppermute | solution.py:32
  88.0 13.4 %collective-permute-start.8 = (bf16[128,1152]{1,0:T(8,128)(2,1)S(1)}, bf16[128,1152]{1,0:T(8,128)(2,1)S(1)}, u32[]{:S(2)}, u32[]{:S(2)}) collective-permute-start(bf16[128,1152]{1,0:T(8,128)(2,1)S(1)} %pad_maximum_fusion.2.refs_0_), channel_id=1, source_target_pairs={{0,3},{1,0},{2,1},{3,2},{4,7},{5,4},{6,5},{7,6},{8,11},{9,8},{10,9... | collective-permute-start | bytes 884744 | tf_op jit(solution)/shard_map/gather_others/ppermute | solution.py:32
  92.3 10.8 %collective-permute-start.7 = (bf16[128,1152]{1,0:T(8,128)(2,1)S(1)}, bf16[128,1152]{1,0:T(8,128)(2,1)S(1)}, u32[]{:S(2)}, u32[]{:S(2)}) collective-permute-start(bf16[128,1152]{1,0:T(8,128)(2,1)S(1)} %pad_maximum_fusion.2.refs_0_), channel_id=1, source_target_pairs={{0,1},{1,2},{2,3},{3,0},{4,5},{5,6},{6,7},{7,4},{8,9},{9,10},{10,1... | collective-permute-start | bytes 884744 | tf_op jit(solution)/shard_map/gather_others/ppermute | solution.py:32
  94.2 8.9 %collective-permute-start.3 = (bf16[128,1152]{1,0:T(8,128)(2,1)S(1)}, bf16[128,1152]{1,0:T(8,128)(2,1)S(1)}, u32[]{:S(2)}, u32[]{:S(2)}) collective-permute-start(bf16[128,1152]{1,0:T(8,128)(2,1)S(1)} %bitcast.51), channel_id=1, source_target_pairs={{0,8},{8,0},{1,9},{9,1},{2,10},{10,2},{3,11},{11,3},{4,12},{12,4},... | collective-permute-start | bytes 884744 | tf_op jit(solution)/shard_map/gather_own/ppermute | solution.py:32
  104.6 5.8 %collective-permute-start.10 = (f32[128,1152]{1,0:T(8,128)S(1)}, f32[128,1152]{1,0:T(8,128)S(1)}, u32[]{:S(2)}, u32[]{:S(2)}) collective-permute-start(f32[128,1152]{1,0:T(8,128)S(1)} %get-tuple-element.7), channel_id=1, source_target_pairs={{0,8},{8,0},{1,9},{9,1},{2,10},{10,2},{3,11},{11,3},{4,12},{12,4},... | collective-permute-start | bytes 1769480 | tf_op jit(solution)/shard_map/reduce_pairs/ppermute | solution.py:32
  111.2 19.0 %all-to-all-start.2 = ((bf16[8,16,1152]{2,1,0:T(8,128)(2,1)}), bf16[8,16,1152]{2,1,0:T(8,128)(2,1)S(1)}, u32[]{:S(2)}, u32[]{:S(2)}) async-start(bf16[8,16,1152]{2,1,0:T(8,128)(2,1)} %bitcast.14), calls=%async_computation.2 | async-start | bytes 589824 | tf_op jit(solution)/shard_map/reduce_pairs/all_to_all | solution.py:23
  117.8 30.8 %copy-start.2 = (bf16[64,144]{1,0:T(8,128)(2,1)S(1)}, bf16[64,144]{1,0:T(8,128)(2,1)}, u32[]{:S(2)}) copy-start(bf16[64,144]{1,0:T(8,128)(2,1)} %param.7) | copy-start | bytes 55300
  117.8 30.8 %copy-start.3 = (bf16[64,144]{1,0:T(8,128)(2,1)S(1)}, bf16[64,144]{1,0:T(8,128)(2,1)}, u32[]{:S(2)}) copy-start(bf16[64,144]{1,0:T(8,128)(2,1)} %param.6) | copy-start | bytes 55300
  130.5 13.7 %collective-permute-start.11 = (bf16[16,1152]{1,0:T(8,128)(2,1)S(1)}, bf16[16,1152]{1,0:T(8,128)(2,1)S(1)}, u32[]{:S(2)}, u32[]{:S(2)}) collective-permute-start(bf16[16,1152]{1,0:T(8,128)(2,1)S(1)} %fusion.15), channel_id=1, source_target_pairs={{0,4},{4,0},{1,5},{5,1},{2,6},{6,2},{3,7},{7,3},{8,12},{12,8},{9,1... | collective-permute-start | bytes 110600 | tf_op jit(solution)/shard_map/back/ppermute | solution.py:32
  144.9 9.1 %all-to-all-start.3 = ((bf16[4,32,1152]{2,1,0:T(8,128)(2,1)}), bf16[4,32,1152]{2,1,0:T(8,128)(2,1)S(1)}, u32[]{:S(2)}, u32[]{:S(2)}) async-start(bf16[4,32,1152]{2,1,0:T(8,128)(2,1)} %broadcast_in_dim.43), calls=%async_computation.3 | async-start | bytes 589824 | tf_op jit(solution)/shard_map/back/all_to_all | solution.py:23
  155.7 7.2 %collective-permute-start.12 = (f32[576,288]{0,1:T(8,128)S(1)}, f32[576,288]{0,1:T(8,128)S(1)}, u32[]{:S(2)}, u32[]{:S(2)}) collective-permute-start(f32[576,288]{0,1:T(8,128)S(1)} %slice.59), channel_id=1, source_target_pairs={{0,8},{8,0},{1,9},{9,1},{2,10},{10,2},{3,11},{11,3},{4,12},{12,4},... | collective-permute-start | bytes 1990664 | tf_op jit(solution)/shard_map/weight_grad/ppermute | solution.py:32
  163.2 10.1 %copy-start = (bf16[144,1152]{1,0:T(8,128)(2,1)S(1)}, bf16[144,1152]{1,0:T(8,128)(2,1)}, u32[]{:S(2)}) copy-start(bf16[144,1152]{1,0:T(8,128)(2,1)} %param.9) | copy-start | bytes 995332
  163.2 10.1 %copy-start.1 = (bf16[144,1152]{1,0:T(8,128)(2,1)S(1)}, bf16[144,1152]{1,0:T(8,128)(2,1)}, u32[]{:S(2)}) copy-start(bf16[144,1152]{1,0:T(8,128)(2,1)} %param.8) | copy-start | bytes 995332
  165.0 32.2 %all-to-all-start.4 = ((bf16[64,2,1296]{2,1,0:T(2,128)(2,1)}), bf16[64,2,1296]{2,1,0:T(2,128)(2,1)S(1)}, u32[]{:S(2)}, u32[]{:S(2)}) async-start(bf16[64,2,1296]{2,1,0:T(2,128)(2,1)} %reshape.206), calls=%async_computation.4 | async-start | bytes 720896 | tf_op jit(solution)/shard_map/weight_grad/all_to_all | solution.py:23

commit v10 on v8

--- a/solution.py
+++ b/solution.py
@@ -146,34 +146,32 @@
         inverse = lax.dynamic_index_in_dim(inverse.reshape(2, own, 1), zh, 0, keepdims=False)
         inner = jnp.sum(unit * direction, axis=-1, keepdims=True)
         back = (inverse * (direction - unit * inner)).astype(BF16)
+        back = spread(back, "x", SIZES["x"]).reshape(-1, width)
         swapped = shifted(back, "zh", 1)
-        back = jnp.concatenate(
-            [jnp.where(zh == 0, back, swapped), jnp.where(zh == 0, swapped, back)]
-        )
-        back = spread(back, "x", SIZES["x"]).reshape(-1, width)
 
     with jax.named_scope("feature_grad"):
         weights = jnp.concatenate([image_weight, text_weight])
-        grads = dot(back, weights, ((1,), (1,))).reshape(SIZES["x"], 2, own, 2 * depth)
-        image_feature_grad = grads[:, 0, :, :depth].reshape(rows, depth)
-        text_feature_grad = grads[:, 1, :, depth:].reshape(rows, depth)
+        own_grads = dot(back, weights, ((1,), (1,)))
+        other_grads = dot(swapped, weights, ((1,), (1,)))
+        image_feature_grad = jnp.where(zh == 0, own_grads[:, :depth], other_grads[:, :depth])
+        text_feature_grad = jnp.where(zh == 0, other_grads[:, depth:], own_grads[:, depth:])
 
     with jax.named_scope("weight_grad"):
-        blank = jnp.zeros((SIZES["x"], own, depth), BF16)
-        features = jnp.concatenate(
-            [
-                jnp.concatenate([image_features.reshape(SIZES["x"], own, depth), blank], axis=2),
-                jnp.concatenate([blank, text_features.reshape(SIZES["x"], own, depth)], axis=2),
-            ],
-            axis=1,
-        ).reshape(2 * rows, 2 * depth)
+        blank = jnp.zeros((rows, depth), BF16)
+        image_block = jnp.concatenate([image_features, blank], axis=1)
+        text_block = jnp.concatenate([blank, text_features], axis=1)
+        own_block = jnp.where(zh == 0, image_block, text_block)
+        other_block = jnp.where(zh == 0, text_block, image_block)
         chips = SIZES["zl"] * SIZES["y"]
         share = width // (chips * 2)
         pc, pchip, pk = flat(2, chips, share)
         source = (pchip * 2 + jnp.where(pc == 0, c, 1 - c)) * share + pk
         order = lax.broadcasted_iota(jnp.int32, (width, width), 0) == source[None, :]
-        sorted_back = dot(back, order.astype(BF16), ((1,), (0,))).astype(BF16)
-        partial = dot(sorted_back, features, ((0,), (0,)))
+        order = order.astype(BF16)
+        partial = 0.0
+        for rows_back, block in ((back, own_block), (swapped, other_block)):
+            sorted_back = dot(rows_back, order, ((1,), (0,))).astype(BF16)
+            partial = partial + dot(sorted_back, block, ((0,), (0,)))
         partial = partial[: width // 2] + shifted(partial[width // 2 :], "c", 1)
         partial = exchange(partial.astype(BF16).reshape(chips, share, 2 * depth), ("zl", "y"))
         total = jnp.sum(partial.astype(F32), axis=0).T

time: 191 us -> 198 us (1.037)
  starting transfers between devices: 112 us -> 116 us
    ppermute x8, starting transfers between devices: 56.8 us -> 59.3 us  [shifted(): lax.ppermute(value, axis, [(i, (i + by) % size) for i in range(size)])]
    ppermute x8, waiting for transfers between devices: 9.6 us -> 11.9 us  [shifted(): lax.ppermute(value, axis, [(i, (i + by) % size) for i in range(size)])]
    dot_general x4 -> x6, matrix products: 4.15 us -> 5.77 us  [dot(): return lax.dot_general(a, b, (dims, ((), ())), preferred_element_type=F32)]
  transfers between devices with their start and end apart: 17 -> 17, of which waited for: 12 -> 12; matrix products, arithmetic and copies ran while one was open for 1% -> 2% of each run, Pallas kernels for 0% -> 0%
where the time goes in v10:
time: 198 us; the launch traced here: 197 us
  starting transfers between devices  116 us (59%)
  waiting for transfers between devices  62.7 us (32%)
  local copies, waits for them, and re-layouts  5.78 us (3%)
  matrix products  5.77 us (3%)
  other arithmetic  3.32 us (2%)
  between operations  2.51 us (1%)
    ppermute x8, starting transfers between devices, shifted(): lax.ppermute(value, axis, [(i, (i + by) % size) for i in range(size)])  59.3 us
    all_to_all x5, waiting for transfers between devices, exchange(): return lax.all_to_all(blocks, axes, 0, 0, tiled=True)  44.9 us
    all_to_all x5, starting transfers between devices, exchange(): return lax.all_to_all(blocks, axes, 0, 0, tiled=True)  32.6 us
    ppermute x4, starting transfers between devices, along_z(): return lax.ppermute(value, ('zl', 'zh'), pairs)  23.8 us
    ppermute x8, waiting for transfers between devices, shifted(): lax.ppermute(value, axis, [(i, (i + by) % size) for i in range(size)])  11.9 us
    ppermute x4, waiting for transfers between devices, along_z(): return lax.ppermute(value, ('zl', 'zh'), pairs)  5.93 us
    dot_general x6, matrix products, dot(): return lax.dot_general(a, b, (dims, ((), ())), preferred_element_type=F32)  5.77 us
  transfers between devices with their start and end apart: 17, of which 12 were waited for; matrix products, arithmetic and copies ran while one was open for 2% of the time, Pallas kernels for 0%

profile of v10, /device:TPU:1, one launch (start us, length us, event | category | flops | bytes accessed | tf_op | source)
XLA Modules:
  0.0 197.3 jit_solution(4491961271723938275)
XLA Ops:
  3.7 4.8 %all-to-all-start = ((bf16[4,32,1152]{2,1,0:T(8,128)(2,1)}), bf16[4,32,1152]{2,1,0:T(8,128)(2,1)S(1)}, u32[]{:S(2)}, u32[]{:S(2)}) async-start(bf16[4,32,1152]{2,1,0:T(8,128)(2,1)} %pad_maximum_fusion), calls=%async_computation | async-start | bytes 589824 | tf_op jit(solution)/shard_map/embed/all_to_all | solution.py:23
  8.7 5.5 %all-to-all-done = bf16[4,32,1152]{2,1,0:T(8,128)(2,1)S(1)} async-done(((bf16[4,32,1152]{2,1,0:T(8,128)(2,1)}), bf16[4,32,1152]{2,1,0:T(8,128)(2,1)S(1)}, u32[]{:S(2)}, u32[]{:S(2)}) %all-to-all-start) | async-done | bytes 294944 | tf_op jit(solution)/shard_map/embed/all_to_all | solution.py:23
  14.3 19.2 %collective-permute-start = (f32[32,1152]{1,0:T(8,128)S(1)}, f32[32,1152]{1,0:T(8,128)S(1)}, u32[]{:S(2)}, u32[]{:S(2)}) collective-permute-start(f32[32,1152]{1,0:T(8,128)S(1)} %convert_reduce_fusion.2), channel_id=1, source_target_pairs={{0,4},{4,0},{1,5},{5,1},{2,6},{6,2},{3,7},{7,3},{8,12},{12,8},{9,1... | collective-permute-start | bytes 442376 | tf_op jit(solution)/shard_map/embed/ppermute | solution.py:32
  35.1 1.2 collective-permute-done
  36.6 10.8 %collective-permute-start.2 = (bf16[32,1152]{1,0:T(8,128)(2,1)S(1)}, bf16[32,1152]{1,0:T(8,128)(2,1)S(1)}, u32[]{:S(2)}, u32[]{:S(2)}) collective-permute-start(bf16[32,1152]{1,0:T(8,128)(2,1)S(1)} %get-tuple-element.11), channel_id=1, source_target_pairs={{0,512},{128,640},{256,768},{384,896},{512,4},{640,132},{768,260},... | collective-permute-start | bytes 221192 | tf_op jit(solution)/shard_map/gather_others/ppermute | solution.py:39
  48.1 8.4 %all-to-all-start.1 = ((bf16[8,16,1152]{2,1,0:T(8,128)(2,1)}), bf16[8,16,1152]{2,1,0:T(8,128)(2,1)S(1)}, u32[]{:S(2)}, u32[]{:S(2)}) async-start(bf16[8,16,1152]{2,1,0:T(8,128)(2,1)} %broadcast_in_dim.44), calls=%async_computation.1 | async-start | bytes 589824 | tf_op jit(solution)/shard_map/gather_own/all_to_all | solution.py:23
  56.5 1.6 collective-permute-done.2
  58.2 7.7 %collective-permute-start.5 = (bf16[32,1152]{1,0:T(8,128)(2,1)S(1)}, bf16[32,1152]{1,0:T(8,128)(2,1)S(1)}, u32[]{:S(2)}, u32[]{:S(2)}) collective-permute-start(bf16[32,1152]{1,0:T(8,128)(2,1)S(1)} %bitcast.60), channel_id=1, source_target_pairs={{0,256},{128,384},{256,512},{384,640},{512,768},{640,896},{768,4},... | collective-permute-start | bytes 221192 | tf_op jit(solution)/shard_map/gather_others/ppermute | solution.py:39
  65.9 1.9 collective-permute-start.4
  67.9 3.4 %collective-permute-start.3 = (bf16[32,1152]{1,0:T(8,128)(2,1)S(1)}, bf16[32,1152]{1,0:T(8,128)(2,1)S(1)}, u32[]{:S(2)}, u32[]{:S(2)}) collective-permute-start(bf16[32,1152]{1,0:T(8,128)(2,1)S(1)} %bitcast.58), channel_id=1, source_target_pairs={{0,128},{128,256},{256,384},{384,512},{512,640},{640,768},{768,896... | collective-permute-start | bytes 221192 | tf_op jit(solution)/shard_map/gather_others/ppermute | solution.py:39
  71.4 4.1 %collective-permute-done.3 = bf16[32,1152]{1,0:T(8,128)(2,1)S(1)} collective-permute-done((bf16[32,1152]{1,0:T(8,128)(2,1)S(1)}, bf16[32,1152]{1,0:T(8,128)(2,1)S(1)}, u32[]{:S(2)}, u32[]{:S(2)}) %collective-permute-start.3) | collective-permute-done | bytes 73760 | tf_op jit(solution)/shard_map/gather_others/ppermute | solution.py:39
  75.6 2.2 %collective-permute-start.6 = (bf16[128,1152]{1,0:T(8,128)(2,1)S(1)}, bf16[128,1152]{1,0:T(8,128)(2,1)S(1)}, u32[]{:S(2)}, u32[]{:S(2)}) collective-permute-start(bf16[128,1152]{1,0:T(8,128)(2,1)S(1)} %pad_maximum_fusion.1.refs_0_), channel_id=1, source_target_pairs={{0,1},{1,2},{2,3},{3,0},{4,5},{5,6},{6,7},{7,4},{8,9},{9,10},{10,1... | collective-permute-start | bytes 884744 | tf_op jit(solution)/shard_map/gather_others/ppermute | solution.py:32
  77.8 4.3 %collective-permute-start.7 = (bf16[128,1152]{1,0:T(8,128)(2,1)S(1)}, bf16[128,1152]{1,0:T(8,128)(2,1)S(1)}, u32[]{:S(2)}, u32[]{:S(2)}) collective-permute-start(bf16[128,1152]{1,0:T(8,128)(2,1)S(1)} %pad_maximum_fusion.1.refs_0_), channel_id=1, source_target_pairs={{0,3},{1,0},{2,1},{3,2},{4,7},{5,4},{6,5},{7,6},{8,11},{9,8},{10,9... | collective-permute-start | bytes 884744 | tf_op jit(solution)/shard_map/gather_others/ppermute | solution.py:32
  82.1 2.3 %collective-permute-start.8 = (bf16[128,1152]{1,0:T(8,128)(2,1)S(1)}, bf16[128,1152]{1,0:T(8,128)(2,1)S(1)}, u32[]{:S(2)}, u32[]{:S(2)}) collective-permute-start(bf16[128,1152]{1,0:T(8,128)(2,1)S(1)} %pad_maximum_fusion.1.refs_0_), channel_id=1, source_target_pairs={{0,2},{1,3},{2,0},{3,1},{4,6},{5,7},{6,4},{7,5},{8,10},{9,11},{10,... | collective-permute-start | bytes 884744 | tf_op jit(solution)/shard_map/gather_others/ppermute | solution.py:32
  84.4 5.2 %collective-permute-start.1 = (bf16[128,1152]{1,0:T(8,128)(2,1)S(1)}, bf16[128,1152]{1,0:T(8,128)(2,1)S(1)}, u32[]{:S(2)}, u32[]{:S(2)}) collective-permute-start(bf16[128,1152]{1,0:T(8,128)(2,1)S(1)} %bitcast.44), channel_id=1, source_target_pairs={{0,8},{8,0},{1,9},{9,1},{2,10},{10,2},{3,11},{11,3},{4,12},{12,4},... | collective-permute-start | bytes 884744 | tf_op jit(solution)/shard_map/gather_own/ppermute | solution.py:32
  89.8 1.3 collective-permute-done.8.refs_3_
  91.1 1.6 pairs.1
  92.6 6.7 %collective-permute-start.9 = (f32[128,1152]{1,0:T(8,128)S(1)}, f32[128,1152]{1,0:T(8,128)S(1)}, u32[]{:S(2)}, u32[]{:S(2)}) collective-permute-start(f32[128,1152]{1,0:T(8,128)S(1)} %get-tuple-element.7), channel_id=1, source_target_pairs={{0,8},{8,0},{1,9},{9,1},{2,10},{10,2},{3,11},{11,3},{4,12},{12,4},... | collective-permute-start | bytes 1769480 | tf_op jit(solution)/shard_map/reduce_pairs/ppermute | solution.py:32
  99.3 1.6 collective-permute-done.9
  101.7 6.8 %all-to-all-start.2 = ((bf16[8,16,1152]{2,1,0:T(8,128)(2,1)}), bf16[8,16,1152]{2,1,0:T(8,128)(2,1)S(1)}, u32[]{:S(2)}, u32[]{:S(2)}) async-start(bf16[8,16,1152]{2,1,0:T(8,128)(2,1)} %bitcast.14), calls=%async_computation.2 | async-start | bytes 589824 | tf_op jit(solution)/shard_map/reduce_pairs/all_to_all | solution.py:23
  108.6 12.3 %all-to-all-done.2 = bf16[8,16,1152]{2,1,0:T(8,128)(2,1)S(1)} async-done(((bf16[8,16,1152]{2,1,0:T(8,128)(2,1)}), bf16[8,16,1152]{2,1,0:T(8,128)(2,1)S(1)}, u32[]{:S(2)}, u32[]{:S(2)}) %all-to-all-start.2) | async-done | bytes 294944 | tf_op jit(solution)/shard_map/reduce_pairs/all_to_all | solution.py:23
  121.8 4.6 %all-to-all-start.3 = ((bf16[4,16,1152]{2,1,0:T(8,128)(2,1)}), bf16[4,16,1152]{2,1,0:T(8,128)(2,1)S(1)}, u32[]{:S(2)}, u32[]{:S(2)}) async-start(bf16[4,16,1152]{2,1,0:T(8,128)(2,1)} %broadcast_in_dim.46), calls=%async_computation.3 | async-start | bytes 294912 | tf_op jit(solution)/shard_map/back/all_to_all | solution.py:23
  126.7 4.7 %all-to-all-done.3 = bf16[4,16,1152]{2,1,0:T(8,128)(2,1)S(1)} async-done(((bf16[4,16,1152]{2,1,0:T(8,128)(2,1)}), bf16[4,16,1152]{2,1,0:T(8,128)(2,1)S(1)}, u32[]{:S(2)}, u32[]{:S(2)}) %all-to-all-start.3) | async-done | bytes 147488 | tf_op jit(solution)/shard_map/back/all_to_all | solution.py:23
  131.4 9.7 %collective-permute-start.10 = (bf16[64,1152]{1,0:T(8,128)(2,1)S(1)}, bf16[64,1152]{1,0:T(8,128)(2,1)S(1)}, u32[]{:S(2)}, u32[]{:S(2)}) collective-permute-start(bf16[64,1152]{1,0:T(8,128)(2,1)S(1)} %bitcast.47), channel_id=1, source_target_pairs={{0,4},{4,0},{1,5},{5,1},{2,6},{6,2},{3,7},{7,3},{8,12},{12,8},{9,1... | collective-permute-start | bytes 442376 | tf_op jit(solution)/shard_map/back/ppermute | solution.py:32
  141.1 1.3 fusion.6
  142.5 5.9 %collective-permute-done.10 = bf16[64,1152]{1,0:T(8,128)(2,1)S(1)} collective-permute-done((bf16[64,1152]{1,0:T(8,128)(2,1)S(1)}, bf16[64,1152]{1,0:T(8,128)(2,1)S(1)}, u32[]{:S(2)}, u32[]{:S(2)}) %collective-permute-start.10) | collective-permute-done | bytes 147488 | tf_op jit(solution)/shard_map/back/ppermute | solution.py:32
  148.4 1.3 convolution_add_fusion
  150.0 9.8 %collective-permute-start.11 = (f32[576,288]{0,1:T(8,128)S(1)}, f32[576,288]{0,1:T(8,128)S(1)}, u32[]{:S(2)}, u32[]{:S(2)}) collective-permute-start(f32[576,288]{0,1:T(8,128)S(1)} %slice.51), channel_id=1, source_target_pairs={{0,8},{8,0},{1,9},{9,1},{2,10},{10,2},{3,11},{11,3},{4,12},{12,4},... | collective-permute-start | bytes 1990664 | tf_op jit(solution)/shard_map/weight_grad/ppermute | solution.py:32
  159.8 1.8 collective-permute-done.11
  162.2 1.6 reshape.211
  163.7 8.0 %all-to-all-start.4 = ((bf16[64,2,1296]{2,1,0:T(2,128)(2,1)}), bf16[64,2,1296]{2,1,0:T(2,128)(2,1)S(1)}, u32[]{:S(2)}, u32[]{:S(2)}) async-start(bf16[64,2,1296]{2,1,0:T(2,128)(2,1)} %reshape.211), calls=%async_computation.4 | async-start | bytes 720896 | tf_op jit(solution)/shard_map/weight_grad/all_to_all | solution.py:23
  173.2 22.3 %all-to-all-done.4 = bf16[64,2,1296]{2,1,0:T(2,128)(2,1)S(1)} async-done(((bf16[64,2,1296]{2,1,0:T(2,128)(2,1)}), bf16[64,2,1296]{2,1,0:T(2,128)(2,1)S(1)}, u32[]{:S(2)}, u32[]{:S(2)}) %all-to-all-start.4) | async-done | bytes 331808 | tf_op jit(solution)/shard_map/weight_grad/all_to_all | solution.py:23
  (67 shorter events, 10.8 us)
Async XLA Ops:
  3.7 10.5 %all-to-all-start = ((bf16[4,32,1152]{2,1,0:T(8,128)(2,1)}), bf16[4,32,1152]{2,1,0:T(8,128)(2,1)S(1)}, u32[]{:S(2)}, u32[]{:S(2)}) async-start(bf16[4,32,1152]{2,1,0:T(8,128)(2,1)} %pad_maximum_fusion), calls=%async_computation | async-start | bytes 589824 | tf_op jit(solution)/shard_map/embed/all_to_all | solution.py:23
  14.3 22.0 %collective-permute-start = (f32[32,1152]{1,0:T(8,128)S(1)}, f32[32,1152]{1,0:T(8,128)S(1)}, u32[]{:S(2)}, u32[]{:S(2)}) collective-permute-start(f32[32,1152]{1,0:T(8,128)S(1)} %convert_reduce_fusion.2), channel_id=1, source_target_pairs={{0,4},{4,0},{1,5},{5,1},{2,6},{6,2},{3,7},{7,3},{8,12},{12,8},{9,1... | collective-permute-start | bytes 442376 | tf_op jit(solution)/shard_map/embed/ppermute | solution.py:32
  36.6 21.6 %collective-permute-start.2 = (bf16[32,1152]{1,0:T(8,128)(2,1)S(1)}, bf16[32,1152]{1,0:T(8,128)(2,1)S(1)}, u32[]{:S(2)}, u32[]{:S(2)}) collective-permute-start(bf16[32,1152]{1,0:T(8,128)(2,1)S(1)} %get-tuple-element.11), channel_id=1, source_target_pairs={{0,512},{128,640},{256,768},{384,896},{512,4},{640,132},{768,260},... | collective-permute-start | bytes 221192 | tf_op jit(solution)/shard_map/gather_others/ppermute | solution.py:39
  48.1 36.2 %all-to-all-start.1 = ((bf16[8,16,1152]{2,1,0:T(8,128)(2,1)}), bf16[8,16,1152]{2,1,0:T(8,128)(2,1)S(1)}, u32[]{:S(2)}, u32[]{:S(2)}) async-start(bf16[8,16,1152]{2,1,0:T(8,128)(2,1)} %broadcast_in_dim.44), calls=%async_computation.1 | async-start | bytes 589824 | tf_op jit(solution)/shard_map/gather_own/all_to_all | solution.py:23
  58.2 13.2 %collective-permute-start.5 = (bf16[32,1152]{1,0:T(8,128)(2,1)S(1)}, bf16[32,1152]{1,0:T(8,128)(2,1)S(1)}, u32[]{:S(2)}, u32[]{:S(2)}) collective-permute-start(bf16[32,1152]{1,0:T(8,128)(2,1)S(1)} %bitcast.60), channel_id=1, source_target_pairs={{0,256},{128,384},{256,512},{384,640},{512,768},{640,896},{768,4},... | collective-permute-start | bytes 221192 | tf_op jit(solution)/shard_map/gather_others/ppermute | solution.py:39
  65.9 5.5 %collective-permute-start.4 = (bf16[32,1152]{1,0:T(8,128)(2,1)S(1)}, bf16[32,1152]{1,0:T(8,128)(2,1)S(1)}, u32[]{:S(2)}, u32[]{:S(2)}) collective-permute-start(bf16[32,1152]{1,0:T(8,128)(2,1)S(1)} %bitcast.59), channel_id=1, source_target_pairs={{0,900},{128,0},{256,128},{384,256},{512,384},{640,512},{768,640},... | collective-permute-start | bytes 221192 | tf_op jit(solution)/shard_map/gather_others/ppermute | solution.py:39
  67.9 7.7 %collective-permute-start.3 = (bf16[32,1152]{1,0:T(8,128)(2,1)S(1)}, bf16[32,1152]{1,0:T(8,128)(2,1)S(1)}, u32[]{:S(2)}, u32[]{:S(2)}) collective-permute-start(bf16[32,1152]{1,0:T(8,128)(2,1)S(1)} %bitcast.58), channel_id=1, source_target_pairs={{0,128},{128,256},{256,384},{384,512},{512,640},{640,768},{768,896... | collective-permute-start | bytes 221192 | tf_op jit(solution)/shard_map/gather_others/ppermute | solution.py:39
  75.6 14.2 %collective-permute-start.6 = (bf16[128,1152]{1,0:T(8,128)(2,1)S(1)}, bf16[128,1152]{1,0:T(8,128)(2,1)S(1)}, u32[]{:S(2)}, u32[]{:S(2)}) collective-permute-start(bf16[128,1152]{1,0:T(8,128)(2,1)S(1)} %pad_maximum_fusion.1.refs_0_), channel_id=1, source_target_pairs={{0,1},{1,2},{2,3},{3,0},{4,5},{5,6},{6,7},{7,4},{8,9},{9,10},{10,1... | collective-permute-start | bytes 884744 | tf_op jit(solution)/shard_map/gather_others/ppermute | solution.py:32
  77.8 12.0 %collective-permute-start.7 = (bf16[128,1152]{1,0:T(8,128)(2,1)S(1)}, bf16[128,1152]{1,0:T(8,128)(2,1)S(1)}, u32[]{:S(2)}, u32[]{:S(2)}) collective-permute-start(bf16[128,1152]{1,0:T(8,128)(2,1)S(1)} %pad_maximum_fusion.1.refs_0_), channel_id=1, source_target_pairs={{0,3},{1,0},{2,1},{3,2},{4,7},{5,4},{6,5},{7,6},{8,11},{9,8},{10,9... | collective-permute-start | bytes 884744 | tf_op jit(solution)/shard_map/gather_others/ppermute | solution.py:32
  82.1 9.0 %collective-permute-start.8 = (bf16[128,1152]{1,0:T(8,128)(2,1)S(1)}, bf16[128,1152]{1,0:T(8,128)(2,1)S(1)}, u32[]{:S(2)}, u32[]{:S(2)}) collective-permute-start(bf16[128,1152]{1,0:T(8,128)(2,1)S(1)} %pad_maximum_fusion.1.refs_0_), channel_id=1, source_target_pairs={{0,2},{1,3},{2,0},{3,1},{4,6},{5,7},{6,4},{7,5},{8,10},{9,11},{10,... | collective-permute-start | bytes 884744 | tf_op jit(solution)/shard_map/gather_others/ppermute | solution.py:32
  84.4 6.7 %collective-permute-start.1 = (bf16[128,1152]{1,0:T(8,128)(2,1)S(1)}, bf16[128,1152]{1,0:T(8,128)(2,1)S(1)}, u32[]{:S(2)}, u32[]{:S(2)}) collective-permute-start(bf16[128,1152]{1,0:T(8,128)(2,1)S(1)} %bitcast.44), channel_id=1, source_target_pairs={{0,8},{8,0},{1,9},{9,1},{2,10},{10,2},{3,11},{11,3},{4,12},{12,4},... | collective-permute-start | bytes 884744 | tf_op jit(solution)/shard_map/gather_own/ppermute | solution.py:32
  92.6 8.3 %collective-permute-start.9 = (f32[128,1152]{1,0:T(8,128)S(1)}, f32[128,1152]{1,0:T(8,128)S(1)}, u32[]{:S(2)}, u32[]{:S(2)}) collective-permute-start(f32[128,1152]{1,0:T(8,128)S(1)} %get-tuple-element.7), channel_id=1, source_target_pairs={{0,8},{8,0},{1,9},{9,1},{2,10},{10,2},{3,11},{11,3},{4,12},{12,4},... | collective-permute-start | bytes 1769480 | tf_op jit(solution)/shard_map/reduce_pairs/ppermute | solution.py:32
  101.7 39.4 %copy-start.2 = (bf16[64,144]{1,0:T(8,128)(2,1)S(1)}, bf16[64,144]{1,0:T(8,128)(2,1)}, u32[]{:S(2)}) copy-start(bf16[64,144]{1,0:T(8,128)(2,1)} %param.7) | copy-start | bytes 55300
  101.7 39.4 %copy-start.3 = (bf16[64,144]{1,0:T(8,128)(2,1)S(1)}, bf16[64,144]{1,0:T(8,128)(2,1)}, u32[]{:S(2)}) copy-start(bf16[64,144]{1,0:T(8,128)(2,1)} %param.6) | copy-start | bytes 55300
  101.7 19.2 %all-to-all-start.2 = ((bf16[8,16,1152]{2,1,0:T(8,128)(2,1)}), bf16[8,16,1152]{2,1,0:T(8,128)(2,1)S(1)}, u32[]{:S(2)}, u32[]{:S(2)}) async-start(bf16[8,16,1152]{2,1,0:T(8,128)(2,1)} %bitcast.14), calls=%async_computation.2 | async-start | bytes 589824 | tf_op jit(solution)/shard_map/reduce_pairs/all_to_all | solution.py:23
  121.8 9.6 %all-to-all-start.3 = ((bf16[4,16,1152]{2,1,0:T(8,128)(2,1)}), bf16[4,16,1152]{2,1,0:T(8,128)(2,1)S(1)}, u32[]{:S(2)}, u32[]{:S(2)}) async-start(bf16[4,16,1152]{2,1,0:T(8,128)(2,1)} %broadcast_in_dim.46), calls=%async_computation.3 | async-start | bytes 294912 | tf_op jit(solution)/shard_map/back/all_to_all | solution.py:23
  131.4 17.0 %collective-permute-start.10 = (bf16[64,1152]{1,0:T(8,128)(2,1)S(1)}, bf16[64,1152]{1,0:T(8,128)(2,1)S(1)}, u32[]{:S(2)}, u32[]{:S(2)}) collective-permute-start(bf16[64,1152]{1,0:T(8,128)(2,1)S(1)} %bitcast.47), channel_id=1, source_target_pairs={{0,4},{4,0},{1,5},{5,1},{2,6},{6,2},{3,7},{7,3},{8,12},{12,8},{9,1... | collective-permute-start | bytes 442376 | tf_op jit(solution)/shard_map/back/ppermute | solution.py:32
  150.0 11.6 %collective-permute-start.11 = (f32[576,288]{0,1:T(8,128)S(1)}, f32[576,288]{0,1:T(8,128)S(1)}, u32[]{:S(2)}, u32[]{:S(2)}) collective-permute-start(f32[576,288]{0,1:T(8,128)S(1)} %slice.51), channel_id=1, source_target_pairs={{0,8},{8,0},{1,9},{9,1},{2,10},{10,2},{3,11},{11,3},{4,12},{12,4},... | collective-permute-start | bytes 1990664 | tf_op jit(solution)/shard_map/weight_grad/ppermute | solution.py:32
  161.9 9.8 %copy-start = (bf16[144,1152]{1,0:T(8,128)(2,1)S(1)}, bf16[144,1152]{1,0:T(8,128)(2,1)}, u32[]{:S(2)}) copy-start(bf16[144,1152]{1,0:T(8,128)(2,1)} %param.8) | copy-start | bytes 995332
  162.1 9.6 %copy-start.1 = (bf16[144,1152]{1,0:T(8,128)(2,1)S(1)}, bf16[144,1152]{1,0:T(8,128)(2,1)}, u32[]{:S(2)}) copy-start(bf16[144,1152]{1,0:T(8,128)(2,1)} %param.9) | copy-start | bytes 995332
  163.7 31.9 %all-to-all-start.4 = ((bf16[64,2,1296]{2,1,0:T(2,128)(2,1)}), bf16[64,2,1296]{2,1,0:T(2,128)(2,1)S(1)}, u32[]{:S(2)}, u32[]{:S(2)}) async-start(bf16[64,2,1296]{2,1,0:T(2,128)(2,1)} %reshape.211), calls=%async_computation.4 | async-start | bytes 720896 | tf_op jit(solution)/shard_map/weight_grad/all_to_all | solution.py:23
